TPU v7x, 32 devices: a whole 2x2x4 slice. The times are simulated.
32 devices in a mesh: task: 4 (over z), row: 2 (over x), col: 4 (over y, core).
Axes of the slice: x: 2, y: 2, z: 4, core: 2. Of those that a mesh axis runs over, the one named last changes fastest.
Arguments:
- activations: bfloat16 [4, 512, 13824], P('task', 'col', 'row'), may hold values from -6 to 6
- weights: bfloat16 [4, 13824, 5120], P('task', 'row', 'col'), may hold values from -0.0625 to 0.0625
- labels: int32 [4, 512], P('task'), may hold values from 0 to 127
- prototypes: bfloat16 [4, 128, 5120], P('task', None, 'col'), may hold values from -6 to 6
Outputs:
- merged: bfloat16 [13824, 5120], P('row', 'col')
- merged_out: bfloat16 [4, 512, 5120], P('task', 'row', 'col')
All inputs are finite; a program needn't handle non-finite values.
Results may differ from a plain program's by a relative error of at most 0.02.
Values may be sent and summed in bfloat16 or wider, within the bound.
No kernel may reach another device: no remote copies, remote signals or barrier semaphores. Data moves between devices by JAX's collectives and lax.ppermute only.
A program may use at most 192 MiB of HBM per device.

v0:
```python
import jax
import jax.numpy as jnp
from jax import lax
from jax.sharding import PartitionSpec as P


def class_targets(label_rows, protos):
    count = label_rows.shape[0]
    onehot = (
        label_rows[:, None] == lax.broadcasted_iota(jnp.int32, (count, protos.shape[0]), 1)
    ).astype(jnp.bfloat16)
    return jnp.dot(onehot, protos, preferred_element_type=jnp.float32)


def local(activations, weights, labels, prototypes):
    acts = activations[0]
    weight = weights[0]
    label_row = labels[0]
    protos = prototypes[0]
    full_acts = lax.all_gather(acts, "col", axis=0, tiled=True)
    partial_out = jnp.dot(full_acts, weight, preferred_element_type=jnp.float32)
    output = lax.psum(partial_out.astype(jnp.bfloat16), "row").astype(jnp.float32)
    grad = output - class_targets(label_row, protos)
    gsq = (grad * grad).astype(jnp.bfloat16)
    wide = full_acts.astype(jnp.float32)
    asq = (wide * wide).astype(jnp.bfloat16)
    fisher = lax.dot_general(asq, gsq, (((0,), (0,)), ((), ())), preferred_element_type=jnp.float32)
    weighted = fisher * weight.astype(jnp.float32)
    numer, denom = (
        lax.psum_scatter(weighted, "task", scatter_dimension=0, tiled=True),
        lax.psum_scatter(fisher, "task", scatter_dimension=0, tiled=True),
    )
    piece = (numer / (denom + 1e-06)).astype(jnp.bfloat16)
    merged = lax.all_gather(piece, "task", axis=0, tiled=True)
    result = lax.psum_scatter(
        jnp.dot(full_acts, merged, preferred_element_type=jnp.float32).astype(jnp.bfloat16),
        "row",
        scatter_dimension=0,
        tiled=True,
    )
    return (merged, result[None])


def solution(mesh):
    placed = (
        P("task", "col", "row"),
        P("task", "row", "col"),
        P("task", None),
        P("task", None, "col"),
    )
    return jax.shard_map(
        local,
        mesh=mesh,
        in_specs=placed,
        out_specs=(P("row", "col"), P("task", "row", "col")),
        check_vma=False,
    )
```

profile of v0, /device:TPU:0, one launch (start us, length us, event | category | flops | bytes accessed | tf_op | source)
XLA Modules:
  0.0 1701.7 jit_solution(4506123462578386605)
XLA Ops:
  7.2 0.0 copy-start
  7.2 0.0 all-gather.6.cloned.1.call-start
  7.2 0.7 all-gather.6.cloned.1.call-update
  7.9 0.0 copy-start.2
  7.9 0.0 all-reduce.2.cloned.1.call-start
  8.0 55.2 %all-gather.6.cloned.1.call-done = bf16[1,512,6912]{2,1,0:T(8,128)(2,1)} async-done(((bf16[1,128,6912]{2,1,0:T(8,128)(2,1)}), bf16[1,512,6912]{2,1,0:T(8,128)(2,1)}) %all-gather.6.cloned.1.call-update) | async-done | bytes 7077904 | tf_op jit(solution)/shard_map/all_gather | solution.py:20
  63.2 15.6 fusion.8
  78.7 0.0 all-reduce.2.cloned.1.call-update
  78.7 0.0 reduce-scatter.4.cloned.1.call-start
  78.8 45.9 %all-reduce.2.cloned.1.call-done = bf16[512,1280]{1,0:T(8,128)(2,1)} async-done(((bf16[512,1280]{1,0:T(8,128)(2,1)}), bf16[512,1280]{1,0:T(8,128)(2,1)}) %all-reduce.2.cloned.1.call-update) | async-done | bytes 1310736 | tf_op jit(solution)/shard_map/psum | solution.py:22
  124.7 0.0 copy-done
  124.7 0.0 copy-done.2
  124.7 33.3 %convert_multiply_fusion = (f32[6912,1280]{1,0:T(8,128)}, f32[6912,1280]{1,0:T(8,128)}) fusion(bf16[1,6912,1280]{2,1,0:T(8,128)(2,1)} %param.5, bf16[512,1280]{1,0:T(8,128)(2,1)} %all-reduce.2.cloned.1.call-done, bf16[1,128,1280]{2,1,0:T(8,128)(2,1)S(1)} %copy-done, s32[512]{0:T(512)S(1)} %bitcast.35, bf16[1,512,6912]{2,1,0:T(8,128)(2,1)} %all-gather.6.cloned.1.call-done), kind=kOutput, calls=%fused_computation | convolution fusion | flops 9258467328 | bytes 97191936 | tf_op jit(solution)/shard_map/dot_general | solution.py:27
  158.0 0.0 reduce-scatter.4.cloned.1.call-update
  158.0 0.0 reduce-scatter.6.cloned.1.call-start
  158.1 0.5 reduce-scatter.6.cloned.1.call-update
  158.6 0.0 all-gather.4.cloned.1.call-start
  158.6 581.0 %reduce-scatter.4.cloned.1.call-done = f32[1728,1280]{1,0:T(8,128)} async-done(((f32[6912,1280]{1,0:T(8,128)}), f32[1728,1280]{1,0:T(8,128)}) %reduce-scatter.4.cloned.1.call-update) | async-done | bytes 8847376 | tf_op jit(solution)/shard_map/reduce_scatter | solution.py:30
  739.6 584.6 %reduce-scatter.6.cloned.1.call-done = f32[1728,1280]{1,0:T(8,128)} async-done(((f32[6912,1280]{1,0:T(8,128)}), f32[1728,1280]{1,0:T(8,128)}) %reduce-scatter.6.cloned.1.call-update) | async-done | bytes 8847376 | tf_op jit(solution)/shard_map/reduce_scatter | solution.py:31
  1324.2 9.8 divide_convert_fusion
  1334.0 0.0 all-gather.4.cloned.1.call-update
  1334.0 0.2 reduce-scatter.8.cloned.1.call-start
  1334.2 304.1 %all-gather.4.cloned.1.call-done = bf16[6912,1280]{1,0:T(8,128)(2,1)} async-done(((bf16[1728,1280]{1,0:T(8,128)(2,1)}), bf16[6912,1280]{1,0:T(8,128)(2,1)}) %all-gather.4.cloned.1.call-update) | async-done | bytes 17694736 | tf_op jit(solution)/shard_map/all_gather | solution.py:34
  1638.3 16.2 fusion.17
  1654.5 0.0 reduce-scatter.8.cloned.1.call-update
  1654.6 22.3 %reduce-scatter.8.cloned.1.call-done = bf16[256,1280]{0,1:T(8,128)(2,1)} async-done(((bf16[512,1280]{0,1:T(8,128)(2,1)}), bf16[256,1280]{0,1:T(8,128)(2,1)}) %reduce-scatter.8.cloned.1.call-update) | async-done | bytes 655376 | tf_op jit(solution)/shard_map/reduce_scatter | solution.py:35
  1676.9 2.2 copy.6
  1679.0 0.0 copy-start.1
  1679.0 15.8 copy.9
  1694.8 0.0 copy-done.1
Async XLA Ops:
  7.2 117.5 %copy-start = (bf16[1,128,1280]{2,1,0:T(8,128)(2,1)S(1)}, bf16[1,128,1280]{2,1,0:T(8,128)(2,1)}, u32[]{:S(2)}) copy-start(bf16[1,128,1280]{2,1,0:T(8,128)(2,1)} %param.7) | copy-start | bytes 983044
  7.2 56.0 %all-gather.6.cloned.1.call-start = ((), (), s32[]{:S(2)}) async-start(), calls=%async_computation.8 | async-start | bytes 8847360 | tf_op jit(solution)/shard_map/all_gather | solution.py:20
  7.9 116.8 %copy-start.2 = (s32[1,512]{1,0:T(1,128)S(1)}, s32[1,512]{1,0:T(1,128)}, u32[]{:S(2)}) copy-start(s32[1,512]{1,0:T(1,128)} %param.6) | copy-start | bytes 6148
  7.9 116.7 %all-reduce.2.cloned.1.call-start = ((), (), s32[]{:S(2)}) async-start(), calls=%async_computation.3 | async-start | bytes 2621440 | tf_op jit(solution)/shard_map/psum | solution.py:22
  78.7 660.9 %reduce-scatter.4.cloned.1.call-start = ((), (), s32[]{:S(2)}) async-start(), calls=%async_computation.4 | async-start | bytes 44236800 | tf_op jit(solution)/shard_map/reduce_scatter | solution.py:30
  158.0 1166.2 %reduce-scatter.6.cloned.1.call-start = ((), (), s32[]{:S(2)}) async-start(), calls=%async_computation.5 | async-start | bytes 44236800 | tf_op jit(solution)/shard_map/reduce_scatter | solution.py:31
  158.6 1479.7 %all-gather.4.cloned.1.call-start = ((), (), s32[]{:S(2)}) async-start(), calls=%async_computation.6 | async-start | bytes 22118400 | tf_op jit(solution)/shard_map/all_gather | solution.py:34
  1334.0 342.9 %reduce-scatter.8.cloned.1.call-start = ((), (), s32[]{:S(2)}) async-start(), calls=%async_computation.7 | async-start | bytes 1966080 | tf_op jit(solution)/shard_map/reduce_scatter | solution.py:35
  1679.0 15.8 copy-start.1
Sparse Core Ops, SparseCore 0:
  9.6 53.5 all-gather.5
  78.9 45.7 all-reduce.1
  158.1 581.4 reduce-scatter.3
  741.9 582.2 reduce-scatter.5
  1334.1 304.1 all-gather.3
  1654.7 22.1 reduce-scatter.7
where the time goes:
time: 1700 us
  waiting for transfers between devices  1590 us (94%)
  matrix products  65.1 us (4%)
  local copies, waits for them, and re-layouts  17.9 us (1%)
    reduce_scatter x1, waiting for transfers between devices, local(): lax.psum_scatter(fisher, 'task', scatter_dimension=0, tiled=True)  585 us
    reduce_scatter x1, waiting for transfers between devices, local(): lax.psum_scatter(weighted, 'task', scatter_dimension=0, tiled=True)  581 us
    all_gather x1, waiting for transfers between devices, local(): merged = lax.all_gather(piece, 'task', axis=0, tiled=True)  304 us
    all_gather x1, waiting for transfers between devices, local(): full_acts = lax.all_gather(acts, 'col', axis=0, tiled=True)  55.2 us
    psum x1, waiting for transfers between devices, local(): lax.psum(partial_out.astype(jnp.bfloat16), 'row').astype(jnp.float32)  45.9 us
  transfers between devices with their start and end apart: 6, of which 6 were waited for; matrix products, arithmetic and copies ran while one was open for 0% of the time, Pallas kernels for 0%

commit v1 on v0

v1 whole, which is shorter than its diff:
```python
import functools

import jax
import jax.numpy as jnp
from jax import lax
from jax.experimental import pallas as pl
from jax.experimental.pallas import tpu as pltpu
from jax.sharding import PartitionSpec as P

BF16 = jnp.bfloat16
F32 = jnp.float32
ANY = pl.BlockSpec(memory_space=pl.ANY)
WIDTH = 256
UNIT_ROWS = 384
MOST = 3
LEAST = 1
LAG = 2
VMEM_LIMIT = 60 * 1024 * 1024
COST = pl.CostEstimate(flops=0, bytes_accessed=0, transcendentals=0)


def largest_divisor(total, limit, unit):
    best = total
    for size in range(unit, limit + 1, unit):
        if total % size == 0:
            best = size
    return best


def group_product(lhs, mat, group, groups, deps=()):
    tokens, rows = lhs.shape
    depth = largest_divisor(rows, 1152, 128)
    steps = rows // depth

    def body(lhs_ref, *rest):
        mats, (out_ref, acc_ref) = rest[:groups], rest[-2:]
        step = pl.program_id(0)
        for g in range(groups):
            part = jnp.dot(lhs_ref[...], mats[g][...], preferred_element_type=F32)

            @pl.when(step == 0)
            def _():
                acc_ref[g] = part

            @pl.when(step > 0)
            def _():
                acc_ref[g] += part

        @pl.when(step == steps - 1)
        def _():
            out_ref[...] = acc_ref[...].astype(BF16)

    return pl.pallas_call(
        body,
        grid=(steps,),
        out_shape=jax.ShapeDtypeStruct((groups, tokens, WIDTH), BF16),
        in_specs=[pl.BlockSpec((tokens, depth), lambda k: (0, k))]
        + [pl.BlockSpec((depth, WIDTH), lambda k, g=g: (k, group + g)) for g in range(groups)]
        + [ANY] * len(deps),
        out_specs=pl.BlockSpec((groups, tokens, WIDTH), lambda k: (0, 0, 0)),
        scratch_shapes=[pltpu.VMEM((groups, tokens, WIDTH), F32)],
        compiler_params=pltpu.CompilerParams(vmem_limit_bytes=VMEM_LIMIT),
        cost_estimate=COST,
        name="group_product",
    )(lhs, *[mat] * groups, *deps)


def squares(acts, deps):
    tokens, rows = acts.shape
    depth = largest_divisor(rows, 768, 128)

    def body(acts_ref, *rest):
        wide = acts_ref[...].astype(F32)
        rest[-1][...] = (wide * wide).astype(BF16).T

    return pl.pallas_call(
        body,
        grid=(rows // depth,),
        out_shape=jax.ShapeDtypeStruct((rows, tokens), BF16),
        in_specs=[pl.BlockSpec((tokens, depth), lambda k: (0, k))] + [ANY] * len(deps),
        out_specs=pl.BlockSpec((depth, tokens), lambda k: (k, 0)),
        compiler_params=pltpu.CompilerParams(vmem_limit_bytes=VMEM_LIMIT),
        cost_estimate=COST,
        name="squares",
    )(acts, *deps)


class Piece:
    def __init__(self, group, first, units, place):
        self.group, self.first, self.units, self.place = group, first, units, place


class Plan:
    def __init__(self, rows, cols):
        self.rows, self.cols = rows, cols
        self.half = rows // 2
        self.groups = cols // WIDTH
        self.unit = largest_divisor(self.half, UNIT_ROWS, 16)
        self.units = self.half // self.unit
        self.part_units = largest_divisor(self.units, MOST, 1)
        self.parts = self.units // self.part_units
        self.pieces = []
        for group in range(self.groups):
            first = 0
            while first < self.units:
                left = self.units - first
                units = min(self.part_units, left)
                if group == self.groups - 1:
                    units = max(min(units, LEAST), min(units, left // 3))
                units = min(units, self.part_units - first % self.part_units)
                self.pieces.append(Piece(group, first, units, len([p for p in self.pieces if p.group == group])))
                first += units

    def part_of(self, piece):
        return piece.first // self.part_units, piece.first % self.part_units


def cut(plan, tasks, deps):
    parts, tokens = plan.parts, tasks[0].shape[0]
    part = plan.half // parts
    unit = largest_divisor(part, 384, 128)
    halves = sum(task.shape[1] // plan.half for task in tasks)
    if unit % 128:
        wide = jnp.concatenate(tasks, axis=1).astype(F32)
        whole = (wide * wide).astype(BF16).T.reshape(halves, parts, part, tokens)
        return [whole[:, q] for q in range(parts)]
    ins, in_specs = [], []
    for task in tasks:
        for h in range(task.shape[1] // plan.half):
            for q in range(parts):
                ins.append(task)
                first = (h * parts + q) * (part // unit)
                in_specs.append(pl.BlockSpec((tokens, unit), lambda j, first=first: (0, first + j)))

    def body(*refs):
        for h in range(halves):
            for q in range(parts):
                wide = refs[h * parts + q][...].astype(F32)
                refs[len(refs) - parts + q][h] = (wide * wide).T.astype(BF16)

    return pl.pallas_call(
        body,
        grid=(part // unit,),
        out_shape=[jax.ShapeDtypeStruct((halves, part, tokens), BF16)] * parts,
        in_specs=in_specs + [ANY] * len(deps),
        out_specs=[pl.BlockSpec((halves, unit, tokens), lambda j: (0, j, 0))] * parts,
        compiler_params=pltpu.CompilerParams(vmem_limit_bytes=VMEM_LIMIT),
        cost_estimate=COST,
        name="cut",
    )(*ins, *deps)


def slot_call(plan, flags, last, fold=None, merge=None, gather=None, send=None, final=None, carry=None, cross=None, deps=()):
    unit = plan.unit
    ins, in_specs, outs, out_specs, aliases, kinds = [], [], [], [], {}, []
    most = lambda *some: max([part[0].units for part in some if part is not None] + [0])
    extra = lambda array: 0 if array is None else -(-array.shape[1] // unit)
    steps = max(
        most(final), most(gather, send) + extra(carry), most(fold, merge) + extra(cross)
    )

    def take(array, spec):
        ins.append(array)
        in_specs.append(spec)
        return len(ins) - 1

    def give(kind, shape, spec):
        outs.append(jax.ShapeDtypeStruct(shape, BF16))
        out_specs.append(spec)
        kinds.append(kind)
        return len(outs) - 1

    def at(piece, j):
        return jnp.minimum(j, piece.units - 1) if piece.units < steps else j

    def half_of(kind, flag):
        return {"sent": flag[0], "kept": 1 - flag[0]}.get(kind, kind)

    def rows_spec(piece, kind, width, column):
        return pl.BlockSpec(
            (unit, width),
            lambda j, flag: (half_of(kind, flag) * plan.units + piece.first + at(piece, j), column),
        )

    def half_spec(piece, kind):
        return pl.BlockSpec((None, unit, WIDTH), lambda j, flag: (half_of(kind, flag), at(piece, j), 0))

    def both_spec(piece):
        return pl.BlockSpec((2, unit, WIDTH), lambda j, flag: (0, at(piece, j), 0))

    def take_gsq(gsq, h):
        array, g = gsq
        shape = (array.shape[0], None, None) + array.shape[3:]
        return take(array, pl.BlockSpec(shape, lambda j, flag: (0, h, g, 0, 0)))

    def give_long(kind, count, units, tail):
        total = units + extra(tail)
        last_block = total - 1
        out = give(
            kind,
            (count, units * unit + (0 if tail is None else tail.shape[1]), WIDTH),
            pl.BlockSpec((count, unit, WIDTH), lambda j, flag: (0, jnp.minimum(j, last_block), 0)),
        )
        if tail is None:
            return out, None
        blocks = extra(tail) - 1
        spec = pl.BlockSpec((2, unit, WIDTH), lambda j, flag: (0, jnp.clip(j - units, 0, blocks), 0))
        return out, (take(tail, spec), units, total)

    def take_side(piece, kind, tasks):
        ids = []
        squared, gsq = tasks
        for h, asq in enumerate(squared):
            if isinstance(asq, list):
                q, offset = plan.part_of(piece)
                array = asq[q]
                spec = pl.BlockSpec(
                    (array.shape[0], None, unit, array.shape[3]),
                    lambda j, flag: (0, half_of(kind, flag), offset + at(piece, j), 0),
                )
            else:
                array, spec = asq, rows_spec(piece, kind, asq.shape[1], 0)
            ids.append((take(array, spec), take_gsq(gsq, h)))
        return ids

    def take_other(piece, tasks):
        parts, gsq = tasks
        q, offset = plan.part_of(piece)
        array = parts[q]
        return [
            (
                take(
                    array,
                    pl.BlockSpec(
                        (array.shape[0], None, unit, array.shape[3]),
                        lambda j, flag, h=h: (0, h, offset + at(piece, j), 0),
                    ),
                ),
                take_gsq(gsq, h),
            )
            for h in range(gsq[0].shape[1])
        ]

    if fold is not None:
        piece, weight, received, side = fold
        fold_w = take(weight, rows_spec(piece, "sent", WIDTH, piece.group))
        fold_in = take(received, half_spec(piece, "sent"))
        fold_side = take_side(piece, "sent", side)
    if merge is not None:
        piece, weight, received, side, mean, other = merge
        merge_w = take(weight, rows_spec(piece, "kept", WIDTH, piece.group))
        merge_in = take(received, half_spec(piece, "kept"))
        merge_side = take_side(piece, "kept", side)
        merge_mean = take(mean, half_spec(piece, 0))
        merge_other = take_other(piece, other)
    across = [part for part in (fold, merge) if part is not None]
    if across:
        sections = 1 if fold is None else 2
        across_out, across_tail = give_long("across", sections, most(fold, merge), cross)
    if gather is not None or send is not None:
        if gather is not None:
            piece, kept, came, slot = gather
            gather_kept, gather_came = take(kept, half_spec(piece, slot)), take(came, half_spec(piece, slot))
        if send is not None:
            piece, inward, own = send
            if own:
                send_in = [take(inward, rows_spec(piece, h, WIDTH, piece.group)) for h in (0, 1)]
            else:
                send_in = [take(inward, half_spec(piece, h)) for h in (0, 1)]
        pass_out, pass_tail = give_long("pass", 2, most(gather, send), carry)
    if final is not None:
        piece, own, came, buffer = final
        final_own, final_in = take(own, both_spec(piece)), take(came, both_spec(piece))
        first, group = piece.first, piece.group
        final_piece = piece
        final_out = give(
            "final",
            (2, plan.half, plan.cols),
            pl.BlockSpec((2, unit, WIDTH), lambda j, flag: (0, first + at(final_piece, j), group)),
        )
        if buffer is not None:
            aliases[1 + take(buffer, ANY)] = final_out
    for dep in deps:
        take(dep, ANY)

    def body(flag, *refs):
        inr, outr = refs[: len(ins)], refs[len(ins) :]
        j = pl.program_id(0)

        def during(part, extra=True):
            units = part[0].units
            if units < steps:
                return pl.when((j < units) & extra)
            return pl.when(extra) if extra is not True else (lambda f: f())

        def fisher(task):
            ref = inr[task[0]]
            if len(ref.shape) == 3:
                asq = jnp.concatenate([ref[b] for b in range(ref.shape[0])], axis=1)
            else:
                asq = ref[...]
            gsq = inr[task[1]][...]
            return jnp.dot(asq, gsq.reshape(-1, gsq.shape[-1]), preferred_element_type=F32)

        def summed(tasks):
            return functools.reduce(lambda a, b: a + b, [fisher(task) for task in tasks])

        def follow(out, tail):
            ref, start, stop = tail

            @pl.when((j >= start) & (j < stop))
            def _():
                outr[out][...] = inr[ref][...]

        if carry is not None:
            follow(pass_out, pass_tail)
        if cross is not None:
            follow(across_out, across_tail)
        if send is not None:

            @during(send, flag[1] != last)
            def _():
                for h in (0, 1):
                    outr[pass_out][h] = inr[send_in[h]][...]

        if gather is not None:

            @during(gather, flag[1] == last)
            def _():
                outr[pass_out][flag[0]] = inr[gather_came][...]
                outr[pass_out][1 - flag[0]] = inr[gather_kept][...]

        if final is not None:

            @during(final, flag[1] == last)
            def _():
                outr[final_out][...] = inr[final_own][...]

            @during(final, flag[1] != last)
            def _():
                outr[final_out][...] = inr[final_in][...]

        if fold is not None:

            @during(fold)
            def _():
                here, before = fisher(fold_side[0]), summed(fold_side[1:])
                total = here + before
                mean = (here * inr[fold_w][...].astype(F32) + before * inr[fold_in][...].astype(F32)) / total
                outr[across_out][0] = jnp.where(total > 0, mean, 0.0).astype(BF16)

        if merge is not None:

            @during(merge)
            def _():
                here, before, there = fisher(merge_side[0]), summed(merge_side[1:]), summed(merge_other)
                numer = (
                    here * inr[merge_w][...].astype(F32)
                    + before * inr[merge_in][...].astype(F32)
                    + there * inr[merge_mean][...].astype(F32)
                )
                outr[across_out][sections - 1] = (numer / (here + before + there + 1e-6)).astype(BF16)

    result = pl.pallas_call(
        body,
        grid_spec=pltpu.PrefetchScalarGridSpec(
            num_scalar_prefetch=1, grid=(steps,), in_specs=in_specs, out_specs=out_specs
        ),
        out_shape=outs,
        input_output_aliases=aliases,
        compiler_params=pltpu.CompilerParams(vmem_limit_bytes=VMEM_LIMIT),
        cost_estimate=COST,
        name="slot",
    )(flags, *ins)
    return dict(zip(kinds, result))


def local(sizes, activations, weights, labels, prototypes):
    tasks, rows_n, cols_n = sizes
    side_n = tasks // 2
    last = side_n - 1
    acts, weight, label_row, protos = activations[0], weights[0], labels[0], prototypes[0]
    block_tokens = acts.shape[0]
    tokens = block_tokens * cols_n
    share = tokens // rows_n
    plan = Plan(*weight.shape)
    place, row = lax.axis_index("task"), lax.axis_index("row")
    depth = jnp.minimum(place, tasks - 1 - place)
    sent = (place >= side_n).astype(jnp.int32)
    flags = jnp.stack([sent, depth.astype(jnp.int32)])

    mirrored = lambda pairs: pairs + [(tasks - 1 - a, tasks - 1 - b) for a, b in pairs]
    step_in = lambda d: mirrored([(d, d + 1)])
    step_out = lambda d: mirrored([(d + 1, d)])
    all_in = mirrored([(d, d + 1) for d in range(last)])
    send_in = lambda x: lax.ppermute(x, "task", all_in)
    send_mid = lambda x: lax.ppermute(x, "task", [(last, side_n), (side_n, last)])
    swap = lambda x: lax.ppermute(x, "task", step_in(last - 1) + step_out(last - 1))
    send_row = lambda x, s: lax.ppermute(x, "row", [(i, (i + s) % rows_n) for i in range(rows_n)])

    def sum_rows(full):
        cut_out = lambda r: lax.dynamic_slice_in_dim(full, r * share, share, 1)
        got = [send_row(cut_out((row + s) % rows_n), s) for s in range(1, rows_n)]
        total = cut_out(row).astype(F32)
        for part in got:
            total = total + part.astype(F32)
        return total

    def gather_rows(part):
        full = jnp.zeros((rows_n,) + part.shape, part.dtype)
        full = lax.dynamic_update_index_in_dim(full, part, row, 0)
        for s in range(1, rows_n):
            full = lax.dynamic_update_index_in_dim(full, send_row(part, s), (row - s) % rows_n, 0)
        return full

    full_acts = lax.all_gather(acts, "col", axis=0, tiled=True)

    near = [acts]
    for _ in range(last):
        near.append(send_in(near[-1]))
    cross = [send_mid(lax.dynamic_slice_in_dim(x, sent * plan.half, plan.half, 1)) for x in near]

    my_labels = lax.dynamic_slice_in_dim(label_row, row * share, share, 0)
    onehot = (my_labels[:, None] == lax.broadcasted_iota(jnp.int32, (share, protos.shape[0]), 1)).astype(BF16)
    target = jnp.dot(onehot, protos, preferred_element_type=F32)

    def squared_grad(product, group):
        groups = product.shape[0]
        wanted = target[:, group * WIDTH : (group + groups) * WIDTH].reshape(share, groups, WIDTH)
        grad = sum_rows(product) - jnp.moveaxis(wanted, 1, 0)
        return (grad * grad).astype(BF16)

    def packed(array):
        flat = array.reshape(-1, WIDTH)
        fill = -flat.shape[0] % 32
        return jnp.pad(flat, ((0, fill), (0, 0))).reshape(2, -1, WIDTH)

    def unpacked(array, shape):
        size = functools.reduce(lambda a, b: a * b, shape[:-1])
        rows = size + -size % 32
        return array[:, array.shape[1] - rows // 2 :].reshape(-1, WIDTH)[:size].reshape(shape)

    class Gradient:
        def __init__(self, group, groups):
            self.first, self.groups = group, groups
            self.outer, self.far = [None] * groups, [[None, None] for _ in range(groups)]

        def start(self, product):
            self.near = [squared_grad(product, self.first)]
            for _ in range(last - 1):
                self.near.append(send_in(self.near[-1]))

        def inwards(self, g):
            return packed(jnp.stack([x[g] for x in self.near]))

        def inside(self, g, came):
            self.outer[g] = unpacked(came, (last, share, WIDTH))
            if all(x is not None for x in self.outer):
                stacked = jnp.concatenate([self.near[0][None], jnp.stack(self.outer, 1)])
                self.own = gather_rows(stacked)

        def outside(self, g, part, came):
            self.far[g][part] = unpacked(came, (last if part else 1, share, WIDTH))
            if all(x is not None for pair in self.far for x in pair):
                self.oth = gather_rows(jnp.stack([jnp.concatenate(pair) for pair in self.far], 1))

    count = len(plan.pieces)
    batches = [Gradient(0, 1)]
    while batches[-1].first + batches[-1].groups < plan.groups:
        group = batches[-1].first + batches[-1].groups
        batches.append(Gradient(group, min(2, plan.groups - group)))
    batch_of = {b.first + g: b for b in batches for g in range(b.groups)}
    own_of = lambda piece: (batch_of[piece.group].own, piece.group - batch_of[piece.group].first)
    other_of = lambda piece: (batch_of[piece.group].oth, piece.group - batch_of[piece.group].first)

    def inward(index):
        piece = plan.pieces[index]
        if last == 1:
            return (piece, weight, True)
        a, b = piece.first * plan.unit, (piece.first + piece.units) * plan.unit
        q, offset = plan.part_of(piece)
        offset *= plan.unit
        columns = slice(piece.group * WIDTH, (piece.group + 1) * WIDTH)
        mine = weight.reshape(2, plan.half, plan.cols)[:, a:b, columns]
        squared = [own_square.reshape(2, plan.half, tokens)[:, a:b]]
        for task in outer_parts[: last - 1]:
            blocks = task[q][:, :, offset : offset + b - a]
            squared.append(jnp.moveaxis(blocks, 0, 2).reshape(2, b - a, tokens))
        own, g = own_of(piece)
        gsq = jnp.moveaxis(own[:, :, g], 0, 1).reshape(side_n, tokens, WIDTH)
        shares = [
            jnp.einsum("hrt,tc->hrc", s, g, preferred_element_type=F32)
            for s, g in zip(squared, gsq)
        ]
        mean, before = mine, jnp.zeros(mine.shape, F32)
        for d in range(1, last):
            came = lax.ppermute(mean, "task", step_in(d - 1)).astype(F32)
            before = before + shares[d]
            total = shares[0] + before
            value = (shares[0] * mine.astype(F32) + before * came) / total
            mean = jnp.where(depth == 0, mine, jnp.where(total > 0, value, 0.0).astype(BF16))
        return (piece, mean, False)

    def outward(came):
        for d in reversed(range(last - 1)):
            arrived = lax.ppermute(came, "task", step_out(d))
            came = jnp.where(depth == d, arrived, came)
        return came

    sent_pass, came_pass = {}, {}

    def start_pass(slot, got):
        if "pass" in got:
            sent_pass[slot] = got["pass"]
            came_pass[slot] = swap(got["pass"])

    if last == 1:
        start_pass(-2, slot_call(plan, flags, last, send=inward(0), deps=[near[-1], cross[0]]))
    lead = batches[0]
    product = group_product(full_acts, weight, 0, 1, deps=list(sent_pass.values()) + cross[1:])
    outer_cuts = [cut(plan, [task], [product]) for task in near[1:]]
    other_cuts = cut(plan, cross, [product])
    gather_col = lambda x: lax.all_gather(x, "col", axis=0)
    outer_parts = [[None] * plan.parts for _ in range(last)]
    other_parts = []
    for q in range(plan.parts):
        for h in range(last):
            outer_parts[h][q] = gather_col(outer_cuts[h][q])
        other_parts.append(gather_col(other_cuts[q]))

    def at_once(b, product):
        b.start(product)
        came = swap(jnp.stack(b.near))
        b.outer = [came[:, g] for g in range(b.groups)]
        stacked = jnp.concatenate([b.near[0][None], came])
        b.own = gather_rows(stacked)
        crossed = send_mid(stacked)
        b.oth = gather_rows(crossed)
        return crossed

    lead_far = at_once(lead, product)
    own_square = squares(full_acts, [lead.near[0], outer_cuts[0][0], other_cuts[0]])
    carries, crossings, starts = {}, {}, {}

    def ship(slot, b):
        for g in range(b.groups):
            carries[slot + g] = (b, g)
            crossings[slot + g] = (b, g, 0)
            crossings[slot + LAG + g] = (b, g, 1)

    if last == 1 and count > 1:
        start_pass(-1, slot_call(plan, flags, last, send=inward(1), deps=[own_square, lead.outer[0]]))
    product = own_square
    for b in batches[1:]:
        first = min(i for i, p in enumerate(plan.pieces) if p.group == b.first)
        ready = first - (0 if last == 1 else LAG) - LAG - (b.groups - 1)
        if ready >= 2:
            starts[ready - 2] = b
            continue
        deps = [product, lead.outer[0]] + list(sent_pass.values())[-1:]
        product = group_product(full_acts, weight, b.first, b.groups, deps=deps)
        if ready >= 0:
            b.start(product)
            ship(0, b)
        else:
            at_once(b, product)
    if last > 1:
        for index in range(min(LAG, count)):
            start_pass(index - LAG, slot_call(plan, flags, last, send=inward(index)))

    sent_mid, came_mid, places = {}, {}, {}
    buffer = None
    results, finished = [], 0
    chain = [product, lead_far] + list(sent_pass.values())[-1:]
    for slot in range(count + 3 * LAG):
        deps = list(chain)
        stage = {}
        now = lambda index: 0 <= index < count
        side_of = lambda piece: ([own_square] + outer_parts, own_of(piece))
        if slot - LAG in carries:
            b, g = carries[slot - LAG]
            b.inside(g, came_pass[slot - LAG])
        if slot - LAG in crossings:
            b, g, part = crossings[slot - LAG]
            b.outside(g, part, came_mid[slot - LAG])
        if slot in crossings:
            b, g, part = crossings[slot]
            stage["cross"] = packed(b.outer[g] if part else b.near[0][g])
        if slot in carries:
            b, g = carries[slot]
            stage["carry"] = b.inwards(g)
        if now(slot):
            piece = plan.pieces[slot]
            stage["fold"] = (piece, weight, came_pass[slot - LAG], side_of(piece))
        if now(slot + LAG):
            stage["send"] = inward(slot + LAG)
        index = slot - LAG
        if now(index):
            piece = plan.pieces[index]
            stage["merge"] = (
                piece,
                weight,
                came_pass[index - LAG],
                side_of(piece),
                came_mid[index],
                (other_parts, other_of(piece)),
            )
        index = slot - 2 * LAG
        if now(index):
            stage["gather"] = (plan.pieces[index], sent_mid[slot - LAG], came_mid[slot - LAG], places[slot - LAG])
        index = slot - 3 * LAG
        if now(index):
            stage["final"] = (
                plan.pieces[index],
                sent_pass[slot - LAG],
                outward(came_pass[slot - LAG]),
                buffer,
            )
        got = slot_call(plan, flags, last, deps=deps, **stage)
        chain = [got[name] for name in ("across", "pass") if name in got][:1]
        if "across" in got:
            sent_mid[slot], came_mid[slot] = got["across"], send_mid(got["across"])
            places[slot] = got["across"].shape[0] - 1
        start_pass(slot, got)
        if "final" in got:
            buffer = got["final"]
            done = plan.pieces[slot - 3 * LAG]
            stored = done.group + 1 - finished
            if done.first + done.units == plan.units and (stored == 2 or done.group == plan.groups - 1):
                whole = buffer.reshape(plan.rows, plan.cols)
                out = group_product(full_acts, whole, finished, stored)
                chain = [out]
                results.append(sum_rows(out).astype(BF16))
                finished = done.group + 1
        if slot in starts:
            b = starts[slot]
            product = group_product(full_acts, weight, b.first, b.groups, deps=chain)
            chain = [product]
            b.start(product)
            ship(slot + 1, b)
    result = jnp.moveaxis(jnp.concatenate(results), 0, 1).reshape(1, share, plan.cols)
    return buffer.reshape(plan.rows, plan.cols), result


def solution(mesh):
    placed = (
        P("task", "col", "row"),
        P("task", "row", "col"),
        P("task", None),
        P("task", None, "col"),
    )
    sizes = (mesh.shape["task"], mesh.shape["row"], mesh.shape["col"])
    return jax.shard_map(
        functools.partial(local, sizes),
        mesh=mesh,
        in_specs=placed,
        out_specs=(P("row", "col"), P("task", "row", "col")),
        check_vma=False,
    )
```

time: 1700 us -> 717 us (0.42)
  waiting for transfers between devices: 1590 us -> 201 us
  Pallas kernels: 0 us -> 276 us
  starting transfers between devices: 0.42 us -> 166 us
  matrix products: 65.1 us -> 0.37 us
  local copies, waits for them, and re-layouts: 17.9 us -> 43.8 us
    reduce_scatter x3 -> x0, waiting for transfers between devices: 1190 us -> none  [the longest x1 585 us: local(): lax.psum_scatter(fisher, 'task', scatter_dimension=0, tiled=True)]
    all_gather x1 -> x6, waiting for transfers between devices: 304 us -> 1.16 us  [local(): gather_col = lambda x: lax.all_gather(x, 'col', axis=0)]
    pallas_call x0 -> x35, Pallas kernels: none -> 276 us  [the longest x26 190 us: slot_call(): pl.pallas_call(body, grid_spec=pltpu.PrefetchScalarGridSpec(num_scalar_pr...]
    ppermute x0 -> x61, waiting for transfers between devices: none -> 194 us  [the longest x25 134 us: local(): lax.ppermute(x, 'task', step_in(last - 1) + step_out(last - 1))]
    ppermute x0 -> x61, starting transfers between devices: none -> 165 us  [the longest x25 115 us: local(): lax.ppermute(x, 'task', step_in(last - 1) + step_out(last - 1))]
    dot_general x3 -> x1, matrix products: 65.1 us -> 0.37 us  [local(): target = jnp.dot(onehot, protos, preferred_element_type=F32)]
    all_gather x1, waiting for transfers between devices: 55.2 us -> 3.85 us  [local(): full_acts = lax.all_gather(acts, 'col', axis=0, tiled=True)]
    psum x1 -> x0, waiting for transfers between devices: 45.9 us -> none  [local(): lax.psum(partial_out.astype(jnp.bfloat16), 'row').astype(jnp.float32)]
  transfers between devices with their start and end apart: 6 -> 68, of which waited for: 6 -> 26; matrix products, arithmetic and copies ran while one was open for 0% -> 3% of each run, Pallas kernels for 0% -> 37%
where the time goes in v1:
time: 717 us; the launch traced here: 707 us
  Pallas kernels  276 us (38%)
  waiting for transfers between devices  201 us (28%)
  starting transfers between devices  166 us (23%)
  local copies, waits for them, and re-layouts  43.8 us (6%)
  between operations  15.5 us (2%)
    pallas_call x26, Pallas kernels, slot_call(): pl.pallas_call(body, grid_spec=pltpu.PrefetchScalarGridSpec(num_scalar_pr...  190 us
    ppermute x25, waiting for transfers between devices, local(): lax.ppermute(x, 'task', step_in(last - 1) + step_out(last - 1))  134 us
    ppermute x25, starting transfers between devices, local(): lax.ppermute(x, 'task', step_in(last - 1) + step_out(last - 1))  115 us
    pallas_call x6, Pallas kernels, group_product(): pl.pallas_call(body, grid=(steps,), out_shape=jax.ShapeDtypeStruct((group...  67.5 us
    ppermute x1, waiting for transfers between devices, local(): send_in = lambda x: lax.ppermute(x, 'task', all_in)  35.1 us
    ppermute x23, starting transfers between devices, local(): lax.ppermute(x, 'task', [(last, side_n), (side_n, last)])  30.6 us
    ppermute x12, waiting for transfers between devices, local(): lax.ppermute(x, 'row', [(i, (i + s) % rows_n) for i in range(rows_n)])  24.4 us
    unnamed x113, local copies, waits for them, and re-layouts  22.9 us
  transfers between devices with their start and end apart: 68, of which 26 were waited for; matrix products, arithmetic and copies ran while one was open for 3% of the time, Pallas kernels for 37%

profile of v1, /device:TPU:0, one launch (start us, length us, event | category | flops | bytes accessed | tf_op | source)
XLA Modules:
  0.0 706.5 jit_solution(10905262259052670980)
XLA Ops:
  16.0 35.1 %collective-permute-done.refs_2_.refs_0_.refs_1_.refs_3_.refs_4_.refs_5_ = bf16[128,6912]{1,0:T(8,128)(2,1)S(1)} collective-permute-done((bf16[128,6912]{1,0:T(8,128)(2,1)}, bf16[128,6912]{1,0:T(8,128)(2,1)S(1)}, u32[]{:S(2)}, u32[]{:S(2)}) %collective-permute-start) | collective-permute-done | bytes 1769504 | tf_op jit(solution)/shard_map/ppermute | solution.py:396
  86.7 13.6 %collective-permute-start.4 = (bf16[1,1,256,256]{3,2,0,1:T(8,128)(2,1)S(1)}, bf16[1,1,256,256]{3,2,0,1:T(8,128)(2,1)S(1)}, u32[]{:S(2)}, u32[]{:S(2)}) collective-permute-start(bf16[1,1,256,256]{3,2,0,1:T(8,128)(2,1)S(1)} %bitcast.274), channel_id=1, source_target_pairs={{0,8},{24,16},{8,0},{16,24},{1,9},{25,17},{9,1},{17,25},{2,10},{26... | collective-permute-start | bytes 393224 | tf_op jit(solution)/shard_map/ppermute | solution.py:398
  100.3 10.2 %squares.1.refs_2_.rest_2_.refs_8_ = bf16[6912,512]{1,0:T(8,128)(2,1)} custom-call(bf16[512,6912]{1,0:T(8,128)(2,1)} %bitcast.216, bf16[1,256,256]{2,1,0:T(8,128)(2,1)} %copy-done.33, bf16[2,1152,128]{2,1,0:T(8,128)(2,1)} %get-tuple-element.66.rest_1_, bf16[2,1152,128]{2,1,0:T(8,128)(2,1)} %get-tuple-element.67.rest_2_), custom_call_target="tpu_custom_call" | custom-call | tf_op jit(solution)/shard_map/squares/pallas_call | solution.py:76
  115.1 13.3 %group_product.7.refs_10_ = bf16[2,512,256]{2,1,0:T(8,128)(2,1)} custom-call(bf16[512,6912]{1,0:T(8,128)(2,1)} %bitcast.217, bf16[6912,1280]{1,0:T(8,128)(2,1)} %bitcast.109, bf16[6912,1280]{1,0:T(8,128)(2,1)} %bitcast.110, bf16[6912,512]{1,0:T(8,128)(2,1)} %squares.1.refs_2_.rest_2_.refs_8_, bf16[1,256,256]{2,1,0:T(8,128)(2,1)} %bitcast.273, ...), custom_call_target="tpu_custom_call" | custom-call | tf_op jit(solution)/shard_map/group_product/pallas_call | solution.py:53
  168.1 15.5 %collective-permute-done.11.refs_1_.refs_7_ = bf16[2,1280,256]{2,1,0:T(8,128)(2,1)} collective-permute-done((bf16[2,1280,256]{2,1,0:T(8,128)(2,1)}, bf16[2,1280,256]{2,1,0:T(8,128)(2,1)}, u32[]{:S(2)}, u32[]{:S(2)}) %collective-permute-start.11) | collective-permute-done | bytes 1310752 | tf_op jit(solution)/shard_map/ppermute | solution.py:398
  184.5 24.6 %collective-permute-done.10.refs_1_.refs_7_ = bf16[2,1280,256]{2,1,0:T(8,128)(2,1)S(1)} collective-permute-done((bf16[2,1280,256]{2,1,0:T(8,128)(2,1)}, bf16[2,1280,256]{2,1,0:T(8,128)(2,1)S(1)}, u32[]{:S(2)}, u32[]{:S(2)}) %collective-permute-start.10) | collective-permute-done | bytes 1310752 | tf_op jit(solution)/shard_map/ppermute | solution.py:398
  211.5 9.1 %slot.30 = (bf16[2,1280,256]{2,1,0:T(8,128)(2,1)}, bf16[2,1152,256]{2,1,0:T(8,128)(2,1)}) custom-call(s32[2]{0:T(128)} %pad_add_fusion.flag, bf16[6912,1280]{1,0:T(8,128)(2,1)} %bitcast.117, bf16[2,1280,256]{2,1,0:T(8,128)(2,1)} %collective-permute-done.11.refs_1_.refs_7_, bf16[6912,512]{1,0:T(8,128)(2,1)} %squares.1.refs_2_.rest_2_.refs_8_, ...), custom_call_target="tpu_custom_call" | custom-call | tf_op jit(solution)/shard_map/slot/pallas_call | solution.py:364
  223.6 9.0 %slot.31 = (bf16[2,1280,256]{2,1,0:T(8,128)(2,1)}, bf16[2,1152,256]{2,1,0:T(8,128)(2,1)}) custom-call(s32[2]{0:T(128)} %pad_add_fusion.flag, bf16[6912,1280]{1,0:T(8,128)(2,1)} %bitcast.121, bf16[2,1280,256]{2,1,0:T(8,128)(2,1)} %copy-done.21, bf16[6912,512]{1,0:T(8,128)(2,1)} %squares.1.refs_2_.rest_2_.refs_8_, bf16[2,2,2,256,256]{4,3,2,1,0:T(8,128)(2,1)} %copy-done.3, ...), custom_call_target="tpu_custom_call" | custom-call | tf_op jit(solution)/shard_map/slot/pallas_call | solution.py:364
  239.7 25.9 %collective-permute-done.20.refs_1_.refs_7_ = bf16[2,1152,256]{2,1,0:T(8,128)(2,1)S(1)} collective-permute-done((bf16[2,1152,256]{2,1,0:T(8,128)(2,1)}, bf16[2,1152,256]{2,1,0:T(8,128)(2,1)S(1)}, u32[]{:S(2)}, u32[]{:S(2)}) %collective-permute-start.20) | collective-permute-done | bytes 1179680 | tf_op jit(solution)/shard_map/ppermute | solution.py:398
  266.7 8.9 %slot.32 = (bf16[2,1152,256]{2,1,0:T(8,128)(2,1)}, bf16[2,1152,256]{2,1,0:T(8,128)(2,1)}) custom-call(s32[2]{0:T(128)} %pad_add_fusion.flag, bf16[6912,1280]{1,0:T(8,128)(2,1)} %bitcast.125, bf16[2,1152,256]{2,1,0:T(8,128)(2,1)} %copy-done.27, bf16[6912,512]{1,0:T(8,128)(2,1)} %squares.1.refs_2_.rest_2_.refs_8_, bf16[2,2,2,256,256]{4,3,2,1,0:T(8,128)(2,1)} %copy-done.3, ...), custom_call_target="tpu_custom_call" | custom-call | tf_op jit(solution)/shard_map/slot/pallas_call | solution.py:364
  275.6 13.1 %group_product.8.refs_23_ = bf16[2,512,256]{2,1,0:T(8,128)(2,1)} custom-call(bf16[512,6912]{1,0:T(8,128)(2,1)} %bitcast.218, bf16[6912,1280]{1,0:T(8,128)(2,1)} %bitcast.129, bf16[6912,1280]{1,0:T(8,128)(2,1)} %bitcast.130, bf16[2,1152,256]{2,1,0:T(8,128)(2,1)} %get-tuple-element.80.rest_2_.refs_18_), custom_call_target="tpu_custom_call" | custom-call | tf_op jit(solution)/shard_map/group_product/pallas_call | solution.py:53
  309.7 9.8 %slot.33 = (bf16[2,1280,256]{2,1,0:T(8,128)(2,1)}, bf16[2,1280,256]{2,1,0:T(8,128)(2,1)}) custom-call(s32[2]{0:T(128)} %pad_add_fusion.flag, bf16[6912,1280]{1,0:T(8,128)(2,1)} %bitcast.131, bf16[2,1152,256]{2,1,0:T(8,128)(2,1)} %collective-permute-done.16.refs_1_.refs_7_, bf16[6912,512]{1,0:T(8,128)(2,1)} %squares.1.refs_2_.rest_2_.refs_8_, ...), custom_call_target="tpu_custom_call" | custom-call | tf_op jit(solution)/shard_map/slot/pallas_call | solution.py:364
  321.6 10.3 %slot.34 = (bf16[2,1280,256]{2,1,0:T(8,128)(2,1)}, bf16[2,1280,256]{2,1,0:T(8,128)(2,1)}, bf16[2,3456,1280]{2,1,0:T(8,128)(2,1)}) custom-call(s32[2]{0:T(128)} %pad_add_fusion.flag, bf16[6912,1280]{1,0:T(8,128)(2,1)} %bitcast.135, bf16[2,1152,256]{2,1,0:T(8,128)(2,1)} %collective-permute-done.24.refs_1_.refs_24_.refs_7_, ...), custom_call_target="tpu_custom_call" | custom-call | tf_op jit(solution)/shard_map/slot/pallas_call | solution.py:364
  335.9 15.6 %collective-permute-done.22.refs_1_.refs_23_.refs_7_ = bf16[2,1280,256]{2,1,0:T(8,128)(2,1)S(1)} collective-permute-done((bf16[2,1280,256]{2,1,0:T(8,128)(2,1)}, bf16[2,1280,256]{2,1,0:T(8,128)(2,1)S(1)}, u32[]{:S(2)}, u32[]{:S(2)}) %collective-permute-start.22) | collective-permute-done | bytes 1310752 | tf_op jit(solution)/shard_map/ppermute | solution.py:398
  352.6 10.2 %slot.35 = (bf16[2,1280,256]{2,1,0:T(8,128)(2,1)}, bf16[2,1152,256]{2,1,0:T(8,128)(2,1)}, bf16[2,3456,1280]{2,1,0:T(8,128)(2,1)}) custom-call(s32[2]{0:T(128)} %pad_add_fusion.flag, bf16[6912,1280]{1,0:T(8,128)(2,1)} %bitcast.142, bf16[2,1280,256]{2,1,0:T(8,128)(2,1)} %copy-done.11, ...), custom_call_target="tpu_custom_call", output_to_operand_aliasing={{2}: (25, {})} | custom-call | tf_op jit(solution)/shard_map/slot/pallas_call | solution.py:364
  367.9 11.7 %collective-permute-done.27.refs_1_.refs_23_.refs_7_ = bf16[2,1280,256]{2,1,0:T(8,128)(2,1)S(1)} collective-permute-done((bf16[2,1280,256]{2,1,0:T(8,128)(2,1)}, bf16[2,1280,256]{2,1,0:T(8,128)(2,1)S(1)}, u32[]{:S(2)}, u32[]{:S(2)}) %collective-permute-start.27) | collective-permute-done | bytes 1310752 | tf_op jit(solution)/shard_map/ppermute | solution.py:398
  380.7 10.4 %slot.36 = (bf16[2,1280,256]{2,1,0:T(8,128)(2,1)}, bf16[2,1152,256]{2,1,0:T(8,128)(2,1)}, bf16[2,3456,1280]{2,1,0:T(8,128)(2,1)}) custom-call(s32[2]{0:T(128)} %pad_add_fusion.flag, bf16[6912,1280]{1,0:T(8,128)(2,1)} %bitcast.143, bf16[2,1280,256]{2,1,0:T(8,128)(2,1)} %copy-done.10, ...), custom_call_target="tpu_custom_call", output_to_operand_aliasing={{2}: (25, {})} | custom-call | tf_op jit(solution)/shard_map/slot/pallas_call | solution.py:364
  405.9 9.9 %slot.37 = (bf16[2,1152,256]{2,1,0:T(8,128)(2,1)}, bf16[2,1152,256]{2,1,0:T(8,128)(2,1)}, bf16[2,3456,1280]{2,1,0:T(8,128)(2,1)}) custom-call(s32[2]{0:T(128)} %pad_add_fusion.flag, bf16[6912,1280]{1,0:T(8,128)(2,1)} %bitcast.147, bf16[2,1152,256]{2,1,0:T(8,128)(2,1)} %copy-done.12, ...), custom_call_target="tpu_custom_call", output_to_operand_aliasing={{2}: (24, {})} | custom-call | tf_op jit(solution)/shard_map/slot/pallas_call | solution.py:364
  431.2 9.9 %slot.38 = (bf16[2,1152,256]{2,1,0:T(8,128)(2,1)}, bf16[2,1152,256]{2,1,0:T(8,128)(2,1)}, bf16[2,3456,1280]{2,1,0:T(8,128)(2,1)}) custom-call(s32[2]{0:T(128)} %pad_add_fusion.flag, bf16[6912,1280]{1,0:T(8,128)(2,1)} %bitcast.151, bf16[2,1152,256]{2,1,0:T(8,128)(2,1)} %copy-done.16, ...), custom_call_target="tpu_custom_call", output_to_operand_aliasing={{2}: (24, {})} | custom-call | tf_op jit(solution)/shard_map/slot/pallas_call | solution.py:364
  441.1 12.8 %collective-permute-start.38 = (bf16[2,1152,256]{2,1,0:T(8,128)(2,1)}, bf16[2,1152,256]{2,1,0:T(8,128)(2,1)S(1)}, u32[]{:S(2)}, u32[]{:S(2)}) collective-permute-start(bf16[2,1152,256]{2,1,0:T(8,128)(2,1)} %get-tuple-element.100.refs_21_), channel_id=1, source_target_pairs={{0,8},{24,16},{8,0},{16,24},{1,9},{25,17},{9,1},{17,25},{2,10},{26... | collective-permute-start | bytes 3538952 | tf_op jit(solution)/shard_map/ppermute | solution.py:398
  458.1 9.7 %slot.39 = (bf16[2,1152,256]{2,1,0:T(8,128)(2,1)}, bf16[2,1152,256]{2,1,0:T(8,128)(2,1)}, bf16[2,3456,1280]{2,1,0:T(8,128)(2,1)}) custom-call(s32[2]{0:T(128)} %pad_add_fusion.flag, bf16[6912,1280]{1,0:T(8,128)(2,1)} %bitcast.155, bf16[2,1152,256]{2,1,0:T(8,128)(2,1)} %copy-done.20, ...), custom_call_target="tpu_custom_call", output_to_operand_aliasing={{2}: (24, {})} | custom-call | tf_op jit(solution)/shard_map/slot/pallas_call | solution.py:364
  476.6 13.0 %group_product.9.refs_24_ = bf16[2,512,256]{2,1,0:T(8,128)(2,1)} custom-call(bf16[512,6912]{1,0:T(8,128)(2,1)} %bitcast.219, bf16[6912,1280]{1,0:T(8,128)(2,1)} %bitcast.181, bf16[6912,1280]{1,0:T(8,128)(2,1)} %bitcast.182), custom_call_target="tpu_custom_call" | custom-call | tf_op jit(solution)/shard_map/group_product/pallas_call | solution.py:53
  490.6 9.7 %slot.40 = (bf16[2,1152,256]{2,1,0:T(8,128)(2,1)}, bf16[2,1152,256]{2,1,0:T(8,128)(2,1)}, bf16[2,3456,1280]{2,1,0:T(8,128)(2,1)}) custom-call(s32[2]{0:T(128)} %pad_add_fusion.flag, bf16[6912,1280]{1,0:T(8,128)(2,1)} %bitcast.160, bf16[2,1152,256]{2,1,0:T(8,128)(2,1)} %copy-done.14, ...), custom_call_target="tpu_custom_call", output_to_operand_aliasing={{2}: (24, {})} | custom-call | tf_op jit(solution)/shard_map/slot/pallas_call | solution.py:364
  506.4 9.0 %slot.41 = (bf16[2,1152,256]{2,1,0:T(8,128)(2,1)}, bf16[2,1152,256]{2,1,0:T(8,128)(2,1)}, bf16[2,3456,1280]{2,1,0:T(8,128)(2,1)}) custom-call(s32[2]{0:T(128)} %pad_add_fusion.flag, bf16[6912,1280]{1,0:T(8,128)(2,1)} %bitcast.163, bf16[2,1152,256]{2,1,0:T(8,128)(2,1)} %collective-permute-done.36.refs_1_.refs_22_.refs_7_, ...), custom_call_target="tpu_custom_call", output_to_operand_aliasing={{2}: (24, {})} | custom-call | tf_op jit(solution)/shard_map/slot/pallas_call | solution.py:364
  515.4 9.3 %collective-permute-start.40 = (bf16[2,1152,256]{2,1,0:T(8,128)(2,1)}, bf16[2,1152,256]{2,1,0:T(8,128)(2,1)S(1)}, u32[]{:S(2)}, u32[]{:S(2)}) collective-permute-start(bf16[2,1152,256]{2,1,0:T(8,128)(2,1)} %get-tuple-element.104.refs_21_), channel_id=1, source_target_pairs={{0,8},{24,16},{8,0},{16,24},{1,9},{25,17},{9,1},{17,25},{2,10},{26... | collective-permute-start | bytes 3538952 | tf_op jit(solution)/shard_map/ppermute | solution.py:398
  532.9 9.4 %slot.42 = (bf16[2,1152,256]{2,1,0:T(8,128)(2,1)}, bf16[2,1152,256]{2,1,0:T(8,128)(2,1)}, bf16[2,3456,1280]{2,1,0:T(8,128)(2,1)}) custom-call(s32[2]{0:T(128)} %pad_add_fusion.flag, bf16[6912,1280]{1,0:T(8,128)(2,1)} %bitcast.167, bf16[2,1152,256]{2,1,0:T(8,128)(2,1)} %copy-done.18, ...), custom_call_target="tpu_custom_call", output_to_operand_aliasing={{2}: (24, {})} | custom-call | tf_op jit(solution)/shard_map/slot/pallas_call | solution.py:364
  542.3 9.0 %collective-permute-start.46 = (bf16[2,1152,256]{2,1,0:T(8,128)(2,1)}, bf16[2,1152,256]{2,1,0:T(8,128)(2,1)S(1)}, u32[]{:S(2)}, u32[]{:S(2)}) collective-permute-start(bf16[2,1152,256]{2,1,0:T(8,128)(2,1)} %get-tuple-element.112.refs_19_), channel_id=1, source_target_pairs={{0,8},{24,16},{8,0},{16,24},{1,9},{25,17},{9,1},{17,25},{2,10},{26... | collective-permute-start | bytes 3538952 | tf_op jit(solution)/shard_map/ppermute | solution.py:398
  557.8 7.7 %slot.43 = (bf16[2,768,256]{2,1,0:T(8,128)(2,1)}, bf16[2,1152,256]{2,1,0:T(8,128)(2,1)}, bf16[2,3456,1280]{2,1,0:T(8,128)(2,1)}) custom-call(s32[2]{0:T(128)} %pad_add_fusion.flag, bf16[6912,1280]{1,0:T(8,128)(2,1)} %bitcast.171, bf16[2,1152,256]{2,1,0:T(8,128)(2,1)} %copy-done.19, ...), custom_call_target="tpu_custom_call", output_to_operand_aliasing={{2}: (24, {})} | custom-call | tf_op jit(solution)/shard_map/slot/pallas_call | solution.py:364
  565.5 8.5 %collective-permute-start.44 = (bf16[2,1152,256]{2,1,0:T(8,128)(2,1)}, bf16[2,1152,256]{2,1,0:T(8,128)(2,1)S(1)}, u32[]{:S(2)}, u32[]{:S(2)}) collective-permute-start(bf16[2,1152,256]{2,1,0:T(8,128)(2,1)} %get-tuple-element.110.refs_19_), channel_id=1, source_target_pairs={{0,8},{24,16},{8,0},{16,24},{1,9},{25,17},{9,1},{17,25},{2,10},{26... | collective-permute-start | bytes 3538952 | tf_op jit(solution)/shard_map/ppermute | solution.py:398
  590.9 9.1 %collective-permute-start.51 = (bf16[2,1152,256]{2,1,0:T(8,128)(2,1)}, bf16[2,1152,256]{2,1,0:T(8,128)(2,1)S(1)}, u32[]{:S(2)}, u32[]{:S(2)}) collective-permute-start(bf16[2,1152,256]{2,1,0:T(8,128)(2,1)} %get-tuple-element.118.refs_13_), channel_id=1, source_target_pairs={{0,8},{24,16},{8,0},{16,24},{1,9},{25,17},{9,1},{17,25},{2,10},{26... | collective-permute-start | bytes 3538952 | tf_op jit(solution)/shard_map/ppermute | solution.py:398
  619.2 13.0 %group_product.10.refs_16_ = bf16[2,512,256]{2,1,0:T(8,128)(2,1)} custom-call(bf16[512,6912]{1,0:T(8,128)(2,1)} %bitcast.220, bf16[6912,1280]{1,0:T(8,128)(2,1)} %bitcast.183, bf16[6912,1280]{1,0:T(8,128)(2,1)} %bitcast.184), custom_call_target="tpu_custom_call" | custom-call | tf_op jit(solution)/shard_map/group_product/pallas_call | solution.py:53
  683.4 7.5 %group_product.11 = bf16[1,512,256]{2,1,0:T(8,128)(2,1)} custom-call(bf16[512,6912]{1,0:T(8,128)(2,1)} %bitcast.221, bf16[6912,1280]{1,0:T(8,128)(2,1)} %bitcast.185), custom_call_target="tpu_custom_call" | custom-call | tf_op jit(solution)/shard_map/group_product/pallas_call | solution.py:53
  (323 shorter events, 297.3 us)
Async XLA Ops:
  7.2 56.0 %all-gather.15.cloned.1.call-start = ((), (), s32[]{:S(2)}) async-start(), calls=%async_computation | async-start | bytes 8847360 | tf_op jit(solution)/shard_map/all_gather | solution.py:416
  7.9 135.9 %all-gather.19.cloned.1.call-start = ((), (), s32[]{:S(2)}) async-start(), calls=%async_computation.2 | async-start | bytes 2949120 | tf_op jit(solution)/shard_map/all_gather | solution.py:523
  8.0 43.1 %collective-permute-start = (bf16[128,6912]{1,0:T(8,128)(2,1)}, bf16[128,6912]{1,0:T(8,128)(2,1)S(1)}, u32[]{:S(2)}, u32[]{:S(2)}) collective-permute-start(bf16[128,6912]{1,0:T(8,128)(2,1)} %bitcast.270), channel_id=1, source_target_pairs={{0,8},{24,16},{1,9},{25,17},{2,10},{26,18},{3,11},{27,19},{4,12},{... | collective-permute-start | bytes 5308424 | tf_op jit(solution)/shard_map/ppermute | solution.py:396
  15.3 39.1 %collective-permute-start.1 = (bf16[128,3456]{1,0:T(8,128)(2,1)}, bf16[128,3456]{1,0:T(8,128)(2,1)S(1)}, u32[]{:S(2)}, u32[]{:S(2)}) collective-permute-start(bf16[128,3456]{1,0:T(8,128)(2,1)} %dynamic-slice_bitcast_fusion), channel_id=1, source_target_pairs={{8,16},{16,8},{9,17},{17,9},{10,18},{18,10},{11,19},{19,11},{12,20... | collective-permute-start | bytes 2654216 | tf_op jit(solution)/shard_map/ppermute | solution.py:397
  74.7 80.4 %all-gather.17.cloned.1.call-start = ((), (), s32[]{:S(2)}) async-start(), calls=%async_computation.1 | async-start | bytes 2949120 | tf_op jit(solution)/shard_map/all_gather | solution.py:523
  75.5 135.3 %all-gather.25.cloned.1.call-start = ((), (), s32[]{:S(2)}) async-start(), calls=%async_computation.5 | async-start | bytes 2949120 | tf_op jit(solution)/shard_map/all_gather | solution.py:523
  79.6 131.2 %all-gather.23.cloned.1.call-start = ((), (), s32[]{:S(2)}) async-start(), calls=%async_computation.4 | async-start | bytes 2949120 | tf_op jit(solution)/shard_map/all_gather | solution.py:523
  80.2 142.5 %all-gather.21.cloned.1.call-start = ((), (), s32[]{:S(2)}) async-start(), calls=%async_computation.3 | async-start | bytes 2949120 | tf_op jit(solution)/shard_map/all_gather | solution.py:523
  80.7 159.0 %all-gather.27.cloned.1.call-start = ((), (), s32[]{:S(2)}) async-start(), calls=%async_computation.6 | async-start | bytes 2949120 | tf_op jit(solution)/shard_map/all_gather | solution.py:523
  100.2 43.5 %collective-permute-start.8 = (bf16[2,1152,256]{2,1,0:T(8,128)(2,1)}, bf16[2,1152,256]{2,1,0:T(8,128)(2,1)}, u32[]{:S(2)}, u32[]{:S(2)}) collective-permute-start(bf16[2,1152,256]{2,1,0:T(8,128)(2,1)} %slot.26.rest_1_), channel_id=1, source_target_pairs={{0,8},{24,16},{8,0},{16,24},{1,9},{25,17},{9,1},{17,25},{2,10},{26... | collective-permute-start | bytes 3538952 | tf_op jit(solution)/shard_map/ppermute | solution.py:398
  161.6 47.5 %collective-permute-start.10 = (bf16[2,1280,256]{2,1,0:T(8,128)(2,1)}, bf16[2,1280,256]{2,1,0:T(8,128)(2,1)S(1)}, u32[]{:S(2)}, u32[]{:S(2)}) collective-permute-start(bf16[2,1280,256]{2,1,0:T(8,128)(2,1)} %get-tuple-element.70), channel_id=1, source_target_pairs={{0,8},{24,16},{8,0},{16,24},{1,9},{25,17},{9,1},{17,25},{2,10},{26... | collective-permute-start | bytes 3932168 | tf_op jit(solution)/shard_map/ppermute | solution.py:398
  163.0 47.8 %collective-permute-start.15 = (bf16[2,1280,256]{2,1,0:T(8,128)(2,1)}, bf16[2,1280,256]{2,1,0:T(8,128)(2,1)}, u32[]{:S(2)}, u32[]{:S(2)}) collective-permute-start(bf16[2,1280,256]{2,1,0:T(8,128)(2,1)} %get-tuple-element.69.refs_10_), channel_id=1, source_target_pairs={{8,16},{16,8},{9,17},{17,9},{10,18},{18,10},{11,19},{19,11},{12,20... | collective-permute-start | bytes 3932168 | tf_op jit(solution)/shard_map/ppermute | solution.py:397
  164.7 57.9 %collective-permute-start.13 = (bf16[2,1280,256]{2,1,0:T(8,128)(2,1)}, bf16[2,1280,256]{2,1,0:T(8,128)(2,1)}, u32[]{:S(2)}, u32[]{:S(2)}) collective-permute-start(bf16[2,1280,256]{2,1,0:T(8,128)(2,1)} %get-tuple-element.72.refs_20_), channel_id=1, source_target_pairs={{8,16},{16,8},{9,17},{17,9},{10,18},{18,10},{11,19},{19,11},{12,20... | collective-permute-start | bytes 3932168 | tf_op jit(solution)/shard_map/ppermute | solution.py:397
  166.4 44.3 %collective-permute-start.14 = (bf16[2,1,256,256]{3,2,0,1:T(8,128)(2,1)S(1)}, bf16[2,1,256,256]{3,2,0,1:T(8,128)(2,1)S(1)}, u32[]{:S(2)}, u32[]{:S(2)}) collective-permute-start(bf16[2,1,256,256]{3,2,0,1:T(8,128)(2,1)S(1)} %copy-done.46), channel_id=1, source_target_pairs={{0,4},{4,0},{1,5},{5,1},{2,6},{6,2},{3,7},{7,3},{8,12},{12,8},{9,1... | collective-permute-start | bytes 786440 | tf_op jit(solution)/shard_map/ppermute | solution.py:399
  220.7 45.0 %collective-permute-start.18 = (bf16[2,1280,256]{2,1,0:T(8,128)(2,1)}, bf16[2,1280,256]{2,1,0:T(8,128)(2,1)}, u32[]{:S(2)}, u32[]{:S(2)}) collective-permute-start(bf16[2,1280,256]{2,1,0:T(8,128)(2,1)} %get-tuple-element.75.refs_20_.refs_17_), channel_id=1, source_target_pairs={{8,16},{16,8},{9,17},{17,9},{10,18},{18,10},{11,19},{19,11},{12,20... | collective-permute-start | bytes 3932168 | tf_op jit(solution)/shard_map/ppermute | solution.py:397
  232.6 66.7 %collective-permute-start.17 = (bf16[2,1280,256]{2,1,0:T(8,128)(2,1)}, bf16[2,1280,256]{2,1,0:T(8,128)(2,1)S(1)}, u32[]{:S(2)}, u32[]{:S(2)}) collective-permute-start(bf16[2,1280,256]{2,1,0:T(8,128)(2,1)} %get-tuple-element.77.refs_21_.refs_18_), channel_id=1, source_target_pairs={{8,16},{16,8},{9,17},{17,9},{10,18},{18,10},{11,19},{19,11},{12,20... | collective-permute-start | bytes 3932168 | tf_op jit(solution)/shard_map/ppermute | solution.py:397
  238.5 70.2 %collective-permute-start.16 = (bf16[2,1152,256]{2,1,0:T(8,128)(2,1)}, bf16[2,1152,256]{2,1,0:T(8,128)(2,1)}, u32[]{:S(2)}, u32[]{:S(2)}) collective-permute-start(bf16[2,1152,256]{2,1,0:T(8,128)(2,1)} %get-tuple-element.76), channel_id=1, source_target_pairs={{0,8},{24,16},{8,0},{16,24},{1,9},{25,17},{9,1},{17,25},{2,10},{26... | collective-permute-start | bytes 3538952 | tf_op jit(solution)/shard_map/ppermute | solution.py:398
  331.9 47.7 %collective-permute-start.27 = (bf16[2,1280,256]{2,1,0:T(8,128)(2,1)}, bf16[2,1280,256]{2,1,0:T(8,128)(2,1)S(1)}, u32[]{:S(2)}, u32[]{:S(2)}) collective-permute-start(bf16[2,1280,256]{2,1,0:T(8,128)(2,1)} %get-tuple-element.87.refs_22_), channel_id=1, source_target_pairs={{0,8},{24,16},{8,0},{16,24},{1,9},{25,17},{9,1},{17,25},{2,10},{26... | collective-permute-start | bytes 3932168 | tf_op jit(solution)/shard_map/ppermute | solution.py:398
  334.2 46.1 %collective-permute-start.30 = (bf16[2,1280,256]{2,1,0:T(8,128)(2,1)}, bf16[2,1280,256]{2,1,0:T(8,128)(2,1)}, u32[]{:S(2)}, u32[]{:S(2)}) collective-permute-start(bf16[2,1280,256]{2,1,0:T(8,128)(2,1)} %get-tuple-element.85.refs_25_.refs_18_), channel_id=1, source_target_pairs={{8,16},{16,8},{9,17},{17,9},{10,18},{18,10},{11,19},{19,11},{12,20... | collective-permute-start | bytes 3932168 | tf_op jit(solution)/shard_map/ppermute | solution.py:397
  362.8 42.1 %collective-permute-start.29 = (bf16[2,1280,256]{2,1,0:T(8,128)(2,1)}, bf16[2,1280,256]{2,1,0:T(8,128)(2,1)}, u32[]{:S(2)}, u32[]{:S(2)}) collective-permute-start(bf16[2,1280,256]{2,1,0:T(8,128)(2,1)} %get-tuple-element.88.refs_25_.refs_17_), channel_id=1, source_target_pairs={{8,16},{16,8},{9,17},{17,9},{10,18},{18,10},{11,19},{19,11},{12,20... | collective-permute-start | bytes 3932168 | tf_op jit(solution)/shard_map/ppermute | solution.py:397
  364.6 40.3 %collective-permute-start.26 = (bf16[2,1152,256]{2,1,0:T(8,128)(2,1)}, bf16[2,1152,256]{2,1,0:T(8,128)(2,1)S(1)}, u32[]{:S(2)}, u32[]{:S(2)}) collective-permute-start(bf16[2,1152,256]{2,1,0:T(8,128)(2,1)} %get-tuple-element.86.refs_21_), channel_id=1, source_target_pairs={{0,8},{24,16},{8,0},{16,24},{1,9},{25,17},{9,1},{17,25},{2,10},{26... | collective-permute-start | bytes 3538952 | tf_op jit(solution)/shard_map/ppermute | solution.py:398
  391.1 35.3 %collective-permute-start.33 = (bf16[2,1280,256]{2,1,0:T(8,128)(2,1)}, bf16[2,1280,256]{2,1,0:T(8,128)(2,1)}, u32[]{:S(2)}, u32[]{:S(2)}) collective-permute-start(bf16[2,1280,256]{2,1,0:T(8,128)(2,1)} %get-tuple-element.91.refs_24_.refs_17_), channel_id=1, source_target_pairs={{8,16},{16,8},{9,17},{17,9},{10,18},{18,10},{11,19},{19,11},{12,20... | collective-permute-start | bytes 3932168 | tf_op jit(solution)/shard_map/ppermute | solution.py:397
  394.3 35.9 %collective-permute-start.35 = (bf16[2,1152,256]{2,1,0:T(8,128)(2,1)}, bf16[2,1152,256]{2,1,0:T(8,128)(2,1)S(1)}, u32[]{:S(2)}, u32[]{:S(2)}) collective-permute-start(bf16[2,1152,256]{2,1,0:T(8,128)(2,1)} %get-tuple-element.94.refs_21_), channel_id=1, source_target_pairs={{0,8},{24,16},{8,0},{16,24},{1,9},{25,17},{9,1},{17,25},{2,10},{26... | collective-permute-start | bytes 3538952 | tf_op jit(solution)/shard_map/ppermute | solution.py:398
  415.7 41.0 %collective-permute-start.31 = (bf16[2,1152,256]{2,1,0:T(8,128)(2,1)}, bf16[2,1152,256]{2,1,0:T(8,128)(2,1)S(1)}, u32[]{:S(2)}, u32[]{:S(2)}) collective-permute-start(bf16[2,1152,256]{2,1,0:T(8,128)(2,1)} %get-tuple-element.92.refs_21_), channel_id=1, source_target_pairs={{0,8},{24,16},{8,0},{16,24},{1,9},{25,17},{9,1},{17,25},{2,10},{26... | collective-permute-start | bytes 3538952 | tf_op jit(solution)/shard_map/ppermute | solution.py:398
  421.7 35.1 %collective-permute-start.32 = (bf16[2,1152,256]{2,1,0:T(8,128)(2,1)}, bf16[2,1152,256]{2,1,0:T(8,128)(2,1)}, u32[]{:S(2)}, u32[]{:S(2)}) collective-permute-start(bf16[2,1152,256]{2,1,0:T(8,128)(2,1)} %get-tuple-element.93.refs_24_.refs_17_), channel_id=1, source_target_pairs={{8,16},{16,8},{9,17},{17,9},{10,18},{18,10},{11,19},{19,11},{12,20... | collective-permute-start | bytes 3538952 | tf_op jit(solution)/shard_map/ppermute | solution.py:397
  441.1 48.5 %collective-permute-start.38 = (bf16[2,1152,256]{2,1,0:T(8,128)(2,1)}, bf16[2,1152,256]{2,1,0:T(8,128)(2,1)S(1)}, u32[]{:S(2)}, u32[]{:S(2)}) collective-permute-start(bf16[2,1152,256]{2,1,0:T(8,128)(2,1)} %get-tuple-element.100.refs_21_), channel_id=1, source_target_pairs={{0,8},{24,16},{8,0},{16,24},{1,9},{25,17},{9,1},{17,25},{2,10},{26... | collective-permute-start | bytes 3538952 | tf_op jit(solution)/shard_map/ppermute | solution.py:398
  453.9 35.7 %collective-permute-start.39 = (bf16[2,1152,256]{2,1,0:T(8,128)(2,1)}, bf16[2,1152,256]{2,1,0:T(8,128)(2,1)}, u32[]{:S(2)}, u32[]{:S(2)}) collective-permute-start(bf16[2,1152,256]{2,1,0:T(8,128)(2,1)} %get-tuple-element.97.refs_24_.refs_17_), channel_id=1, source_target_pairs={{8,16},{16,8},{9,17},{17,9},{10,18},{18,10},{11,19},{19,11},{12,20... | collective-permute-start | bytes 3538952 | tf_op jit(solution)/shard_map/ppermute | solution.py:397
  467.9 38.5 %collective-permute-start.36 = (bf16[2,1152,256]{2,1,0:T(8,128)(2,1)}, bf16[2,1152,256]{2,1,0:T(8,128)(2,1)}, u32[]{:S(2)}, u32[]{:S(2)}) collective-permute-start(bf16[2,1152,256]{2,1,0:T(8,128)(2,1)} %get-tuple-element.98.refs_21_), channel_id=1, source_target_pairs={{0,8},{24,16},{8,0},{16,24},{1,9},{25,17},{9,1},{17,25},{2,10},{26... | collective-permute-start | bytes 3538952 | tf_op jit(solution)/shard_map/ppermute | solution.py:398
  515.4 41.4 %collective-permute-start.40 = (bf16[2,1152,256]{2,1,0:T(8,128)(2,1)}, bf16[2,1152,256]{2,1,0:T(8,128)(2,1)S(1)}, u32[]{:S(2)}, u32[]{:S(2)}) collective-permute-start(bf16[2,1152,256]{2,1,0:T(8,128)(2,1)} %get-tuple-element.104.refs_21_), channel_id=1, source_target_pairs={{0,8},{24,16},{8,0},{16,24},{1,9},{25,17},{9,1},{17,25},{2,10},{26... | collective-permute-start | bytes 3538952 | tf_op jit(solution)/shard_map/ppermute | solution.py:398
  542.3 39.8 %collective-permute-start.46 = (bf16[2,1152,256]{2,1,0:T(8,128)(2,1)}, bf16[2,1152,256]{2,1,0:T(8,128)(2,1)S(1)}, u32[]{:S(2)}, u32[]{:S(2)}) collective-permute-start(bf16[2,1152,256]{2,1,0:T(8,128)(2,1)} %get-tuple-element.112.refs_19_), channel_id=1, source_target_pairs={{0,8},{24,16},{8,0},{16,24},{1,9},{25,17},{9,1},{17,25},{2,10},{26... | collective-permute-start | bytes 3538952 | tf_op jit(solution)/shard_map/ppermute | solution.py:398
  565.5 41.9 %collective-permute-start.44 = (bf16[2,1152,256]{2,1,0:T(8,128)(2,1)}, bf16[2,1152,256]{2,1,0:T(8,128)(2,1)S(1)}, u32[]{:S(2)}, u32[]{:S(2)}) collective-permute-start(bf16[2,1152,256]{2,1,0:T(8,128)(2,1)} %get-tuple-element.110.refs_19_), channel_id=1, source_target_pairs={{0,8},{24,16},{8,0},{16,24},{1,9},{25,17},{9,1},{17,25},{2,10},{26... | collective-permute-start | bytes 3538952 | tf_op jit(solution)/shard_map/ppermute | solution.py:398
  590.9 41.7 %collective-permute-start.51 = (bf16[2,1152,256]{2,1,0:T(8,128)(2,1)}, bf16[2,1152,256]{2,1,0:T(8,128)(2,1)S(1)}, u32[]{:S(2)}, u32[]{:S(2)}) collective-permute-start(bf16[2,1152,256]{2,1,0:T(8,128)(2,1)} %get-tuple-element.118.refs_13_), channel_id=1, source_target_pairs={{0,8},{24,16},{8,0},{16,24},{1,9},{25,17},{9,1},{17,25},{2,10},{26... | collective-permute-start | bytes 3538952 | tf_op jit(solution)/shard_map/ppermute | solution.py:398
  (92 other events, 996.2 us)
Sparse Core Ops, SparseCore 0:
  9.6 53.5 all-gather.14
  74.8 36.9 all-gather.18
  113.4 24.0 all-gather.16
  138.9 24.0 all-gather.24
  164.4 24.0 all-gather.22
  189.9 24.0 all-gather.20
  215.6 24.0 all-gather.26

commit v2 on v1

--- a/solution.py
+++ b/solution.py
@@ -13,7 +13,7 @@
 WIDTH = 256
 UNIT_ROWS = 384
 MOST = 3
-LEAST = 1
+AHEAD = 3
 LAG = 2
 VMEM_LIMIT = 60 * 1024 * 1024
 COST = pl.CostEstimate(flops=0, bytes_accessed=0, transcendentals=0)
@@ -25,6 +25,23 @@
         if total % size == 0:
             best = size
     return best
+
+
+def tie(arrays, deps):
+    count = len(arrays)
+
+    def body(*refs):
+        pass
+
+    return pl.pallas_call(
+        body,
+        out_shape=[jax.ShapeDtypeStruct(x.shape, x.dtype) for x in arrays],
+        in_specs=[ANY] * (count + len(deps)),
+        out_specs=[ANY] * count,
+        input_output_aliases={i: i for i in range(count)},
+        cost_estimate=COST,
+        name="tie",
+    )(*arrays, *deps)
 
 
 def group_product(lhs, mat, group, groups, deps=()):
@@ -97,66 +114,73 @@
         self.groups = cols // WIDTH
         self.unit = largest_divisor(self.half, UNIT_ROWS, 16)
         self.units = self.half // self.unit
-        self.part_units = largest_divisor(self.units, MOST, 1)
-        self.parts = self.units // self.part_units
+        lead = largest_divisor(self.units, MOST, 1)
+        self.bounds = [(0, self.units)]
         self.pieces = []
         for group in range(self.groups):
             first = 0
             while first < self.units:
                 left = self.units - first
-                units = min(self.part_units, left)
-                if group == self.groups - 1:
-                    units = max(min(units, LEAST), min(units, left // 3))
-                units = min(units, self.part_units - first % self.part_units)
+                units = min(lead, left)
                 self.pieces.append(Piece(group, first, units, len([p for p in self.pieces if p.group == group])))
                 first += units
 
     def part_of(self, piece):
-        return piece.first // self.part_units, piece.first % self.part_units
+        q = [a <= piece.first < b for a, b in self.bounds].index(True)
+        return q, piece.first - self.bounds[q][0]
 
 
 def cut(plan, tasks, deps):
-    parts, tokens = plan.parts, tasks[0].shape[0]
-    part = plan.half // parts
-    unit = largest_divisor(part, 384, 128)
+    unit, tokens = plan.unit, tasks[0].shape[0]
+    parts = [b - a for a, b in plan.bounds]
     halves = sum(task.shape[1] // plan.half for task in tasks)
-    if unit % 128:
+    steps = MOST
+    if unit % 128 or any(part % steps for part in parts):
         wide = jnp.concatenate(tasks, axis=1).astype(F32)
-        whole = (wide * wide).astype(BF16).T.reshape(halves, parts, part, tokens)
-        return [whole[:, q] for q in range(parts)]
-    ins, in_specs = [], []
+        whole = (wide * wide).astype(BF16).T.reshape(halves, plan.half, tokens)
+        return [whole[:, a * unit : b * unit] for a, b in plan.bounds]
+    ins, in_specs, places = [], [], []
+    count = 0
     for task in tasks:
         for h in range(task.shape[1] // plan.half):
-            for q in range(parts):
-                ins.append(task)
-                first = (h * parts + q) * (part // unit)
-                in_specs.append(pl.BlockSpec((tokens, unit), lambda j, first=first: (0, first + j)))
+            for q, (a, b) in enumerate(plan.bounds):
+                per = (b - a) // steps
+                for i in range(per):
+                    first = h * plan.units + a + i
+                    ins.append(task)
+                    in_specs.append(
+                        pl.BlockSpec((tokens, unit), lambda j, first=first, per=per: (0, first + per * j))
+                    )
+                    places.append((q, count, i))
+            count += 1
 
     def body(*refs):
-        for h in range(halves):
-            for q in range(parts):
-                wide = refs[h * parts + q][...].astype(F32)
-                refs[len(refs) - parts + q][h] = (wide * wide).T.astype(BF16)
+        outs = refs[len(refs) - len(parts) :]
+        for ref, (q, h, i) in zip(refs, places):
+            wide = ref[...].astype(F32)
+            outs[q][h, i * unit : (i + 1) * unit] = (wide * wide).T.astype(BF16)
 
     return pl.pallas_call(
         body,
-        grid=(part // unit,),
-        out_shape=[jax.ShapeDtypeStruct((halves, part, tokens), BF16)] * parts,
+        grid=(steps,),
+        out_shape=[jax.ShapeDtypeStruct((halves, part * unit, tokens), BF16) for part in parts],
         in_specs=in_specs + [ANY] * len(deps),
-        out_specs=[pl.BlockSpec((halves, unit, tokens), lambda j: (0, j, 0))] * parts,
+        out_specs=[
+            pl.BlockSpec((halves, part // steps * unit, tokens), lambda j: (0, j, 0)) for part in parts
+        ],
         compiler_params=pltpu.CompilerParams(vmem_limit_bytes=VMEM_LIMIT),
         cost_estimate=COST,
         name="cut",
     )(*ins, *deps)
 
 
-def slot_call(plan, flags, last, fold=None, merge=None, gather=None, send=None, final=None, carry=None, cross=None, deps=()):
+def slot_call(plan, flags, last, fold=None, merge=None, gather=None, send=None, final=None, ahead=None, carry=None, cross=None, deps=()):
     unit = plan.unit
     ins, in_specs, outs, out_specs, aliases, kinds = [], [], [], [], {}, []
     most = lambda *some: max([part[0].units for part in some if part is not None] + [0])
     extra = lambda array: 0 if array is None else -(-array.shape[1] // unit)
     steps = max(
-        most(final), most(gather, send) + extra(carry), most(fold, merge) + extra(cross)
+        most(final), most(merge, gather, send) + extra(carry), most(fold, merge) + extra(cross), 0 if ahead is None else AHEAD
     )
 
     def take(array, spec):
@@ -164,8 +188,8 @@
         in_specs.append(spec)
         return len(ins) - 1
 
-    def give(kind, shape, spec):
-        outs.append(jax.ShapeDtypeStruct(shape, BF16))
+    def give(kind, shape, spec, dtype=BF16):
+        outs.append(jax.ShapeDtypeStruct(shape, dtype))
         out_specs.append(spec)
         kinds.append(kind)
         return len(outs) - 1
@@ -185,13 +209,9 @@
     def half_spec(piece, kind):
         return pl.BlockSpec((None, unit, WIDTH), lambda j, flag: (half_of(kind, flag), at(piece, j), 0))
 
-    def both_spec(piece):
-        return pl.BlockSpec((2, unit, WIDTH), lambda j, flag: (0, at(piece, j), 0))
-
     def take_gsq(gsq, h):
-        array, g = gsq
-        shape = (array.shape[0], None, None) + array.shape[3:]
-        return take(array, pl.BlockSpec(shape, lambda j, flag: (0, h, g, 0, 0)))
+        shape = (gsq.shape[0], None) + gsq.shape[2:]
+        return take(gsq, pl.BlockSpec(shape, lambda j, flag: (0, h, 0, 0)))
 
     def give_long(kind, count, units, tail):
         total = units + extra(tail)
@@ -238,7 +258,7 @@
                 ),
                 take_gsq(gsq, h),
             )
-            for h in range(gsq[0].shape[1])
+            for h in range(gsq.shape[1])
         ]
 
     if fold is not None:
@@ -253,24 +273,30 @@
         merge_side = take_side(piece, "kept", side)
         merge_mean = take(mean, half_spec(piece, 0))
         merge_other = take_other(piece, other)
-    across = [part for part in (fold, merge) if part is not None]
-    if across:
-        sections = 1 if fold is None else 2
-        across_out, across_tail = give_long("across", sections, most(fold, merge), cross)
-    if gather is not None or send is not None:
+    apart = fold is not None and merge is not None and fold[0].units != merge[0].units
+    if fold is not None or merge is not None:
+        sections = 1 if fold is None or apart else 2
+        across_out, across_tail = give_long("across", sections, most(merge if fold is None else fold), cross)
+        back_out, back_place = across_out, sections - 1
+        if apart:
+            back_out, back_place = give_long("back", 1, most(merge), None)[0], 0
+    outgoing = [part for part in (merge, gather) if part is not None]
+    if outgoing or send is not None:
         if gather is not None:
-            piece, kept, came, slot = gather
-            gather_kept, gather_came = take(kept, half_spec(piece, slot)), take(came, half_spec(piece, slot))
+            piece, came, section = gather
+            gather_came = take(came, half_spec(piece, section))
         if send is not None:
             piece, inward, own = send
             if own:
                 send_in = [take(inward, rows_spec(piece, h, WIDTH, piece.group)) for h in (0, 1)]
             else:
                 send_in = [take(inward, half_spec(piece, h)) for h in (0, 1)]
-        pass_out, pass_tail = give_long("pass", 2, most(gather, send), carry)
+        pass_count = 2 if send is not None or merge is not None else 1
+        pass_out, pass_tail = give_long("pass", pass_count, most(merge, gather, send), carry)
     if final is not None:
-        piece, own, came, buffer = final
-        final_own, final_in = take(own, both_spec(piece)), take(came, both_spec(piece))
+        piece, kept, crossed, buffer, acts, total = final
+        final_kept = [take(x, half_spec(piece, kept[2])) for x in kept[:2]]
+        final_crossed = [take(x, half_spec(piece, crossed[2])) for x in crossed[:2]]
         first, group = piece.first, piece.group
         final_piece = piece
         final_out = give(
@@ -280,6 +306,29 @@
         )
         if buffer is not None:
             aliases[1 + take(buffer, ANY)] = final_out
+        if acts is not None:
+            result_acts = [
+                take(
+                    acts,
+                    pl.BlockSpec(
+                        (acts.shape[0], unit),
+                        lambda j, flag, h=h: (0, h * plan.units + first + at(final_piece, j)),
+                    ),
+                )
+                for h in (0, 1)
+            ]
+            whole = pl.BlockSpec((acts.shape[0], WIDTH), lambda j, flag: (0, 0))
+            result_in = None if total is None else take(total, whole)
+            result_out = give("result", (acts.shape[0], WIDTH), whole, F32)
+    if ahead is not None:
+        ahead_acts, ahead_weight, ahead_group, ahead_turn, ahead_total = ahead
+        tokens, depth = ahead_acts.shape[0], plan.rows // AHEAD**2
+        block_at = lambda j: ahead_turn * AHEAD + jnp.minimum(j, AHEAD - 1)
+        ahead_lhs = take(ahead_acts, pl.BlockSpec((tokens, depth), lambda j, flag: (0, block_at(j))))
+        ahead_mat = take(ahead_weight, pl.BlockSpec((depth, WIDTH), lambda j, flag: (block_at(j), ahead_group)))
+        everything = pl.BlockSpec((tokens, WIDTH), lambda j, flag: (0, 0))
+        ahead_in = None if ahead_total is None else take(ahead_total, everything)
+        ahead_out = give("ahead", (tokens, WIDTH), everything, F32)
     for dep in deps:
         take(dep, ANY)
 
@@ -327,18 +376,48 @@
 
             @during(gather, flag[1] == last)
             def _():
-                outr[pass_out][flag[0]] = inr[gather_came][...]
-                outr[pass_out][1 - flag[0]] = inr[gather_kept][...]
+                outr[pass_out][pass_count - 1] = inr[gather_came][...]
 
         if final is not None:
 
             @during(final, flag[1] == last)
             def _():
-                outr[final_out][...] = inr[final_own][...]
+                outr[final_out][1 - flag[0]] = inr[final_kept[0]][...]
+                outr[final_out][flag[0]] = inr[final_crossed[0]][...]
 
             @during(final, flag[1] != last)
             def _():
-                outr[final_out][...] = inr[final_in][...]
+                outr[final_out][1 - flag[0]] = inr[final_kept[1]][...]
+                outr[final_out][flag[0]] = inr[final_crossed[1]][...]
+
+        def add_to(out, before, value):
+            @pl.when(j == 0)
+            def _():
+                outr[out][...] = value if before is None else inr[before][...] + value
+
+            @pl.when(j > 0)
+            def _():
+                outr[out][...] += value
+
+        if final is not None and final[4] is not None:
+
+            @during(final)
+            def _():
+                parts = [
+                    jnp.dot(inr[result_acts[h]][...], outr[final_out][h], preferred_element_type=F32)
+                    for h in (0, 1)
+                ]
+                add_to(result_out, result_in, parts[0] + parts[1])
+
+        if ahead is not None:
+
+            @pl.when(j < AHEAD)
+            def _():
+                add_to(
+                    ahead_out,
+                    ahead_in,
+                    jnp.dot(inr[ahead_lhs][...], inr[ahead_mat][...], preferred_element_type=F32),
+                )
 
         if fold is not None:
 
@@ -359,7 +438,12 @@
                     + before * inr[merge_in][...].astype(F32)
                     + there * inr[merge_mean][...].astype(F32)
                 )
-                outr[across_out][sections - 1] = (numer / (here + before + there + 1e-6)).astype(BF16)
+                value = (numer / (here + before + there + 1e-6)).astype(BF16)
+                outr[back_out][back_place] = value
+
+                @pl.when(flag[1] == last)
+                def _():
+                    outr[pass_out][0] = value
 
     result = pl.pallas_call(
         body,
@@ -415,10 +499,11 @@
 
     full_acts = lax.all_gather(acts, "col", axis=0, tiled=True)
 
-    near = [acts]
+    crossing = lambda x: send_mid(lax.dynamic_slice_in_dim(x, sent * plan.half, plan.half, 1))
+    near, cross = [acts], [crossing(acts)]
     for _ in range(last):
-        near.append(send_in(near[-1]))
-    cross = [send_mid(lax.dynamic_slice_in_dim(x, sent * plan.half, plan.half, 1)) for x in near]
+        near += tie([send_in(near[-1])], cross[-1:])
+        cross.append(crossing(near[-1]))
 
     my_labels = lax.dynamic_slice_in_dim(label_row, row * share, share, 0)
     onehot = (my_labels[:, None] == lax.broadcasted_iota(jnp.int32, (share, protos.shape[0]), 1)).astype(BF16)
@@ -443,7 +528,7 @@
     class Gradient:
         def __init__(self, group, groups):
             self.first, self.groups = group, groups
-            self.outer, self.far = [None] * groups, [[None, None] for _ in range(groups)]
+            self.outer, self.own, self.far, self.oth = ([None] * groups for _ in range(4))
 
         def start(self, product):
             self.near = [squared_grad(product, self.first)]
@@ -455,23 +540,23 @@
 
         def inside(self, g, came):
             self.outer[g] = unpacked(came, (last, share, WIDTH))
-            if all(x is not None for x in self.outer):
-                stacked = jnp.concatenate([self.near[0][None], jnp.stack(self.outer, 1)])
-                self.own = gather_rows(stacked)
+            self.own[g] = gather_rows(jnp.concatenate([self.near[0][g][None], self.outer[g]]))
 
         def outside(self, g, part, came):
-            self.far[g][part] = unpacked(came, (last if part else 1, share, WIDTH))
-            if all(x is not None for pair in self.far for x in pair):
-                self.oth = gather_rows(jnp.stack([jnp.concatenate(pair) for pair in self.far], 1))
+            came = unpacked(came, (last if part else 1, share, WIDTH))
+            if part:
+                self.oth[g] = gather_rows(jnp.concatenate([self.far[g], came]))
+            else:
+                self.far[g] = came
 
     count = len(plan.pieces)
     batches = [Gradient(0, 1)]
     while batches[-1].first + batches[-1].groups < plan.groups:
         group = batches[-1].first + batches[-1].groups
-        batches.append(Gradient(group, min(2, plan.groups - group)))
+        batches.append(Gradient(group, 1))
     batch_of = {b.first + g: b for b in batches for g in range(b.groups)}
-    own_of = lambda piece: (batch_of[piece.group].own, piece.group - batch_of[piece.group].first)
-    other_of = lambda piece: (batch_of[piece.group].oth, piece.group - batch_of[piece.group].first)
+    own_of = lambda piece: batch_of[piece.group].own[piece.group - batch_of[piece.group].first]
+    other_of = lambda piece: batch_of[piece.group].oth[piece.group - batch_of[piece.group].first]
 
     def inward(index):
         piece = plan.pieces[index]
@@ -486,8 +571,7 @@
         for task in outer_parts[: last - 1]:
             blocks = task[q][:, :, offset : offset + b - a]
             squared.append(jnp.moveaxis(blocks, 0, 2).reshape(2, b - a, tokens))
-        own, g = own_of(piece)
-        gsq = jnp.moveaxis(own[:, :, g], 0, 1).reshape(side_n, tokens, WIDTH)
+        gsq = jnp.moveaxis(own_of(piece), 0, 1).reshape(side_n, tokens, WIDTH)
         shares = [
             jnp.einsum("hrt,tc->hrc", s, g, preferred_element_type=F32)
             for s, g in zip(squared, gsq)
@@ -507,39 +591,34 @@
             came = jnp.where(depth == d, arrived, came)
         return came
 
-    sent_pass, came_pass = {}, {}
+    sent_pass, came_pass, came_out = {}, {}, {}
 
     def start_pass(slot, got):
         if "pass" in got:
             sent_pass[slot] = got["pass"]
             came_pass[slot] = swap(got["pass"])
+            came_out[slot] = outward(came_pass[slot])
 
     if last == 1:
         start_pass(-2, slot_call(plan, flags, last, send=inward(0), deps=[near[-1], cross[0]]))
     lead = batches[0]
-    product = group_product(full_acts, weight, 0, 1, deps=list(sent_pass.values()) + cross[1:])
-    outer_cuts = [cut(plan, [task], [product]) for task in near[1:]]
-    other_cuts = cut(plan, cross, [product])
+    outer_cuts = [cut(plan, [task], list(sent_pass.values())) for task in near[1:]]
+    product = group_product(full_acts, weight, 0, 1, deps=[x[0] for x in outer_cuts])
     gather_col = lambda x: lax.all_gather(x, "col", axis=0)
-    outer_parts = [[None] * plan.parts for _ in range(last)]
-    other_parts = []
-    for q in range(plan.parts):
-        for h in range(last):
-            outer_parts[h][q] = gather_col(outer_cuts[h][q])
-        other_parts.append(gather_col(other_cuts[q]))
+    outer_parts = [[gather_col(x) for x in task] for task in outer_cuts]
 
     def at_once(b, product):
         b.start(product)
         came = swap(jnp.stack(b.near))
         b.outer = [came[:, g] for g in range(b.groups)]
         stacked = jnp.concatenate([b.near[0][None], came])
-        b.own = gather_rows(stacked)
         crossed = send_mid(stacked)
-        b.oth = gather_rows(crossed)
+        b.own = [gather_rows(stacked[:, g]) for g in range(b.groups)]
+        b.oth = [gather_rows(crossed[:, g]) for g in range(b.groups)]
         return crossed
 
     lead_far = at_once(lead, product)
-    own_square = squares(full_acts, [lead.near[0], outer_cuts[0][0], other_cuts[0]])
+    own_square = squares(full_acts, [lead.near[0]] + list(came_pass.values()))
     carries, crossings, starts = {}, {}, {}
 
     def ship(slot, b):
@@ -549,29 +628,39 @@
             crossings[slot + LAG + g] = (b, g, 1)
 
     if last == 1 and count > 1:
-        start_pass(-1, slot_call(plan, flags, last, send=inward(1), deps=[own_square, lead.outer[0]]))
-    product = own_square
-    for b in batches[1:]:
-        first = min(i for i, p in enumerate(plan.pieces) if p.group == b.first)
-        ready = first - (0 if last == 1 else LAG) - LAG - (b.groups - 1)
-        if ready >= 2:
-            starts[ready - 2] = b
-            continue
-        deps = [product, lead.outer[0]] + list(sent_pass.values())[-1:]
-        product = group_product(full_acts, weight, b.first, b.groups, deps=deps)
-        if ready >= 0:
-            b.start(product)
-            ship(0, b)
-        else:
-            at_once(b, product)
+        start_pass(-1, slot_call(plan, flags, last, send=inward(1), deps=[lead.near[0]] + list(came_pass.values())))
+    other_cuts = cut(plan, cross, [own_square] + list(sent_pass.values())[-1:])
+    other_parts = [gather_col(x) for x in other_cuts]
+    early = min(LAG, plan.groups - 1) if last == 1 else plan.groups - 1
+    deps = [other_cuts[0], lead.outer[0]] + list(sent_pass.values())[-1:]
+    next_products = group_product(full_acts, weight, 1, early, deps=deps)
+    fused = last == 1 and plan.unit % 128 == 0 and plan.rows % (AHEAD**2 * 128) == 0
+    first_of = lambda b: min(i for i, p in enumerate(plan.pieces) if p.group == b.first)
+    rest = list(batches[1:])
+    if fused and all(first_of(b) >= AHEAD * (i + 1) for i, b in enumerate(rest)):
+        for slot, b in enumerate(rest[:LAG]):
+            b.start(next_products[slot : slot + 1])
+            ship(slot, b)
+        turn = 0
+        for b in rest[LAG:]:
+            starts.update({turn + k: (b, k) for k in range(AHEAD)})
+            turn += AHEAD
+            slot = turn
+            while {slot, slot + LAG} & set(crossings):
+                slot += 1
+            ship(slot, b)
+    else:
+        for i, b in enumerate(rest):
+            at_once(b, next_products[i : i + 1])
     if last > 1:
         for index in range(min(LAG, count)):
             start_pass(index - LAG, slot_call(plan, flags, last, send=inward(index)))
 
-    sent_mid, came_mid, places = {}, {}, {}
+    came_mid, backs = {}, {}
     buffer = None
-    results, finished = [], 0
-    chain = [product, lead_far] + list(sent_pass.values())[-1:]
+    results = []
+    chain = [next_products, lead_far] + list(came_pass.values())[-1:]
+    ahead_total, result_total = None, None
     for slot in range(count + 3 * LAG):
         deps = list(chain)
         stage = {}
@@ -594,6 +683,9 @@
             stage["fold"] = (piece, weight, came_pass[slot - LAG], side_of(piece))
         if now(slot + LAG):
             stage["send"] = inward(slot + LAG)
+        if slot < max(carries, default=0):
+            stage.setdefault("cross", packed(lead.near[0][0]))
+            stage.setdefault("carry", lead.inwards(0))
         index = slot - LAG
         if now(index):
             piece = plan.pieces[index]
@@ -607,37 +699,45 @@
             )
         index = slot - 2 * LAG
         if now(index):
-            stage["gather"] = (plan.pieces[index], sent_mid[slot - LAG], came_mid[slot - LAG], places[slot - LAG])
+            stage["gather"] = (plan.pieces[index],) + backs[slot - LAG]
         index = slot - 3 * LAG
         if now(index):
             stage["final"] = (
                 plan.pieces[index],
-                sent_pass[slot - LAG],
-                outward(came_pass[slot - LAG]),
+                (sent_pass[slot - 2 * LAG], came_out[slot - 2 * LAG], 0),
+                (sent_pass[slot - LAG], came_out[slot - LAG], sent_pass[slot - LAG].shape[0] - 1),
                 buffer,
+                full_acts if fused else None,
+                result_total,
             )
+        if slot in starts:
+            b, turn = starts[slot]
+            stage["ahead"] = (full_acts, weight, b.first, turn, ahead_total)
         got = slot_call(plan, flags, last, deps=deps, **stage)
         chain = [got[name] for name in ("across", "pass") if name in got][:1]
         if "across" in got:
-            sent_mid[slot], came_mid[slot] = got["across"], send_mid(got["across"])
-            places[slot] = got["across"].shape[0] - 1
+            came_mid[slot] = send_mid(got["across"])
+            backs[slot] = (came_mid[slot], got["across"].shape[0] - 1)
+            if "back" in got:
+                backs[slot] = (send_mid(got["back"]), 0)
         start_pass(slot, got)
         if "final" in got:
             buffer = got["final"]
             done = plan.pieces[slot - 3 * LAG]
-            stored = done.group + 1 - finished
-            if done.first + done.units == plan.units and (stored == 2 or done.group == plan.groups - 1):
-                whole = buffer.reshape(plan.rows, plan.cols)
-                out = group_product(full_acts, whole, finished, stored)
-                chain = [out]
+            result_total = got.get("result")
+            if done.first + done.units == plan.units:
+                if fused:
+                    out = result_total.astype(BF16)[None]
+                else:
+                    out = group_product(full_acts, buffer.reshape(plan.rows, plan.cols), done.group, 1)
                 results.append(sum_rows(out).astype(BF16))
-                finished = done.group + 1
-        if slot in starts:
-            b = starts[slot]
-            product = group_product(full_acts, weight, b.first, b.groups, deps=chain)
-            chain = [product]
-            b.start(product)
-            ship(slot + 1, b)
+                result_total = None
+        if "ahead" in got:
+            ahead_total = got["ahead"]
+            b, turn = starts[slot]
+            if turn == AHEAD - 1:
+                b.start(ahead_total.astype(BF16)[None])
+                ahead_total = None
     result = jnp.moveaxis(jnp.concatenate(results), 0, 1).reshape(1, share, plan.cols)
     return buffer.reshape(plan.rows, plan.cols), result
 

time: 717 us -> 662 us (0.923)
  waiting for transfers between devices: 201 us -> 170 us
  starting transfers between devices: 166 us -> 148 us
  Pallas kernels: 276 us -> 263 us
  other arithmetic: 4.33 us -> 12.8 us
    pallas_call x6 -> x2, Pallas kernels: 67.5 us -> 20.8 us  [group_product(): pl.pallas_call(body, grid=(steps,), out_shape=jax.ShapeDtypeStruct((group...]
    ppermute x25 -> x22, waiting for transfers between devices: 134 us -> 93.9 us  [local(): lax.ppermute(x, 'task', step_in(last - 1) + step_out(last - 1))]
    pallas_call x26 -> x23, Pallas kernels: 190 us -> 224 us  [slot_call(): pl.pallas_call(body, grid_spec=pltpu.PrefetchScalarGridSpec(num_scalar_pr...]
    ppermute x25 -> x22, starting transfers between devices: 115 us -> 84.5 us  [local(): lax.ppermute(x, 'task', step_in(last - 1) + step_out(last - 1))]
    ppermute x12 -> x20, waiting for transfers between devices: 24.4 us -> 41.1 us  [local(): lax.ppermute(x, 'row', [(i, (i + s) % rows_n) for i in range(rows_n)])]
    ppermute x12 -> x20, starting transfers between devices: 14.2 us -> 28.1 us  [local(): lax.ppermute(x, 'row', [(i, (i + s) % rows_n) for i in range(rows_n)])]
    ppermute x23 -> x20, starting transfers between devices: 30.6 us -> 30 us  [local(): lax.ppermute(x, 'task', [(last, side_n), (side_n, last)])]
    unnamed x113 -> x115, local copies, waits for them, and re-layouts: 22.9 us -> 22.8 us
  transfers between devices with their start and end apart: 68 -> 66, of which waited for: 26 -> 33; matrix products, arithmetic and copies ran while one was open for 3% -> 5% of each run, Pallas kernels for 37% -> 40%
where the time goes in v2:
time: 662 us; the launch traced here: 651 us
  Pallas kernels  263 us (40%)
  waiting for transfers between devices  170 us (26%)
  starting transfers between devices  148 us (22%)
  local copies, waits for them, and re-layouts  41.6 us (6%)
  between operations  15.3 us (2%)
  other arithmetic  12.8 us (2%)
    pallas_call x23, Pallas kernels, slot_call(): pl.pallas_call(body, grid_spec=pltpu.PrefetchScalarGridSpec(num_scalar_pr...  224 us
    ppermute x22, waiting for transfers between devices, local(): lax.ppermute(x, 'task', step_in(last - 1) + step_out(last - 1))  93.9 us
    ppermute x22, starting transfers between devices, local(): lax.ppermute(x, 'task', step_in(last - 1) + step_out(last - 1))  84.5 us
    ppermute x20, waiting for transfers between devices, local(): lax.ppermute(x, 'row', [(i, (i + s) % rows_n) for i in range(rows_n)])  41.1 us
    ppermute x1, waiting for transfers between devices, local(): send_in = lambda x: lax.ppermute(x, 'task', all_in)  34.5 us
    ppermute x20, starting transfers between devices, local(): lax.ppermute(x, 'task', [(last, side_n), (side_n, last)])  30 us
    ppermute x20, starting transfers between devices, local(): lax.ppermute(x, 'row', [(i, (i + s) % rows_n) for i in range(rows_n)])  28.1 us
    unnamed x115, local copies, waits for them, and re-layouts  22.8 us
  transfers between devices with their start and end apart: 66, of which 33 were waited for; matrix products, arithmetic and copies ran while one was open for 5% of the time, Pallas kernels for 40%

profile of v2, /device:TPU:0, one launch (start us, length us, event | category | flops | bytes accessed | tf_op | source)
XLA Modules:
  0.0 651.4 jit_solution(18210766325755443598)
XLA Ops:
  16.5 34.5 %collective-permute-done.refs_0_ = bf16[128,6912]{1,0:T(8,128)(2,1)S(1)} collective-permute-done((bf16[128,6912]{1,0:T(8,128)(2,1)}, bf16[128,6912]{1,0:T(8,128)(2,1)S(1)}, u32[]{:S(2)}, u32[]{:S(2)}) %collective-permute-start) | collective-permute-done | bytes 1769504 | tf_op jit(solution)/shard_map/ppermute | solution.py:480
  64.4 7.6 %group_product.2 = bf16[1,512,256]{2,1,0:T(8,128)(2,1)} custom-call(bf16[512,6912]{1,0:T(8,128)(2,1)} %bitcast.223, bf16[6912,1280]{1,0:T(8,128)(2,1)} %bitcast.156, bf16[2,3456,128]{2,1,0:T(8,128)(2,1)} %cut.2.rest_1_), custom_call_target="tpu_custom_call" | custom-call | tf_op jit(solution)/shard_map/group_product/pallas_call | solution.py:70
  78.7 9.3 %collective-permute-done.2.rest_1_.refs_3_.refs_1_.refs_7_ = bf16[2,1152,256]{2,1,0:T(8,128)(2,1)S(1)} collective-permute-done((bf16[2,1152,256]{2,1,0:T(8,128)(2,1)}, bf16[2,1152,256]{2,1,0:T(8,128)(2,1)S(1)}, u32[]{:S(2)}, u32[]{:S(2)}) %collective-permute-start.2) | collective-permute-done | bytes 1179680 | tf_op jit(solution)/shard_map/ppermute | solution.py:482
  93.0 10.2 %squares.1.refs_6_.refs_2_.refs_8_ = bf16[6912,512]{1,0:T(8,128)(2,1)} custom-call(bf16[512,6912]{1,0:T(8,128)(2,1)} %bitcast.224, bf16[1,256,256]{2,1,0:T(8,128)(2,1)} %fusion.16.rest_0_.refs_2_, bf16[2,1152,256]{2,1,0:T(8,128)(2,1)} %copy-done.22), custom_call_target="tpu_custom_call" | custom-call | tf_op jit(solution)/shard_map/squares/pallas_call | solution.py:93
  116.2 13.2 %group_product.3.refs_12_ = bf16[2,512,256]{2,1,0:T(8,128)(2,1)} custom-call(bf16[512,6912]{1,0:T(8,128)(2,1)} %bitcast.225, bf16[6912,1280]{1,0:T(8,128)(2,1)} %bitcast.159, bf16[6912,1280]{1,0:T(8,128)(2,1)} %bitcast.160, bf16[2,3456,128]{2,1,0:T(8,128)(2,1)} %cut.3.rest_2_, bf16[1,256,256]{2,1,0:T(8,128)(2,1)} %bitcast.349, ...), custom_call_target="tpu_custom_call" | custom-call | tf_op jit(solution)/shard_map/group_product/pallas_call | solution.py:70
  142.1 8.5 %slot.25 = (bf16[2,1280,256]{2,1,0:T(8,128)(2,1)}, bf16[2,1280,256]{2,1,0:T(8,128)(2,1)}, f32[512,256]{1,0:T(8,128)}) custom-call(s32[2]{0:T(128)} %pad_add_fusion.flag, bf16[6912,1280]{1,0:T(8,128)(2,1)} %bitcast.161, bf16[2,1152,256]{2,1,0:T(8,128)(2,1)} %copy-done.22, bf16[6912,512]{1,0:T(8,128)(2,1)} %squares.1.refs_6_.refs_2_.refs_8_, ...), custom_call_target="tpu_custom_call" | custom-call | tf_op jit(solution)/shard_map/slot/pallas_call | solution.py:448
  155.9 8.8 %slot.26 = (bf16[2,1280,256]{2,1,0:T(8,128)(2,1)}, bf16[2,1280,256]{2,1,0:T(8,128)(2,1)}, f32[512,256]{1,0:T(8,128)}) custom-call(s32[2]{0:T(128)} %pad_add_fusion.flag, bf16[6912,1280]{1,0:T(8,128)(2,1)} %bitcast.168, bf16[2,1152,256]{2,1,0:T(8,128)(2,1)} %copy-done.27, bf16[6912,512]{1,0:T(8,128)(2,1)} %squares.1.refs_6_.refs_2_.refs_8_, ...), custom_call_target="tpu_custom_call" | custom-call | tf_op jit(solution)/shard_map/slot/pallas_call | solution.py:448
  171.7 12.4 %collective-permute-done.10.refs_1_.refs_7_ = bf16[2,1280,256]{2,1,0:T(8,128)(2,1)} collective-permute-done((bf16[2,1280,256]{2,1,0:T(8,128)(2,1)}, bf16[2,1280,256]{2,1,0:T(8,128)(2,1)}, u32[]{:S(2)}, u32[]{:S(2)}) %collective-permute-start.10) | collective-permute-done | bytes 1310752 | tf_op jit(solution)/shard_map/ppermute | solution.py:482
  185.8 11.1 %slot.27 = (bf16[2,1280,256]{2,1,0:T(8,128)(2,1)}, bf16[2,1280,256]{2,1,0:T(8,128)(2,1)}, f32[512,256]{1,0:T(8,128)}) custom-call(s32[2]{0:T(128)} %pad_add_fusion.flag, bf16[6912,1280]{1,0:T(8,128)(2,1)} %bitcast.169, bf16[2,1280,256]{2,1,0:T(8,128)(2,1)} %collective-permute-done.10.refs_1_.refs_7_, bf16[6912,512]{1,0:T(8,128)(2,1)} %squares.1.refs_6_.refs_2_.refs_8_, ...), custom_call_target="tpu_custom_call" | custom-call | tf_op jit(solution)/shard_map/slot/pallas_call | solution.py:448
  202.6 9.5 %collective-permute-done.18.refs_1_.refs_7_ = bf16[2,1280,256]{2,1,0:T(8,128)(2,1)S(1)} collective-permute-done((bf16[2,1280,256]{2,1,0:T(8,128)(2,1)}, bf16[2,1280,256]{2,1,0:T(8,128)(2,1)S(1)}, u32[]{:S(2)}, u32[]{:S(2)}) %collective-permute-start.18) | collective-permute-done | bytes 1310752 | tf_op jit(solution)/shard_map/ppermute | solution.py:482
  213.8 10.7 %slot.28 = (bf16[2,1280,256]{2,1,0:T(8,128)(2,1)}, bf16[2,1280,256]{2,1,0:T(8,128)(2,1)}, f32[512,256]{1,0:T(8,128)}) custom-call(s32[2]{0:T(128)} %pad_add_fusion.flag, bf16[6912,1280]{1,0:T(8,128)(2,1)} %bitcast.174, bf16[2,1280,256]{2,1,0:T(8,128)(2,1)} %copy-done.29, bf16[6912,512]{1,0:T(8,128)(2,1)} %squares.1.refs_6_.refs_2_.refs_8_, ...), custom_call_target="tpu_custom_call" | custom-call | tf_op jit(solution)/shard_map/slot/pallas_call | solution.py:448
  241.3 11.2 %slot.29 = (bf16[2,1280,256]{2,1,0:T(8,128)(2,1)}, bf16[2,1280,256]{2,1,0:T(8,128)(2,1)}, f32[512,256]{1,0:T(8,128)}) custom-call(s32[2]{0:T(128)} %pad_add_fusion.flag, bf16[6912,1280]{1,0:T(8,128)(2,1)} %bitcast.179, bf16[2,1280,256]{2,1,0:T(8,128)(2,1)} %copy-done.25, bf16[6912,512]{1,0:T(8,128)(2,1)} %squares.1.refs_6_.refs_2_.refs_8_, ...), custom_call_target="tpu_custom_call" | custom-call | tf_op jit(solution)/shard_map/slot/pallas_call | solution.py:448
  269.4 11.1 %slot.30 = (bf16[2,1280,256]{2,1,0:T(8,128)(2,1)}, bf16[2,1280,256]{2,1,0:T(8,128)(2,1)}, f32[512,256]{1,0:T(8,128)}) custom-call(s32[2]{0:T(128)} %pad_add_fusion.flag, bf16[6912,1280]{1,0:T(8,128)(2,1)} %bitcast.188, bf16[2,1280,256]{2,1,0:T(8,128)(2,1)} %copy-done.24, bf16[6912,512]{1,0:T(8,128)(2,1)} %squares.1.refs_6_.refs_2_.refs_8_, ...), custom_call_target="tpu_custom_call" | custom-call | tf_op jit(solution)/shard_map/slot/pallas_call | solution.py:448
  288.0 8.4 %collective-permute-done.20.refs_1_.refs_25_.refs_7_.refs_21_ = bf16[2,1280,256]{2,1,0:T(8,128)(2,1)S(1)} collective-permute-done((bf16[2,1280,256]{2,1,0:T(8,128)(2,1)}, bf16[2,1280,256]{2,1,0:T(8,128)(2,1)S(1)}, u32[]{:S(2)}, u32[]{:S(2)}) %collective-permute-start.20) | collective-permute-done | bytes 1310752 | tf_op jit(solution)/shard_map/ppermute | solution.py:482
  297.5 12.3 %slot.31 = (bf16[2,1280,256]{2,1,0:T(8,128)(2,1)}, bf16[2,1280,256]{2,1,0:T(8,128)(2,1)}, bf16[2,3456,1280]{2,1,0:T(8,128)(2,1)}, f32[512,256]{1,0:T(8,128)}) custom-call(s32[2]{0:T(128)} %pad_add_fusion.flag, bf16[6912,1280]{1,0:T(8,128)(2,1)} %bitcast.189, bf16[2,1280,256]{2,1,0:T(8,128)(2,1)} %copy-done.15, ...), custom_call_target="tpu_custom_call" | custom-call | tf_op jit(solution)/shard_map/slot/pallas_call | solution.py:448
  325.6 12.5 %slot.32 = (bf16[2,1280,256]{2,1,0:T(8,128)(2,1)}, bf16[2,1280,256]{2,1,0:T(8,128)(2,1)}, bf16[2,3456,1280]{2,1,0:T(8,128)(2,1)}, f32[512,256]{1,0:T(8,128)}) custom-call(s32[2]{0:T(128)} %pad_add_fusion.flag, bf16[6912,1280]{1,0:T(8,128)(2,1)} %bitcast.193, bf16[2,1280,256]{2,1,0:T(8,128)(2,1)} %copy-done.17, ...), custom_call_target="tpu_custom_call", output_to_operand_aliasing={{2}: (27, {})} | custom-call | tf_op jit(solution)/shard_map/slot/pallas_call | solution.py:448
  344.1 8.6 %collective-permute-done.26.refs_1_.refs_23_.refs_7_.refs_21_ = bf16[2,1280,256]{2,1,0:T(8,128)(2,1)} collective-permute-done((bf16[2,1280,256]{2,1,0:T(8,128)(2,1)}, bf16[2,1280,256]{2,1,0:T(8,128)(2,1)}, u32[]{:S(2)}, u32[]{:S(2)}) %collective-permute-start.26) | collective-permute-done | bytes 1310752 | tf_op jit(solution)/shard_map/ppermute | solution.py:482
  352.7 12.3 %slot.33 = (bf16[2,1152,256]{2,1,0:T(8,128)(2,1)}, bf16[2,1152,256]{2,1,0:T(8,128)(2,1)}, bf16[2,3456,1280]{2,1,0:T(8,128)(2,1)}, f32[512,256]{1,0:T(8,128)}) custom-call(s32[2]{0:T(128)} %pad_add_fusion.flag, bf16[6912,1280]{1,0:T(8,128)(2,1)} %bitcast.197, ...), custom_call_target="tpu_custom_call", output_to_operand_aliasing={{2}: (25, {})} | custom-call | tf_op jit(solution)/shard_map/slot/pallas_call | solution.py:448
  381.8 12.3 %slot.34 = (bf16[2,1280,256]{2,1,0:T(8,128)(2,1)}, bf16[2,1152,256]{2,1,0:T(8,128)(2,1)}, bf16[2,3456,1280]{2,1,0:T(8,128)(2,1)}, f32[512,256]{1,0:T(8,128)}) custom-call(s32[2]{0:T(128)} %pad_add_fusion.flag, bf16[6912,1280]{1,0:T(8,128)(2,1)} %bitcast.204, bf16[2,1280,256]{2,1,0:T(8,128)(2,1)} %copy-done.16, ...), custom_call_target="tpu_custom_call", output_to_operand_aliasing={{2}: (26, {})} | custom-call | tf_op jit(solution)/shard_map/slot/pallas_call | solution.py:448
  407.0 12.2 %slot.35 = (bf16[2,1152,256]{2,1,0:T(8,128)(2,1)}, bf16[2,1152,256]{2,1,0:T(8,128)(2,1)}, bf16[2,3456,1280]{2,1,0:T(8,128)(2,1)}, f32[512,256]{1,0:T(8,128)}) custom-call(s32[2]{0:T(128)} %pad_add_fusion.flag, bf16[6912,1280]{1,0:T(8,128)(2,1)} %bitcast.205, bf16[2,1152,256]{2,1,0:T(8,128)(2,1)} %copy-done.19, ...), custom_call_target="tpu_custom_call", output_to_operand_aliasing={{2}: (25, {})} | custom-call | tf_op jit(solution)/shard_map/slot/pallas_call | solution.py:448
  436.4 12.2 %slot.36 = (bf16[2,1152,256]{2,1,0:T(8,128)(2,1)}, bf16[2,1152,256]{2,1,0:T(8,128)(2,1)}, bf16[2,3456,1280]{2,1,0:T(8,128)(2,1)}, f32[512,256]{1,0:T(8,128)}) custom-call(s32[2]{0:T(128)} %pad_add_fusion.flag, bf16[6912,1280]{1,0:T(8,128)(2,1)} %bitcast.209, ...), custom_call_target="tpu_custom_call", output_to_operand_aliasing={{2}: (25, {})} | custom-call | tf_op jit(solution)/shard_map/slot/pallas_call | solution.py:448
  457.5 12.0 %slot.37 = (bf16[2,1152,256]{2,1,0:T(8,128)(2,1)}, bf16[2,1152,256]{2,1,0:T(8,128)(2,1)}, bf16[2,3456,1280]{2,1,0:T(8,128)(2,1)}, f32[512,256]{1,0:T(8,128)}) custom-call(s32[2]{0:T(128)} %pad_add_fusion.flag, bf16[6912,1280]{1,0:T(8,128)(2,1)} %bitcast.213, bf16[2,1152,256]{2,1,0:T(8,128)(2,1)} %copy-done.18, ...), custom_call_target="tpu_custom_call", output_to_operand_aliasing={{2}: (25, {})} | custom-call | tf_op jit(solution)/shard_map/slot/pallas_call | solution.py:448
  471.2 7.7 %collective-permute-start.43 = (bf16[2,1152,256]{2,1,0:T(8,128)(2,1)}, bf16[2,1152,256]{2,1,0:T(8,128)(2,1)S(1)}, u32[]{:S(2)}, u32[]{:S(2)}) collective-permute-start(bf16[2,1152,256]{2,1,0:T(8,128)(2,1)} %get-tuple-element.113.refs_20_.refs_12_), channel_id=1, source_target_pairs={{0,8},{24,16},{8,0},{16,24},{1,9},{25,17},{9,1},{17,25},{2,10},{26... | collective-permute-start | bytes 3538952 | tf_op jit(solution)/shard_map/ppermute | solution.py:482
  488.3 11.8 %slot.38 = (bf16[2,1152,256]{2,1,0:T(8,128)(2,1)}, bf16[2,1152,256]{2,1,0:T(8,128)(2,1)}, bf16[2,3456,1280]{2,1,0:T(8,128)(2,1)}, f32[512,256]{1,0:T(8,128)}) custom-call(s32[2]{0:T(128)} %pad_add_fusion.flag, bf16[6912,1280]{1,0:T(8,128)(2,1)} %bitcast.217, bf16[2,1152,256]{2,1,0:T(8,128)(2,1)} %copy-done.20, ...), custom_call_target="tpu_custom_call", output_to_operand_aliasing={{2}: (23, {})} | custom-call | tf_op jit(solution)/shard_map/slot/pallas_call | solution.py:448
  508.1 11.8 %slot.39 = (bf16[2,1152,256]{2,1,0:T(8,128)(2,1)}, bf16[2,1152,256]{2,1,0:T(8,128)(2,1)}, bf16[2,3456,1280]{2,1,0:T(8,128)(2,1)}, f32[512,256]{1,0:T(8,128)}) custom-call(s32[2]{0:T(128)} %pad_add_fusion.flag, bf16[6912,1280]{1,0:T(8,128)(2,1)} %bitcast.219, bf16[2,1152,256]{2,1,0:T(8,128)(2,1)} %copy-done.21, ...), custom_call_target="tpu_custom_call", output_to_operand_aliasing={{2}: (23, {})} | custom-call | tf_op jit(solution)/shard_map/slot/pallas_call | solution.py:448
  521.6 7.6 %collective-permute-start.49 = (bf16[2,1152,256]{2,1,0:T(8,128)(2,1)}, bf16[2,1152,256]{2,1,0:T(8,128)(2,1)S(1)}, u32[]{:S(2)}, u32[]{:S(2)}) collective-permute-start(bf16[2,1152,256]{2,1,0:T(8,128)(2,1)} %get-tuple-element.122.refs_14_.refs_1_), channel_id=1, source_target_pairs={{0,8},{24,16},{8,0},{16,24},{1,9},{25,17},{9,1},{17,25},{2,10},{26... | collective-permute-start | bytes 3538952 | tf_op jit(solution)/shard_map/ppermute | solution.py:482
  533.4 10.1 %slot.40 = (bf16[1,1152,256]{2,1,0:T(8,128)(2,1)}, bf16[2,1152,256]{2,1,0:T(8,128)(2,1)}, bf16[2,3456,1280]{2,1,0:T(8,128)(2,1)}, f32[512,256]{1,0:T(8,128)}) custom-call(s32[2]{0:T(128)} %pad_add_fusion.flag, bf16[6912,1280]{1,0:T(8,128)(2,1)} %bitcast.221, bf16[2,1152,256]{2,1,0:T(8,128)(2,1)} %copy-done.20, ...), custom_call_target="tpu_custom_call", output_to_operand_aliasing={{2}: (17, {})} | custom-call | tf_op jit(solution)/shard_map/slot/pallas_call | solution.py:448
  543.5 7.0 %collective-permute-start.55 = (bf16[2,1152,256]{2,1,0:T(8,128)(2,1)}, bf16[2,1152,256]{2,1,0:T(8,128)(2,1)S(1)}, u32[]{:S(2)}, u32[]{:S(2)}) collective-permute-start(bf16[2,1152,256]{2,1,0:T(8,128)(2,1)} %get-tuple-element.130.refs_3_.refs_0_), channel_id=1, source_target_pairs={{0,8},{24,16},{8,0},{16,24},{1,9},{25,17},{9,1},{17,25},{2,10},{26... | collective-permute-start | bytes 3538952 | tf_op jit(solution)/shard_map/ppermute | solution.py:482
  550.5 7.1 %collective-permute-done.49.refs_15_.refs_2_ = bf16[2,1152,256]{2,1,0:T(8,128)(2,1)S(1)} collective-permute-done((bf16[2,1152,256]{2,1,0:T(8,128)(2,1)}, bf16[2,1152,256]{2,1,0:T(8,128)(2,1)S(1)}, u32[]{:S(2)}, u32[]{:S(2)}) %collective-permute-start.49) | collective-permute-done | bytes 1179680 | tf_op jit(solution)/shard_map/ppermute | solution.py:482
  558.7 10.4 %slot.41 = (bf16[1,1152,256]{2,1,0:T(8,128)(2,1)}, bf16[2,1152,256]{2,1,0:T(8,128)(2,1)}, bf16[2,3456,1280]{2,1,0:T(8,128)(2,1)}, f32[512,256]{1,0:T(8,128)}) custom-call(s32[2]{0:T(128)} %pad_add_fusion.flag, bf16[6912,1280]{1,0:T(8,128)(2,1)} %bitcast.222, bf16[2,1152,256]{2,1,0:T(8,128)(2,1)} %copy-done.21, ...), custom_call_target="tpu_custom_call", output_to_operand_aliasing={{2}: (17, {})} | custom-call | tf_op jit(solution)/shard_map/slot/pallas_call | solution.py:448
  590.6 8.7 %collective-permute-start.57 = (bf16[1,1152,256]{2,1,0:T(8,128)(2,1)}, bf16[1,1152,256]{2,1,0:T(8,128)(2,1)S(1)}, u32[]{:S(2)}, u32[]{:S(2)}) collective-permute-start(bf16[1,1152,256]{2,1,0:T(8,128)(2,1)} %get-tuple-element.134.refs_8_.refs_2_), channel_id=1, source_target_pairs={{0,8},{24,16},{8,0},{16,24},{1,9},{25,17},{9,1},{17,25},{2,10},{26... | collective-permute-start | bytes 1769480 | tf_op jit(solution)/shard_map/ppermute | solution.py:482
  599.3 8.9 %collective-permute-done.52.refs_4_.refs_1_ = bf16[2,1152,256]{2,1,0:T(8,128)(2,1)S(1)} collective-permute-done((bf16[2,1152,256]{2,1,0:T(8,128)(2,1)}, bf16[2,1152,256]{2,1,0:T(8,128)(2,1)S(1)}, u32[]{:S(2)}, u32[]{:S(2)}) %collective-permute-start.52) | collective-permute-done | bytes 1179680 | tf_op jit(solution)/shard_map/ppermute | solution.py:482
  (331 shorter events, 283.9 us)
Async XLA Ops:
  7.2 57.2 %all-gather.7.cloned.1.call-start = ((), (), s32[]{:S(2)}) async-start(), calls=%async_computation | async-start | bytes 8847360 | tf_op jit(solution)/shard_map/all_gather | solution.py:500
  7.9 132.9 %all-gather.9.cloned.1.call-start = ((), (), s32[]{:S(2)}) async-start(), calls=%async_computation.1 | async-start | bytes 8847360 | tf_op jit(solution)/shard_map/all_gather | solution.py:607
  8.0 43.1 %collective-permute-start = (bf16[128,6912]{1,0:T(8,128)(2,1)}, bf16[128,6912]{1,0:T(8,128)(2,1)S(1)}, u32[]{:S(2)}, u32[]{:S(2)}) collective-permute-start(bf16[128,6912]{1,0:T(8,128)(2,1)} %bitcast.331), channel_id=1, source_target_pairs={{0,8},{24,16},{1,9},{25,17},{2,10},{26,18},{3,11},{27,19},{4,12},{... | collective-permute-start | bytes 5308424 | tf_op jit(solution)/shard_map/ppermute | solution.py:480
  60.2 125.5 %all-gather.11.cloned.1.call-start = ((), (), s32[]{:S(2)}) async-start(), calls=%async_computation.2 | async-start | bytes 8847360 | tf_op jit(solution)/shard_map/all_gather | solution.py:607
  63.6 39.6 %collective-permute-start.6 = (bf16[128,3456]{1,0:T(8,128)(2,1)}, bf16[128,3456]{1,0:T(8,128)(2,1)S(1)}, u32[]{:S(2)}, u32[]{:S(2)}) collective-permute-start(bf16[128,3456]{1,0:T(8,128)(2,1)} %constant_dynamic-slice_fusion.2), channel_id=1, source_target_pairs={{8,16},{16,8},{9,17},{17,9},{10,18},{18,10},{11,19},{19,11},{12,20... | collective-permute-start | bytes 2654216 | tf_op jit(solution)/shard_map/ppermute | solution.py:481
  164.7 47.5 %collective-permute-start.18 = (bf16[2,1280,256]{2,1,0:T(8,128)(2,1)}, bf16[2,1280,256]{2,1,0:T(8,128)(2,1)S(1)}, u32[]{:S(2)}, u32[]{:S(2)}) collective-permute-start(bf16[2,1280,256]{2,1,0:T(8,128)(2,1)} %get-tuple-element.82), channel_id=1, source_target_pairs={{0,8},{24,16},{8,0},{16,24},{1,9},{25,17},{9,1},{17,25},{2,10},{26... | collective-permute-start | bytes 3932168 | tf_op jit(solution)/shard_map/ppermute | solution.py:482
  166.7 46.3 %collective-permute-start.19 = (bf16[2,1280,256]{2,1,0:T(8,128)(2,1)}, bf16[2,1280,256]{2,1,0:T(8,128)(2,1)}, u32[]{:S(2)}, u32[]{:S(2)}) collective-permute-start(bf16[2,1280,256]{2,1,0:T(8,128)(2,1)} %get-tuple-element.78.refs_24_), channel_id=1, source_target_pairs={{8,16},{16,8},{9,17},{17,9},{10,18},{18,10},{11,19},{19,11},{12,20... | collective-permute-start | bytes 3932168 | tf_op jit(solution)/shard_map/ppermute | solution.py:481
  196.9 43.4 %collective-permute-start.14 = (bf16[2,1280,256]{2,1,0:T(8,128)(2,1)}, bf16[2,1280,256]{2,1,0:T(8,128)(2,1)S(1)}, u32[]{:S(2)}, u32[]{:S(2)}) collective-permute-start(bf16[2,1280,256]{2,1,0:T(8,128)(2,1)} %get-tuple-element.79.refs_22_), channel_id=1, source_target_pairs={{0,8},{24,16},{8,0},{16,24},{1,9},{25,17},{9,1},{17,25},{2,10},{26... | collective-permute-start | bytes 3932168 | tf_op jit(solution)/shard_map/ppermute | solution.py:482
  199.2 41.0 %collective-permute-start.16 = (bf16[2,1280,256]{2,1,0:T(8,128)(2,1)}, bf16[2,1280,256]{2,1,0:T(8,128)(2,1)}, u32[]{:S(2)}, u32[]{:S(2)}) collective-permute-start(bf16[2,1280,256]{2,1,0:T(8,128)(2,1)} %get-tuple-element.80.refs_23_), channel_id=1, source_target_pairs={{8,16},{16,8},{9,17},{17,9},{10,18},{18,10},{11,19},{19,11},{12,20... | collective-permute-start | bytes 3932168 | tf_op jit(solution)/shard_map/ppermute | solution.py:481
  224.5 42.7 %collective-permute-start.25 = (bf16[2,1280,256]{2,1,0:T(8,128)(2,1)}, bf16[2,1280,256]{2,1,0:T(8,128)(2,1)}, u32[]{:S(2)}, u32[]{:S(2)}) collective-permute-start(bf16[2,1280,256]{2,1,0:T(8,128)(2,1)} %get-tuple-element.84.refs_25_), channel_id=1, source_target_pairs={{8,16},{16,8},{9,17},{17,9},{10,18},{18,10},{11,19},{19,11},{12,20... | collective-permute-start | bytes 3932168 | tf_op jit(solution)/shard_map/ppermute | solution.py:481
  226.5 41.9 %collective-permute-start.24 = (bf16[2,1280,256]{2,1,0:T(8,128)(2,1)}, bf16[2,1280,256]{2,1,0:T(8,128)(2,1)S(1)}, u32[]{:S(2)}, u32[]{:S(2)}) collective-permute-start(bf16[2,1280,256]{2,1,0:T(8,128)(2,1)} %get-tuple-element.87.refs_22_), channel_id=1, source_target_pairs={{0,8},{24,16},{8,0},{16,24},{1,9},{25,17},{9,1},{17,25},{2,10},{26... | collective-permute-start | bytes 3932168 | tf_op jit(solution)/shard_map/ppermute | solution.py:482
  252.5 43.9 %collective-permute-start.20 = (bf16[2,1280,256]{2,1,0:T(8,128)(2,1)}, bf16[2,1280,256]{2,1,0:T(8,128)(2,1)S(1)}, u32[]{:S(2)}, u32[]{:S(2)}) collective-permute-start(bf16[2,1280,256]{2,1,0:T(8,128)(2,1)} %get-tuple-element.85.refs_24_.refs_20_), channel_id=1, source_target_pairs={{0,8},{24,16},{8,0},{16,24},{1,9},{25,17},{9,1},{17,25},{2,10},{26... | collective-permute-start | bytes 3932168 | tf_op jit(solution)/shard_map/ppermute | solution.py:482
  255.5 41.6 %collective-permute-start.22 = (bf16[2,1280,256]{2,1,0:T(8,128)(2,1)}, bf16[2,1280,256]{2,1,0:T(8,128)(2,1)}, u32[]{:S(2)}, u32[]{:S(2)}) collective-permute-start(bf16[2,1280,256]{2,1,0:T(8,128)(2,1)} %get-tuple-element.86.refs_25_), channel_id=1, source_target_pairs={{8,16},{16,8},{9,17},{17,9},{10,18},{18,10},{11,19},{19,11},{12,20... | collective-permute-start | bytes 3932168 | tf_op jit(solution)/shard_map/ppermute | solution.py:481
  280.5 43.2 %collective-permute-start.30 = (bf16[2,1280,256]{2,1,0:T(8,128)(2,1)}, bf16[2,1280,256]{2,1,0:T(8,128)(2,1)}, u32[]{:S(2)}, u32[]{:S(2)}) collective-permute-start(bf16[2,1280,256]{2,1,0:T(8,128)(2,1)} %get-tuple-element.89.refs_28_), channel_id=1, source_target_pairs={{8,16},{16,8},{9,17},{17,9},{10,18},{18,10},{11,19},{19,11},{12,20... | collective-permute-start | bytes 3932168 | tf_op jit(solution)/shard_map/ppermute | solution.py:481
  282.2 42.3 %collective-permute-start.29 = (bf16[2,1280,256]{2,1,0:T(8,128)(2,1)}, bf16[2,1280,256]{2,1,0:T(8,128)(2,1)S(1)}, u32[]{:S(2)}, u32[]{:S(2)}) collective-permute-start(bf16[2,1280,256]{2,1,0:T(8,128)(2,1)} %get-tuple-element.92.refs_24_.refs_21_), channel_id=1, source_target_pairs={{0,8},{24,16},{8,0},{16,24},{1,9},{25,17},{9,1},{17,25},{2,10},{26... | collective-permute-start | bytes 3932168 | tf_op jit(solution)/shard_map/ppermute | solution.py:482
  309.8 34.3 %collective-permute-start.27 = (bf16[2,1280,256]{2,1,0:T(8,128)(2,1)}, bf16[2,1280,256]{2,1,0:T(8,128)(2,1)}, u32[]{:S(2)}, u32[]{:S(2)}) collective-permute-start(bf16[2,1280,256]{2,1,0:T(8,128)(2,1)} %get-tuple-element.91.refs_30_), channel_id=1, source_target_pairs={{8,16},{16,8},{9,17},{17,9},{10,18},{18,10},{11,19},{19,11},{12,20... | collective-permute-start | bytes 3932168 | tf_op jit(solution)/shard_map/ppermute | solution.py:481
  311.5 41.2 %collective-permute-start.26 = (bf16[2,1280,256]{2,1,0:T(8,128)(2,1)}, bf16[2,1280,256]{2,1,0:T(8,128)(2,1)}, u32[]{:S(2)}, u32[]{:S(2)}) collective-permute-start(bf16[2,1280,256]{2,1,0:T(8,128)(2,1)} %get-tuple-element.90.refs_22_.refs_20_), channel_id=1, source_target_pairs={{0,8},{24,16},{8,0},{16,24},{1,9},{25,17},{9,1},{17,25},{2,10},{26... | collective-permute-start | bytes 3932168 | tf_op jit(solution)/shard_map/ppermute | solution.py:482
  338.2 42.5 %collective-permute-start.35 = (bf16[2,1280,256]{2,1,0:T(8,128)(2,1)}, bf16[2,1280,256]{2,1,0:T(8,128)(2,1)S(1)}, u32[]{:S(2)}, u32[]{:S(2)}) collective-permute-start(bf16[2,1280,256]{2,1,0:T(8,128)(2,1)} %get-tuple-element.101.refs_23_.refs_20_), channel_id=1, source_target_pairs={{0,8},{24,16},{8,0},{16,24},{1,9},{25,17},{9,1},{17,25},{2,10},{26... | collective-permute-start | bytes 3932168 | tf_op jit(solution)/shard_map/ppermute | solution.py:482
  342.3 39.1 %collective-permute-start.36 = (bf16[2,1280,256]{2,1,0:T(8,128)(2,1)}, bf16[2,1280,256]{2,1,0:T(8,128)(2,1)}, u32[]{:S(2)}, u32[]{:S(2)}) collective-permute-start(bf16[2,1280,256]{2,1,0:T(8,128)(2,1)} %get-tuple-element.98.refs_28_), channel_id=1, source_target_pairs={{8,16},{16,8},{9,17},{17,9},{10,18},{18,10},{11,19},{19,11},{12,20... | collective-permute-start | bytes 3932168 | tf_op jit(solution)/shard_map/ppermute | solution.py:481
  365.0 35.0 %collective-permute-start.34 = (bf16[2,1152,256]{2,1,0:T(8,128)(2,1)}, bf16[2,1152,256]{2,1,0:T(8,128)(2,1)}, u32[]{:S(2)}, u32[]{:S(2)}) collective-permute-start(bf16[2,1152,256]{2,1,0:T(8,128)(2,1)} %get-tuple-element.100.refs_28_), channel_id=1, source_target_pairs={{8,16},{16,8},{9,17},{17,9},{10,18},{18,10},{11,19},{19,11},{12,20... | collective-permute-start | bytes 3538952 | tf_op jit(solution)/shard_map/ppermute | solution.py:481
  366.9 39.1 %collective-permute-start.32 = (bf16[2,1152,256]{2,1,0:T(8,128)(2,1)}, bf16[2,1152,256]{2,1,0:T(8,128)(2,1)S(1)}, u32[]{:S(2)}, u32[]{:S(2)}) collective-permute-start(bf16[2,1152,256]{2,1,0:T(8,128)(2,1)} %get-tuple-element.99.refs_22_.refs_20_), channel_id=1, source_target_pairs={{0,8},{24,16},{8,0},{16,24},{1,9},{25,17},{9,1},{17,25},{2,10},{26... | collective-permute-start | bytes 3538952 | tf_op jit(solution)/shard_map/ppermute | solution.py:482
  394.2 41.5 %collective-permute-start.42 = (bf16[2,1280,256]{2,1,0:T(8,128)(2,1)}, bf16[2,1280,256]{2,1,0:T(8,128)(2,1)}, u32[]{:S(2)}, u32[]{:S(2)}) collective-permute-start(bf16[2,1280,256]{2,1,0:T(8,128)(2,1)} %get-tuple-element.105.refs_28_), channel_id=1, source_target_pairs={{8,16},{16,8},{9,17},{17,9},{10,18},{18,10},{11,19},{19,11},{12,20... | collective-permute-start | bytes 3932168 | tf_op jit(solution)/shard_map/ppermute | solution.py:481
  395.9 39.8 %collective-permute-start.41 = (bf16[2,1152,256]{2,1,0:T(8,128)(2,1)}, bf16[2,1152,256]{2,1,0:T(8,128)(2,1)}, u32[]{:S(2)}, u32[]{:S(2)}) collective-permute-start(bf16[2,1152,256]{2,1,0:T(8,128)(2,1)} %get-tuple-element.108.refs_22_.refs_18_), channel_id=1, source_target_pairs={{0,8},{24,16},{8,0},{16,24},{1,9},{25,17},{9,1},{17,25},{2,10},{26... | collective-permute-start | bytes 3538952 | tf_op jit(solution)/shard_map/ppermute | solution.py:482
  421.1 35.5 %collective-permute-start.37 = (bf16[2,1152,256]{2,1,0:T(8,128)(2,1)}, bf16[2,1152,256]{2,1,0:T(8,128)(2,1)S(1)}, u32[]{:S(2)}, u32[]{:S(2)}) collective-permute-start(bf16[2,1152,256]{2,1,0:T(8,128)(2,1)} %get-tuple-element.106.refs_22_.refs_18_), channel_id=1, source_target_pairs={{0,8},{24,16},{8,0},{16,24},{1,9},{25,17},{9,1},{17,25},{2,10},{26... | collective-permute-start | bytes 3538952 | tf_op jit(solution)/shard_map/ppermute | solution.py:482
  448.6 38.6 %collective-permute-start.47 = (bf16[2,1152,256]{2,1,0:T(8,128)(2,1)}, bf16[2,1152,256]{2,1,0:T(8,128)(2,1)}, u32[]{:S(2)}, u32[]{:S(2)}) collective-permute-start(bf16[2,1152,256]{2,1,0:T(8,128)(2,1)} %get-tuple-element.112.refs_27_), channel_id=1, source_target_pairs={{8,16},{16,8},{9,17},{17,9},{10,18},{18,10},{11,19},{19,11},{12,20... | collective-permute-start | bytes 3538952 | tf_op jit(solution)/shard_map/ppermute | solution.py:481
  450.4 36.9 %collective-permute-start.46 = (bf16[2,1152,256]{2,1,0:T(8,128)(2,1)}, bf16[2,1152,256]{2,1,0:T(8,128)(2,1)S(1)}, u32[]{:S(2)}, u32[]{:S(2)}) collective-permute-start(bf16[2,1152,256]{2,1,0:T(8,128)(2,1)} %get-tuple-element.115.refs_20_.refs_12_), channel_id=1, source_target_pairs={{0,8},{24,16},{8,0},{16,24},{1,9},{25,17},{9,1},{17,25},{2,10},{26... | collective-permute-start | bytes 3538952 | tf_op jit(solution)/shard_map/ppermute | solution.py:482
  469.5 34.7 %collective-permute-start.44 = (bf16[2,1152,256]{2,1,0:T(8,128)(2,1)}, bf16[2,1152,256]{2,1,0:T(8,128)(2,1)}, u32[]{:S(2)}, u32[]{:S(2)}) collective-permute-start(bf16[2,1152,256]{2,1,0:T(8,128)(2,1)} %get-tuple-element.114.refs_26_), channel_id=1, source_target_pairs={{8,16},{16,8},{9,17},{17,9},{10,18},{18,10},{11,19},{19,11},{12,20... | collective-permute-start | bytes 3538952 | tf_op jit(solution)/shard_map/ppermute | solution.py:481
  471.2 35.9 %collective-permute-start.43 = (bf16[2,1152,256]{2,1,0:T(8,128)(2,1)}, bf16[2,1152,256]{2,1,0:T(8,128)(2,1)S(1)}, u32[]{:S(2)}, u32[]{:S(2)}) collective-permute-start(bf16[2,1152,256]{2,1,0:T(8,128)(2,1)} %get-tuple-element.113.refs_20_.refs_12_), channel_id=1, source_target_pairs={{0,8},{24,16},{8,0},{16,24},{1,9},{25,17},{9,1},{17,25},{2,10},{26... | collective-permute-start | bytes 3538952 | tf_op jit(solution)/shard_map/ppermute | solution.py:482
  521.6 36.0 %collective-permute-start.49 = (bf16[2,1152,256]{2,1,0:T(8,128)(2,1)}, bf16[2,1152,256]{2,1,0:T(8,128)(2,1)S(1)}, u32[]{:S(2)}, u32[]{:S(2)}) collective-permute-start(bf16[2,1152,256]{2,1,0:T(8,128)(2,1)} %get-tuple-element.122.refs_14_.refs_1_), channel_id=1, source_target_pairs={{0,8},{24,16},{8,0},{16,24},{1,9},{25,17},{9,1},{17,25},{2,10},{26... | collective-permute-start | bytes 3538952 | tf_op jit(solution)/shard_map/ppermute | solution.py:482
  543.5 39.4 %collective-permute-start.55 = (bf16[2,1152,256]{2,1,0:T(8,128)(2,1)}, bf16[2,1152,256]{2,1,0:T(8,128)(2,1)S(1)}, u32[]{:S(2)}, u32[]{:S(2)}) collective-permute-start(bf16[2,1152,256]{2,1,0:T(8,128)(2,1)} %get-tuple-element.130.refs_3_.refs_0_), channel_id=1, source_target_pairs={{0,8},{24,16},{8,0},{16,24},{1,9},{25,17},{9,1},{17,25},{2,10},{26... | collective-permute-start | bytes 3538952 | tf_op jit(solution)/shard_map/ppermute | solution.py:482
  569.1 39.1 %collective-permute-start.52 = (bf16[2,1152,256]{2,1,0:T(8,128)(2,1)}, bf16[2,1152,256]{2,1,0:T(8,128)(2,1)S(1)}, u32[]{:S(2)}, u32[]{:S(2)}) collective-permute-start(bf16[2,1152,256]{2,1,0:T(8,128)(2,1)} %get-tuple-element.128.refs_3_.refs_0_), channel_id=1, source_target_pairs={{0,8},{24,16},{8,0},{16,24},{1,9},{25,17},{9,1},{17,25},{2,10},{26... | collective-permute-start | bytes 3538952 | tf_op jit(solution)/shard_map/ppermute | solution.py:482
  579.4 39.7 %collective-permute-start.59 = (bf16[1,256,256]{2,1,0:T(8,128)(2,1)}, bf16[1,256,256]{2,1,0:T(8,128)(2,1)}, u32[]{:S(2)}, u32[]{:S(2)}) collective-permute-start(bf16[1,256,256]{2,1,0:T(8,128)(2,1)} %dynamic-slice_bitcast_fusion.4), channel_id=1, source_target_pairs={{0,4},{4,0},{1,5},{5,1},{2,6},{6,2},{3,7},{7,3},{8,12},{12,8},{9,1... | collective-permute-start | bytes 393224 | tf_op jit(solution)/shard_map/ppermute | solution.py:483
  (91 other events, 922.1 us)
Sparse Core Ops, SparseCore 0:
  9.6 53.5 all-gather.6
  64.7 50.8 all-gather.8
  117.7 50.8 all-gather.10

commit v3 on v2

--- a/solution.py
+++ b/solution.py
@@ -618,7 +618,7 @@
         return crossed
 
     lead_far = at_once(lead, product)
-    own_square = squares(full_acts, [lead.near[0]] + list(came_pass.values()))
+    own_square = squares(full_acts, [lead.near[0]])
     carries, crossings, starts = {}, {}, {}
 
     def ship(slot, b):
@@ -628,7 +628,7 @@
             crossings[slot + LAG + g] = (b, g, 1)
 
     if last == 1 and count > 1:
-        start_pass(-1, slot_call(plan, flags, last, send=inward(1), deps=[lead.near[0]] + list(came_pass.values())))
+        start_pass(-1, slot_call(plan, flags, last, send=inward(1), deps=[own_square, lead.outer[0]] + list(came_pass.values())))
     other_cuts = cut(plan, cross, [own_square] + list(sent_pass.values())[-1:])
     other_parts = [gather_col(x) for x in other_cuts]
     early = min(LAG, plan.groups - 1) if last == 1 else plan.groups - 1
@@ -659,7 +659,7 @@
     came_mid, backs = {}, {}
     buffer = None
     results = []
-    chain = [next_products, lead_far] + list(came_pass.values())[-1:]
+    chain = [next_products, lead_far]
     ahead_total, result_total = None, None
     for slot in range(count + 3 * LAG):
         deps = list(chain)
@@ -685,7 +685,8 @@
             stage["send"] = inward(slot + LAG)
         if slot < max(carries, default=0):
             stage.setdefault("cross", packed(lead.near[0][0]))
-            stage.setdefault("carry", lead.inwards(0))
+            if slot == 0:
+                stage.setdefault("carry", lead.inwards(0))
         index = slot - LAG
         if now(index):
             piece = plan.pieces[index]

time: 662 us -> 641 us (0.968)
  waiting for transfers between devices: 170 us -> 109 us
  starting transfers between devices: 148 us -> 192 us
    ppermute x22, waiting for transfers between devices: 93.9 us -> 28.1 us  [local(): lax.ppermute(x, 'task', step_in(last - 1) + step_out(last - 1))]
    ppermute x22, starting transfers between devices: 84.5 us -> 128 us  [local(): lax.ppermute(x, 'task', step_in(last - 1) + step_out(last - 1))]
    unnamed x115 -> x119, local copies, waits for them, and re-layouts: 22.8 us -> 22.7 us
  transfers between devices with their start and end apart: 66 -> 66, of which waited for: 33 -> 23; matrix products, arithmetic and copies ran while one was open for 5% -> 4% of each run, Pallas kernels for 40% -> 42%
where the time goes in v3:
time: 641 us; the launch traced here: 631 us
  Pallas kernels  263 us (41%)
  starting transfers between devices  192 us (30%)
  waiting for transfers between devices  109 us (17%)
  local copies, waits for them, and re-layouts  40.6 us (6%)
  between operations  15.4 us (2%)
  other arithmetic  10.4 us (2%)
    pallas_call x23, Pallas kernels, slot_call(): pl.pallas_call(body, grid_spec=pltpu.PrefetchScalarGridSpec(num_scalar_pr...  224 us
    ppermute x22, starting transfers between devices, local(): lax.ppermute(x, 'task', step_in(last - 1) + step_out(last - 1))  128 us
    ppermute x20, waiting for transfers between devices, local(): lax.ppermute(x, 'row', [(i, (i + s) % rows_n) for i in range(rows_n)])  45.6 us
    ppermute x1, waiting for transfers between devices, local(): send_in = lambda x: lax.ppermute(x, 'task', all_in)  34.6 us
    ppermute x20, starting transfers between devices, local(): lax.ppermute(x, 'task', [(last, side_n), (side_n, last)])  29.6 us
    ppermute x20, starting transfers between devices, local(): lax.ppermute(x, 'row', [(i, (i + s) % rows_n) for i in range(rows_n)])  28.9 us
    ppermute x22, waiting for transfers between devices, local(): lax.ppermute(x, 'task', step_in(last - 1) + step_out(last - 1))  28.1 us
    unnamed x119, local copies, waits for them, and re-layouts  22.7 us
  transfers between devices with their start and end apart: 66, of which 23 were waited for; matrix products, arithmetic and copies ran while one was open for 4% of the time, Pallas kernels for 42%

profile of v3, /device:TPU:0, one launch (start us, length us, event | category | flops | bytes accessed | tf_op | source)
XLA Modules:
  0.0 631.1 jit_solution(2537626168981274936)
XLA Ops:
  16.5 34.6 %collective-permute-done.refs_0_ = bf16[128,6912]{1,0:T(8,128)(2,1)S(1)} collective-permute-done((bf16[128,6912]{1,0:T(8,128)(2,1)}, bf16[128,6912]{1,0:T(8,128)(2,1)S(1)}, u32[]{:S(2)}, u32[]{:S(2)}) %collective-permute-start) | collective-permute-done | bytes 1769504 | tf_op jit(solution)/shard_map/ppermute | solution.py:480
  64.4 7.5 %group_product.2 = bf16[1,512,256]{2,1,0:T(8,128)(2,1)} custom-call(bf16[512,6912]{1,0:T(8,128)(2,1)} %bitcast.223, bf16[6912,1280]{1,0:T(8,128)(2,1)} %bitcast.156, bf16[2,3456,128]{2,1,0:T(8,128)(2,1)} %cut.2.rest_1_), custom_call_target="tpu_custom_call" | custom-call | tf_op jit(solution)/shard_map/group_product/pallas_call | solution.py:70
  82.5 10.2 %squares.1.refs_2_.refs_6_.refs_8_ = bf16[6912,512]{1,0:T(8,128)(2,1)} custom-call(bf16[512,6912]{1,0:T(8,128)(2,1)} %bitcast.224, bf16[1,256,256]{2,1,0:T(8,128)(2,1)} %copy-done.37), custom_call_target="tpu_custom_call" | custom-call | tf_op jit(solution)/shard_map/squares/pallas_call | solution.py:93
  102.7 13.2 %group_product.3.refs_12_ = bf16[2,512,256]{2,1,0:T(8,128)(2,1)} custom-call(bf16[512,6912]{1,0:T(8,128)(2,1)} %bitcast.225, bf16[6912,1280]{1,0:T(8,128)(2,1)} %bitcast.159, bf16[6912,1280]{1,0:T(8,128)(2,1)} %bitcast.160, bf16[2,3456,128]{2,1,0:T(8,128)(2,1)} %cut.3.rest_2_, bf16[1,256,256]{2,1,0:T(8,128)(2,1)} %bitcast.338, ...), custom_call_target="tpu_custom_call" | custom-call | tf_op jit(solution)/shard_map/group_product/pallas_call | solution.py:70
  130.0 8.5 %slot.25 = (bf16[2,1280,256]{2,1,0:T(8,128)(2,1)}, bf16[2,1280,256]{2,1,0:T(8,128)(2,1)}, f32[512,256]{1,0:T(8,128)}) custom-call(s32[2]{0:T(128)} %pad_add_fusion.flag, bf16[6912,1280]{1,0:T(8,128)(2,1)} %bitcast.161, bf16[2,1152,256]{2,1,0:T(8,128)(2,1)} %copy-done.22, bf16[6912,512]{1,0:T(8,128)(2,1)} %squares.1.refs_2_.refs_6_.refs_8_, ...), custom_call_target="tpu_custom_call" | custom-call | tf_op jit(solution)/shard_map/slot/pallas_call | solution.py:448
  144.6 8.8 %slot.26 = (bf16[2,1280,256]{2,1,0:T(8,128)(2,1)}, bf16[2,1280,256]{2,1,0:T(8,128)(2,1)}, f32[512,256]{1,0:T(8,128)}) custom-call(s32[2]{0:T(128)} %pad_add_fusion.flag, bf16[6912,1280]{1,0:T(8,128)(2,1)} %bitcast.168, bf16[2,1152,256]{2,1,0:T(8,128)(2,1)} %copy-done.30, bf16[6912,512]{1,0:T(8,128)(2,1)} %squares.1.refs_2_.refs_6_.refs_8_, ...), custom_call_target="tpu_custom_call" | custom-call | tf_op jit(solution)/shard_map/slot/pallas_call | solution.py:448
  163.0 8.8 %collective-permute-done.9.refs_1_.refs_7_ = bf16[2,1280,256]{2,1,0:T(8,128)(2,1)} collective-permute-done((bf16[2,1280,256]{2,1,0:T(8,128)(2,1)}, bf16[2,1280,256]{2,1,0:T(8,128)(2,1)}, u32[]{:S(2)}, u32[]{:S(2)}) %collective-permute-start.9) | collective-permute-done | bytes 1310752 | tf_op jit(solution)/shard_map/ppermute | solution.py:482
  173.4 11.1 %slot.27 = (bf16[2,1280,256]{2,1,0:T(8,128)(2,1)}, bf16[2,1152,256]{2,1,0:T(8,128)(2,1)}, f32[512,256]{1,0:T(8,128)}) custom-call(s32[2]{0:T(128)} %pad_add_fusion.flag, bf16[6912,1280]{1,0:T(8,128)(2,1)} %bitcast.169, bf16[2,1280,256]{2,1,0:T(8,128)(2,1)} %collective-permute-done.9.refs_1_.refs_7_, bf16[6912,512]{1,0:T(8,128)(2,1)} %squares.1.refs_2_.refs_6_.refs_8_, ...), custom_call_target="tpu_custom_call" | custom-call | tf_op jit(solution)/shard_map/slot/pallas_call | solution.py:448
  190.2 9.6 %collective-permute-done.18.refs_1_.refs_7_ = bf16[2,1280,256]{2,1,0:T(8,128)(2,1)S(1)} collective-permute-done((bf16[2,1280,256]{2,1,0:T(8,128)(2,1)}, bf16[2,1280,256]{2,1,0:T(8,128)(2,1)S(1)}, u32[]{:S(2)}, u32[]{:S(2)}) %collective-permute-start.18) | collective-permute-done | bytes 1310752 | tf_op jit(solution)/shard_map/ppermute | solution.py:482
  201.4 10.8 %slot.28 = (bf16[2,1280,256]{2,1,0:T(8,128)(2,1)}, bf16[2,1152,256]{2,1,0:T(8,128)(2,1)}, f32[512,256]{1,0:T(8,128)}) custom-call(s32[2]{0:T(128)} %pad_add_fusion.flag, bf16[6912,1280]{1,0:T(8,128)(2,1)} %bitcast.174, bf16[2,1280,256]{2,1,0:T(8,128)(2,1)} %copy-done.28, bf16[6912,512]{1,0:T(8,128)(2,1)} %squares.1.refs_2_.refs_6_.refs_8_, ...), custom_call_target="tpu_custom_call" | custom-call | tf_op jit(solution)/shard_map/slot/pallas_call | solution.py:448
  226.1 11.0 %slot.29 = (bf16[2,1280,256]{2,1,0:T(8,128)(2,1)}, bf16[2,1280,256]{2,1,0:T(8,128)(2,1)}, f32[512,256]{1,0:T(8,128)}) custom-call(s32[2]{0:T(128)} %pad_add_fusion.flag, bf16[6912,1280]{1,0:T(8,128)(2,1)} %bitcast.179, bf16[2,1152,256]{2,1,0:T(8,128)(2,1)} %copy-done.25, bf16[6912,512]{1,0:T(8,128)(2,1)} %squares.1.refs_2_.refs_6_.refs_8_, ...), custom_call_target="tpu_custom_call" | custom-call | tf_op jit(solution)/shard_map/slot/pallas_call | solution.py:448
  253.1 11.2 %slot.30 = (bf16[2,1280,256]{2,1,0:T(8,128)(2,1)}, bf16[2,1152,256]{2,1,0:T(8,128)(2,1)}, f32[512,256]{1,0:T(8,128)}) custom-call(s32[2]{0:T(128)} %pad_add_fusion.flag, bf16[6912,1280]{1,0:T(8,128)(2,1)} %bitcast.188, bf16[2,1152,256]{2,1,0:T(8,128)(2,1)} %copy-done.24, bf16[6912,512]{1,0:T(8,128)(2,1)} %squares.1.refs_2_.refs_6_.refs_8_, ...), custom_call_target="tpu_custom_call" | custom-call | tf_op jit(solution)/shard_map/slot/pallas_call | solution.py:448
  279.5 12.3 %slot.31 = (bf16[2,1280,256]{2,1,0:T(8,128)(2,1)}, bf16[2,1152,256]{2,1,0:T(8,128)(2,1)}, bf16[2,3456,1280]{2,1,0:T(8,128)(2,1)}, f32[512,256]{1,0:T(8,128)}) custom-call(s32[2]{0:T(128)} %pad_add_fusion.flag, bf16[6912,1280]{1,0:T(8,128)(2,1)} %bitcast.189, bf16[2,1280,256]{2,1,0:T(8,128)(2,1)} %copy-done.15, ...), custom_call_target="tpu_custom_call" | custom-call | tf_op jit(solution)/shard_map/slot/pallas_call | solution.py:448
  293.6 9.0 %collective-permute-start.26 = (bf16[2,1152,256]{2,1,0:T(8,128)(2,1)}, bf16[2,1152,256]{2,1,0:T(8,128)(2,1)}, u32[]{:S(2)}, u32[]{:S(2)}) collective-permute-start(bf16[2,1152,256]{2,1,0:T(8,128)(2,1)} %get-tuple-element.90.refs_22_.refs_20_), channel_id=1, source_target_pairs={{0,8},{24,16},{8,0},{16,24},{1,9},{25,17},{9,1},{17,25},{2,10},{26... | collective-permute-start | bytes 3538952 | tf_op jit(solution)/shard_map/ppermute | solution.py:482
  311.8 12.6 %slot.32 = (bf16[2,1280,256]{2,1,0:T(8,128)(2,1)}, bf16[2,1280,256]{2,1,0:T(8,128)(2,1)}, bf16[2,3456,1280]{2,1,0:T(8,128)(2,1)}, f32[512,256]{1,0:T(8,128)}) custom-call(s32[2]{0:T(128)} %pad_add_fusion.flag, bf16[6912,1280]{1,0:T(8,128)(2,1)} %bitcast.193, bf16[2,1152,256]{2,1,0:T(8,128)(2,1)} %copy-done.20, ...), custom_call_target="tpu_custom_call", output_to_operand_aliasing={{2}: (27, {})} | custom-call | tf_op jit(solution)/shard_map/slot/pallas_call | solution.py:448
  329.8 12.3 %slot.33 = (bf16[2,1152,256]{2,1,0:T(8,128)(2,1)}, bf16[2,1152,256]{2,1,0:T(8,128)(2,1)}, bf16[2,3456,1280]{2,1,0:T(8,128)(2,1)}, f32[512,256]{1,0:T(8,128)}) custom-call(s32[2]{0:T(128)} %pad_add_fusion.flag, bf16[6912,1280]{1,0:T(8,128)(2,1)} %bitcast.197, ...), custom_call_target="tpu_custom_call", output_to_operand_aliasing={{2}: (25, {})} | custom-call | tf_op jit(solution)/shard_map/slot/pallas_call | solution.py:448
  342.1 13.3 %collective-permute-start.32 = (bf16[2,1152,256]{2,1,0:T(8,128)(2,1)}, bf16[2,1152,256]{2,1,0:T(8,128)(2,1)}, u32[]{:S(2)}, u32[]{:S(2)}) collective-permute-start(bf16[2,1152,256]{2,1,0:T(8,128)(2,1)} %get-tuple-element.99.refs_22_.refs_20_), channel_id=1, source_target_pairs={{0,8},{24,16},{8,0},{16,24},{1,9},{25,17},{9,1},{17,25},{2,10},{26... | collective-permute-start | bytes 3538952 | tf_op jit(solution)/shard_map/ppermute | solution.py:482
  365.6 12.3 %slot.34 = (bf16[2,1280,256]{2,1,0:T(8,128)(2,1)}, bf16[2,1152,256]{2,1,0:T(8,128)(2,1)}, bf16[2,3456,1280]{2,1,0:T(8,128)(2,1)}, f32[512,256]{1,0:T(8,128)}) custom-call(s32[2]{0:T(128)} %pad_add_fusion.flag, bf16[6912,1280]{1,0:T(8,128)(2,1)} %bitcast.204, bf16[2,1280,256]{2,1,0:T(8,128)(2,1)} %copy-done.16, ...), custom_call_target="tpu_custom_call", output_to_operand_aliasing={{2}: (26, {})} | custom-call | tf_op jit(solution)/shard_map/slot/pallas_call | solution.py:448
  379.7 8.0 %collective-permute-start.41 = (bf16[2,1152,256]{2,1,0:T(8,128)(2,1)}, bf16[2,1152,256]{2,1,0:T(8,128)(2,1)S(1)}, u32[]{:S(2)}, u32[]{:S(2)}) collective-permute-start(bf16[2,1152,256]{2,1,0:T(8,128)(2,1)} %get-tuple-element.108.refs_22_.refs_18_), channel_id=1, source_target_pairs={{0,8},{24,16},{8,0},{16,24},{1,9},{25,17},{9,1},{17,25},{2,10},{26... | collective-permute-start | bytes 3538952 | tf_op jit(solution)/shard_map/ppermute | solution.py:482
  387.7 12.2 %slot.35 = (bf16[2,1152,256]{2,1,0:T(8,128)(2,1)}, bf16[2,1152,256]{2,1,0:T(8,128)(2,1)}, bf16[2,3456,1280]{2,1,0:T(8,128)(2,1)}, f32[512,256]{1,0:T(8,128)}) custom-call(s32[2]{0:T(128)} %pad_add_fusion.flag, bf16[6912,1280]{1,0:T(8,128)(2,1)} %bitcast.205, ...), custom_call_target="tpu_custom_call", output_to_operand_aliasing={{2}: (25, {})} | custom-call | tf_op jit(solution)/shard_map/slot/pallas_call | solution.py:448
  399.9 8.8 %collective-permute-start.37 = (bf16[2,1152,256]{2,1,0:T(8,128)(2,1)}, bf16[2,1152,256]{2,1,0:T(8,128)(2,1)S(1)}, u32[]{:S(2)}, u32[]{:S(2)}) collective-permute-start(bf16[2,1152,256]{2,1,0:T(8,128)(2,1)} %get-tuple-element.106.refs_22_.refs_18_), channel_id=1, source_target_pairs={{0,8},{24,16},{8,0},{16,24},{1,9},{25,17},{9,1},{17,25},{2,10},{26... | collective-permute-start | bytes 3538952 | tf_op jit(solution)/shard_map/ppermute | solution.py:482
  421.5 12.2 %slot.36 = (bf16[2,1152,256]{2,1,0:T(8,128)(2,1)}, bf16[2,1152,256]{2,1,0:T(8,128)(2,1)}, bf16[2,3456,1280]{2,1,0:T(8,128)(2,1)}, f32[512,256]{1,0:T(8,128)}) custom-call(s32[2]{0:T(128)} %pad_add_fusion.flag, bf16[6912,1280]{1,0:T(8,128)(2,1)} %bitcast.209, bf16[2,1152,256]{2,1,0:T(8,128)(2,1)} %copy-done.21, ...), custom_call_target="tpu_custom_call", output_to_operand_aliasing={{2}: (25, {})} | custom-call | tf_op jit(solution)/shard_map/slot/pallas_call | solution.py:448
  439.7 12.0 %slot.37 = (bf16[2,1152,256]{2,1,0:T(8,128)(2,1)}, bf16[2,1152,256]{2,1,0:T(8,128)(2,1)}, bf16[2,3456,1280]{2,1,0:T(8,128)(2,1)}, f32[512,256]{1,0:T(8,128)}) custom-call(s32[2]{0:T(128)} %pad_add_fusion.flag, bf16[6912,1280]{1,0:T(8,128)(2,1)} %bitcast.213, bf16[2,1152,256]{2,1,0:T(8,128)(2,1)} %copy-done.17, ...), custom_call_target="tpu_custom_call", output_to_operand_aliasing={{2}: (25, {})} | custom-call | tf_op jit(solution)/shard_map/slot/pallas_call | solution.py:448
  451.7 10.2 %collective-permute-start.43 = (bf16[2,1152,256]{2,1,0:T(8,128)(2,1)}, bf16[2,1152,256]{2,1,0:T(8,128)(2,1)S(1)}, u32[]{:S(2)}, u32[]{:S(2)}) collective-permute-start(bf16[2,1152,256]{2,1,0:T(8,128)(2,1)} %get-tuple-element.113.refs_20_.refs_12_), channel_id=1, source_target_pairs={{0,8},{24,16},{8,0},{16,24},{1,9},{25,17},{9,1},{17,25},{2,10},{26... | collective-permute-start | bytes 3538952 | tf_op jit(solution)/shard_map/ppermute | solution.py:482
  472.9 11.8 %slot.38 = (bf16[2,1152,256]{2,1,0:T(8,128)(2,1)}, bf16[2,1152,256]{2,1,0:T(8,128)(2,1)}, bf16[2,3456,1280]{2,1,0:T(8,128)(2,1)}, f32[512,256]{1,0:T(8,128)}) custom-call(s32[2]{0:T(128)} %pad_add_fusion.flag, bf16[6912,1280]{1,0:T(8,128)(2,1)} %bitcast.217, bf16[2,1152,256]{2,1,0:T(8,128)(2,1)} %copy-done.18, ...), custom_call_target="tpu_custom_call", output_to_operand_aliasing={{2}: (23, {})} | custom-call | tf_op jit(solution)/shard_map/slot/pallas_call | solution.py:448
  491.2 11.8 %slot.39 = (bf16[2,1152,256]{2,1,0:T(8,128)(2,1)}, bf16[2,1152,256]{2,1,0:T(8,128)(2,1)}, bf16[2,3456,1280]{2,1,0:T(8,128)(2,1)}, f32[512,256]{1,0:T(8,128)}) custom-call(s32[2]{0:T(128)} %pad_add_fusion.flag, bf16[6912,1280]{1,0:T(8,128)(2,1)} %bitcast.219, bf16[2,1152,256]{2,1,0:T(8,128)(2,1)} %copy-done.19, ...), custom_call_target="tpu_custom_call", output_to_operand_aliasing={{2}: (23, {})} | custom-call | tf_op jit(solution)/shard_map/slot/pallas_call | solution.py:448
  504.7 10.4 %collective-permute-start.49 = (bf16[2,1152,256]{2,1,0:T(8,128)(2,1)}, bf16[2,1152,256]{2,1,0:T(8,128)(2,1)S(1)}, u32[]{:S(2)}, u32[]{:S(2)}) collective-permute-start(bf16[2,1152,256]{2,1,0:T(8,128)(2,1)} %get-tuple-element.122.refs_14_.refs_1_), channel_id=1, source_target_pairs={{0,8},{24,16},{8,0},{16,24},{1,9},{25,17},{9,1},{17,25},{2,10},{26... | collective-permute-start | bytes 3538952 | tf_op jit(solution)/shard_map/ppermute | solution.py:482
  516.1 10.1 %slot.40 = (bf16[1,1152,256]{2,1,0:T(8,128)(2,1)}, bf16[2,1152,256]{2,1,0:T(8,128)(2,1)}, bf16[2,3456,1280]{2,1,0:T(8,128)(2,1)}, f32[512,256]{1,0:T(8,128)}) custom-call(s32[2]{0:T(128)} %pad_add_fusion.flag, bf16[6912,1280]{1,0:T(8,128)(2,1)} %bitcast.221, bf16[2,1152,256]{2,1,0:T(8,128)(2,1)} %copy-done.18, ...), custom_call_target="tpu_custom_call", output_to_operand_aliasing={{2}: (17, {})} | custom-call | tf_op jit(solution)/shard_map/slot/pallas_call | solution.py:448
  526.2 10.8 %collective-permute-start.55 = (bf16[2,1152,256]{2,1,0:T(8,128)(2,1)}, bf16[2,1152,256]{2,1,0:T(8,128)(2,1)S(1)}, u32[]{:S(2)}, u32[]{:S(2)}) collective-permute-start(bf16[2,1152,256]{2,1,0:T(8,128)(2,1)} %get-tuple-element.130.refs_3_.refs_0_), channel_id=1, source_target_pairs={{0,8},{24,16},{8,0},{16,24},{1,9},{25,17},{9,1},{17,25},{2,10},{26... | collective-permute-start | bytes 3538952 | tf_op jit(solution)/shard_map/ppermute | solution.py:482
  538.0 10.4 %slot.41 = (bf16[1,1152,256]{2,1,0:T(8,128)(2,1)}, bf16[2,1152,256]{2,1,0:T(8,128)(2,1)}, bf16[2,3456,1280]{2,1,0:T(8,128)(2,1)}, f32[512,256]{1,0:T(8,128)}) custom-call(s32[2]{0:T(128)} %pad_add_fusion.flag, bf16[6912,1280]{1,0:T(8,128)(2,1)} %bitcast.222, bf16[2,1152,256]{2,1,0:T(8,128)(2,1)} %copy-done.19, ...), custom_call_target="tpu_custom_call", output_to_operand_aliasing={{2}: (17, {})} | custom-call | tf_op jit(solution)/shard_map/slot/pallas_call | solution.py:448
  548.4 10.5 %collective-permute-start.52 = (bf16[2,1152,256]{2,1,0:T(8,128)(2,1)}, bf16[2,1152,256]{2,1,0:T(8,128)(2,1)S(1)}, u32[]{:S(2)}, u32[]{:S(2)}) collective-permute-start(bf16[2,1152,256]{2,1,0:T(8,128)(2,1)} %get-tuple-element.128.refs_3_.refs_0_), channel_id=1, source_target_pairs={{0,8},{24,16},{8,0},{16,24},{1,9},{25,17},{9,1},{17,25},{2,10},{26... | collective-permute-start | bytes 3538952 | tf_op jit(solution)/shard_map/ppermute | solution.py:482
  577.2 8.8 %collective-permute-start.57 = (bf16[1,1152,256]{2,1,0:T(8,128)(2,1)}, bf16[1,1152,256]{2,1,0:T(8,128)(2,1)S(1)}, u32[]{:S(2)}, u32[]{:S(2)}) collective-permute-start(bf16[1,1152,256]{2,1,0:T(8,128)(2,1)} %get-tuple-element.134.refs_8_.refs_2_), channel_id=1, source_target_pairs={{0,8},{24,16},{8,0},{16,24},{1,9},{25,17},{9,1},{17,25},{2,10},{26... | collective-permute-start | bytes 1769480 | tf_op jit(solution)/shard_map/ppermute | solution.py:482
  (335 shorter events, 250.6 us)
Async XLA Ops:
  7.2 57.2 %all-gather.7.cloned.1.call-start = ((), (), s32[]{:S(2)}) async-start(), calls=%async_computation | async-start | bytes 8847360 | tf_op jit(solution)/shard_map/all_gather | solution.py:500
  7.9 121.3 %all-gather.9.cloned.1.call-start = ((), (), s32[]{:S(2)}) async-start(), calls=%async_computation.1 | async-start | bytes 8847360 | tf_op jit(solution)/shard_map/all_gather | solution.py:607
  8.0 43.1 %collective-permute-start = (bf16[128,6912]{1,0:T(8,128)(2,1)}, bf16[128,6912]{1,0:T(8,128)(2,1)S(1)}, u32[]{:S(2)}, u32[]{:S(2)}) collective-permute-start(bf16[128,6912]{1,0:T(8,128)(2,1)} %bitcast.323), channel_id=1, source_target_pairs={{0,8},{24,16},{1,9},{25,17},{2,10},{26,18},{3,11},{27,19},{4,12},{... | collective-permute-start | bytes 5308424 | tf_op jit(solution)/shard_map/ppermute | solution.py:480
  60.2 113.2 %all-gather.11.cloned.1.call-start = ((), (), s32[]{:S(2)}) async-start(), calls=%async_computation.2 | async-start | bytes 8847360 | tf_op jit(solution)/shard_map/all_gather | solution.py:607
  60.2 32.5 %collective-permute-start.2 = (bf16[2,1152,256]{2,1,0:T(8,128)(2,1)}, bf16[2,1152,256]{2,1,0:T(8,128)(2,1)S(1)}, u32[]{:S(2)}, u32[]{:S(2)}) collective-permute-start(bf16[2,1152,256]{2,1,0:T(8,128)(2,1)} %slot.23.refs_6_), channel_id=1, source_target_pairs={{0,8},{24,16},{8,0},{16,24},{1,9},{25,17},{9,1},{17,25},{2,10},{26... | collective-permute-start | bytes 3538952 | tf_op jit(solution)/shard_map/ppermute | solution.py:482
  63.6 34.1 %collective-permute-start.6 = (bf16[128,3456]{1,0:T(8,128)(2,1)}, bf16[128,3456]{1,0:T(8,128)(2,1)S(1)}, u32[]{:S(2)}, u32[]{:S(2)}) collective-permute-start(bf16[128,3456]{1,0:T(8,128)(2,1)} %constant_dynamic-slice_fusion.2), channel_id=1, source_target_pairs={{8,16},{16,8},{9,17},{17,9},{10,18},{18,10},{11,19},{19,11},{12,20... | collective-permute-start | bytes 2654216 | tf_op jit(solution)/shard_map/ppermute | solution.py:481
  138.6 33.2 %collective-permute-start.9 = (bf16[2,1280,256]{2,1,0:T(8,128)(2,1)}, bf16[2,1280,256]{2,1,0:T(8,128)(2,1)}, u32[]{:S(2)}, u32[]{:S(2)}) collective-permute-start(bf16[2,1280,256]{2,1,0:T(8,128)(2,1)} %get-tuple-element.74), channel_id=1, source_target_pairs={{0,8},{24,16},{8,0},{16,24},{1,9},{25,17},{9,1},{17,25},{2,10},{26... | collective-permute-start | bytes 3932168 | tf_op jit(solution)/shard_map/ppermute | solution.py:482
  140.3 33.0 %collective-permute-start.10 = (bf16[2,1280,256]{2,1,0:T(8,128)(2,1)}, bf16[2,1280,256]{2,1,0:T(8,128)(2,1)}, u32[]{:S(2)}, u32[]{:S(2)}) collective-permute-start(bf16[2,1280,256]{2,1,0:T(8,128)(2,1)} %get-tuple-element.75.refs_13_), channel_id=1, source_target_pairs={{8,16},{16,8},{9,17},{17,9},{10,18},{18,10},{11,19},{19,11},{12,20... | collective-permute-start | bytes 3932168 | tf_op jit(solution)/shard_map/ppermute | solution.py:481
  153.5 46.3 %collective-permute-start.18 = (bf16[2,1280,256]{2,1,0:T(8,128)(2,1)}, bf16[2,1280,256]{2,1,0:T(8,128)(2,1)S(1)}, u32[]{:S(2)}, u32[]{:S(2)}) collective-permute-start(bf16[2,1280,256]{2,1,0:T(8,128)(2,1)} %get-tuple-element.82), channel_id=1, source_target_pairs={{0,8},{24,16},{8,0},{16,24},{1,9},{25,17},{9,1},{17,25},{2,10},{26... | collective-permute-start | bytes 3932168 | tf_op jit(solution)/shard_map/ppermute | solution.py:482
  154.9 45.7 %collective-permute-start.19 = (bf16[2,1280,256]{2,1,0:T(8,128)(2,1)}, bf16[2,1280,256]{2,1,0:T(8,128)(2,1)}, u32[]{:S(2)}, u32[]{:S(2)}) collective-permute-start(bf16[2,1280,256]{2,1,0:T(8,128)(2,1)} %get-tuple-element.78.refs_23_), channel_id=1, source_target_pairs={{8,16},{16,8},{9,17},{17,9},{10,18},{18,10},{11,19},{19,11},{12,20... | collective-permute-start | bytes 3932168 | tf_op jit(solution)/shard_map/ppermute | solution.py:481
  184.5 40.6 %collective-permute-start.16 = (bf16[2,1280,256]{2,1,0:T(8,128)(2,1)}, bf16[2,1280,256]{2,1,0:T(8,128)(2,1)}, u32[]{:S(2)}, u32[]{:S(2)}) collective-permute-start(bf16[2,1280,256]{2,1,0:T(8,128)(2,1)} %get-tuple-element.80.refs_22_), channel_id=1, source_target_pairs={{8,16},{16,8},{9,17},{17,9},{10,18},{18,10},{11,19},{19,11},{12,20... | collective-permute-start | bytes 3932168 | tf_op jit(solution)/shard_map/ppermute | solution.py:481
  186.2 38.8 %collective-permute-start.14 = (bf16[2,1152,256]{2,1,0:T(8,128)(2,1)}, bf16[2,1152,256]{2,1,0:T(8,128)(2,1)S(1)}, u32[]{:S(2)}, u32[]{:S(2)}) collective-permute-start(bf16[2,1152,256]{2,1,0:T(8,128)(2,1)} %get-tuple-element.79.refs_21_), channel_id=1, source_target_pairs={{0,8},{24,16},{8,0},{16,24},{1,9},{25,17},{9,1},{17,25},{2,10},{26... | collective-permute-start | bytes 3538952 | tf_op jit(solution)/shard_map/ppermute | solution.py:482
  212.1 39.8 %collective-permute-start.25 = (bf16[2,1280,256]{2,1,0:T(8,128)(2,1)}, bf16[2,1280,256]{2,1,0:T(8,128)(2,1)}, u32[]{:S(2)}, u32[]{:S(2)}) collective-permute-start(bf16[2,1280,256]{2,1,0:T(8,128)(2,1)} %get-tuple-element.84.refs_25_), channel_id=1, source_target_pairs={{8,16},{16,8},{9,17},{17,9},{10,18},{18,10},{11,19},{19,11},{12,20... | collective-permute-start | bytes 3932168 | tf_op jit(solution)/shard_map/ppermute | solution.py:481
  214.0 37.9 %collective-permute-start.24 = (bf16[2,1152,256]{2,1,0:T(8,128)(2,1)}, bf16[2,1152,256]{2,1,0:T(8,128)(2,1)S(1)}, u32[]{:S(2)}, u32[]{:S(2)}) collective-permute-start(bf16[2,1152,256]{2,1,0:T(8,128)(2,1)} %get-tuple-element.87.refs_22_), channel_id=1, source_target_pairs={{0,8},{24,16},{8,0},{16,24},{1,9},{25,17},{9,1},{17,25},{2,10},{26... | collective-permute-start | bytes 3538952 | tf_op jit(solution)/shard_map/ppermute | solution.py:482
  237.2 41.3 %collective-permute-start.20 = (bf16[2,1280,256]{2,1,0:T(8,128)(2,1)}, bf16[2,1280,256]{2,1,0:T(8,128)(2,1)S(1)}, u32[]{:S(2)}, u32[]{:S(2)}) collective-permute-start(bf16[2,1280,256]{2,1,0:T(8,128)(2,1)} %get-tuple-element.85.refs_23_.refs_20_), channel_id=1, source_target_pairs={{0,8},{24,16},{8,0},{16,24},{1,9},{25,17},{9,1},{17,25},{2,10},{26... | collective-permute-start | bytes 3932168 | tf_op jit(solution)/shard_map/ppermute | solution.py:482
  241.8 37.3 %collective-permute-start.22 = (bf16[2,1280,256]{2,1,0:T(8,128)(2,1)}, bf16[2,1280,256]{2,1,0:T(8,128)(2,1)}, u32[]{:S(2)}, u32[]{:S(2)}) collective-permute-start(bf16[2,1280,256]{2,1,0:T(8,128)(2,1)} %get-tuple-element.86.refs_24_), channel_id=1, source_target_pairs={{8,16},{16,8},{9,17},{17,9},{10,18},{18,10},{11,19},{19,11},{12,20... | collective-permute-start | bytes 3932168 | tf_op jit(solution)/shard_map/ppermute | solution.py:481
  264.3 46.5 %collective-permute-start.30 = (bf16[2,1280,256]{2,1,0:T(8,128)(2,1)}, bf16[2,1280,256]{2,1,0:T(8,128)(2,1)}, u32[]{:S(2)}, u32[]{:S(2)}) collective-permute-start(bf16[2,1280,256]{2,1,0:T(8,128)(2,1)} %get-tuple-element.89.refs_27_), channel_id=1, source_target_pairs={{8,16},{16,8},{9,17},{17,9},{10,18},{18,10},{11,19},{19,11},{12,20... | collective-permute-start | bytes 3932168 | tf_op jit(solution)/shard_map/ppermute | solution.py:481
  267.6 43.2 %collective-permute-start.29 = (bf16[2,1152,256]{2,1,0:T(8,128)(2,1)}, bf16[2,1152,256]{2,1,0:T(8,128)(2,1)S(1)}, u32[]{:S(2)}, u32[]{:S(2)}) collective-permute-start(bf16[2,1152,256]{2,1,0:T(8,128)(2,1)} %get-tuple-element.92.refs_24_.refs_21_), channel_id=1, source_target_pairs={{0,8},{24,16},{8,0},{16,24},{1,9},{25,17},{9,1},{17,25},{2,10},{26... | collective-permute-start | bytes 3538952 | tf_op jit(solution)/shard_map/ppermute | solution.py:482
  291.9 37.9 %collective-permute-start.27 = (bf16[2,1280,256]{2,1,0:T(8,128)(2,1)}, bf16[2,1280,256]{2,1,0:T(8,128)(2,1)}, u32[]{:S(2)}, u32[]{:S(2)}) collective-permute-start(bf16[2,1280,256]{2,1,0:T(8,128)(2,1)} %get-tuple-element.91.refs_30_), channel_id=1, source_target_pairs={{8,16},{16,8},{9,17},{17,9},{10,18},{18,10},{11,19},{19,11},{12,20... | collective-permute-start | bytes 3932168 | tf_op jit(solution)/shard_map/ppermute | solution.py:481
  293.6 36.2 %collective-permute-start.26 = (bf16[2,1152,256]{2,1,0:T(8,128)(2,1)}, bf16[2,1152,256]{2,1,0:T(8,128)(2,1)}, u32[]{:S(2)}, u32[]{:S(2)}) collective-permute-start(bf16[2,1152,256]{2,1,0:T(8,128)(2,1)} %get-tuple-element.90.refs_22_.refs_20_), channel_id=1, source_target_pairs={{0,8},{24,16},{8,0},{16,24},{1,9},{25,17},{9,1},{17,25},{2,10},{26... | collective-permute-start | bytes 3538952 | tf_op jit(solution)/shard_map/ppermute | solution.py:482
  324.4 39.5 %collective-permute-start.35 = (bf16[2,1280,256]{2,1,0:T(8,128)(2,1)}, bf16[2,1280,256]{2,1,0:T(8,128)(2,1)S(1)}, u32[]{:S(2)}, u32[]{:S(2)}) collective-permute-start(bf16[2,1280,256]{2,1,0:T(8,128)(2,1)} %get-tuple-element.101.refs_23_.refs_20_), channel_id=1, source_target_pairs={{0,8},{24,16},{8,0},{16,24},{1,9},{25,17},{9,1},{17,25},{2,10},{26... | collective-permute-start | bytes 3932168 | tf_op jit(solution)/shard_map/ppermute | solution.py:482
  327.6 37.0 %collective-permute-start.36 = (bf16[2,1280,256]{2,1,0:T(8,128)(2,1)}, bf16[2,1280,256]{2,1,0:T(8,128)(2,1)S(1)}, u32[]{:S(2)}, u32[]{:S(2)}) collective-permute-start(bf16[2,1280,256]{2,1,0:T(8,128)(2,1)} %get-tuple-element.98.refs_28_), channel_id=1, source_target_pairs={{8,16},{16,8},{9,17},{17,9},{10,18},{18,10},{11,19},{19,11},{12,20... | collective-permute-start | bytes 3932168 | tf_op jit(solution)/shard_map/ppermute | solution.py:481
  342.1 45.6 %collective-permute-start.32 = (bf16[2,1152,256]{2,1,0:T(8,128)(2,1)}, bf16[2,1152,256]{2,1,0:T(8,128)(2,1)}, u32[]{:S(2)}, u32[]{:S(2)}) collective-permute-start(bf16[2,1152,256]{2,1,0:T(8,128)(2,1)} %get-tuple-element.99.refs_22_.refs_20_), channel_id=1, source_target_pairs={{0,8},{24,16},{8,0},{16,24},{1,9},{25,17},{9,1},{17,25},{2,10},{26... | collective-permute-start | bytes 3538952 | tf_op jit(solution)/shard_map/ppermute | solution.py:482
  378.0 42.4 %collective-permute-start.42 = (bf16[2,1280,256]{2,1,0:T(8,128)(2,1)}, bf16[2,1280,256]{2,1,0:T(8,128)(2,1)}, u32[]{:S(2)}, u32[]{:S(2)}) collective-permute-start(bf16[2,1280,256]{2,1,0:T(8,128)(2,1)} %get-tuple-element.105.refs_28_), channel_id=1, source_target_pairs={{8,16},{16,8},{9,17},{17,9},{10,18},{18,10},{11,19},{19,11},{12,20... | collective-permute-start | bytes 3932168 | tf_op jit(solution)/shard_map/ppermute | solution.py:481
  379.7 40.6 %collective-permute-start.41 = (bf16[2,1152,256]{2,1,0:T(8,128)(2,1)}, bf16[2,1152,256]{2,1,0:T(8,128)(2,1)S(1)}, u32[]{:S(2)}, u32[]{:S(2)}) collective-permute-start(bf16[2,1152,256]{2,1,0:T(8,128)(2,1)} %get-tuple-element.108.refs_22_.refs_18_), channel_id=1, source_target_pairs={{0,8},{24,16},{8,0},{16,24},{1,9},{25,17},{9,1},{17,25},{2,10},{26... | collective-permute-start | bytes 3538952 | tf_op jit(solution)/shard_map/ppermute | solution.py:482
  399.9 38.6 %collective-permute-start.37 = (bf16[2,1152,256]{2,1,0:T(8,128)(2,1)}, bf16[2,1152,256]{2,1,0:T(8,128)(2,1)S(1)}, u32[]{:S(2)}, u32[]{:S(2)}) collective-permute-start(bf16[2,1152,256]{2,1,0:T(8,128)(2,1)} %get-tuple-element.106.refs_22_.refs_18_), channel_id=1, source_target_pairs={{0,8},{24,16},{8,0},{16,24},{1,9},{25,17},{9,1},{17,25},{2,10},{26... | collective-permute-start | bytes 3538952 | tf_op jit(solution)/shard_map/ppermute | solution.py:482
  433.7 38.2 %collective-permute-start.46 = (bf16[2,1152,256]{2,1,0:T(8,128)(2,1)}, bf16[2,1152,256]{2,1,0:T(8,128)(2,1)S(1)}, u32[]{:S(2)}, u32[]{:S(2)}) collective-permute-start(bf16[2,1152,256]{2,1,0:T(8,128)(2,1)} %get-tuple-element.115.refs_20_.refs_12_), channel_id=1, source_target_pairs={{0,8},{24,16},{8,0},{16,24},{1,9},{25,17},{9,1},{17,25},{2,10},{26... | collective-permute-start | bytes 3538952 | tf_op jit(solution)/shard_map/ppermute | solution.py:482
  436.8 35.2 %collective-permute-start.47 = (bf16[2,1152,256]{2,1,0:T(8,128)(2,1)}, bf16[2,1152,256]{2,1,0:T(8,128)(2,1)}, u32[]{:S(2)}, u32[]{:S(2)}) collective-permute-start(bf16[2,1152,256]{2,1,0:T(8,128)(2,1)} %get-tuple-element.112.refs_27_), channel_id=1, source_target_pairs={{8,16},{16,8},{9,17},{17,9},{10,18},{18,10},{11,19},{19,11},{12,20... | collective-permute-start | bytes 3538952 | tf_op jit(solution)/shard_map/ppermute | solution.py:481
  451.7 38.4 %collective-permute-start.43 = (bf16[2,1152,256]{2,1,0:T(8,128)(2,1)}, bf16[2,1152,256]{2,1,0:T(8,128)(2,1)S(1)}, u32[]{:S(2)}, u32[]{:S(2)}) collective-permute-start(bf16[2,1152,256]{2,1,0:T(8,128)(2,1)} %get-tuple-element.113.refs_20_.refs_12_), channel_id=1, source_target_pairs={{0,8},{24,16},{8,0},{16,24},{1,9},{25,17},{9,1},{17,25},{2,10},{26... | collective-permute-start | bytes 3538952 | tf_op jit(solution)/shard_map/ppermute | solution.py:482
  502.9 34.0 %collective-permute-start.48 = (bf16[2,1152,256]{2,1,0:T(8,128)(2,1)}, bf16[2,1152,256]{2,1,0:T(8,128)(2,1)}, u32[]{:S(2)}, u32[]{:S(2)}) collective-permute-start(bf16[2,1152,256]{2,1,0:T(8,128)(2,1)} %get-tuple-element.121.refs_19_), channel_id=1, source_target_pairs={{8,16},{16,8},{9,17},{17,9},{10,18},{18,10},{11,19},{19,11},{12,20... | collective-permute-start | bytes 3538952 | tf_op jit(solution)/shard_map/ppermute | solution.py:481
  526.2 42.6 %collective-permute-start.55 = (bf16[2,1152,256]{2,1,0:T(8,128)(2,1)}, bf16[2,1152,256]{2,1,0:T(8,128)(2,1)S(1)}, u32[]{:S(2)}, u32[]{:S(2)}) collective-permute-start(bf16[2,1152,256]{2,1,0:T(8,128)(2,1)} %get-tuple-element.130.refs_3_.refs_0_), channel_id=1, source_target_pairs={{0,8},{24,16},{8,0},{16,24},{1,9},{25,17},{9,1},{17,25},{2,10},{26... | collective-permute-start | bytes 3538952 | tf_op jit(solution)/shard_map/ppermute | solution.py:482
  548.4 38.3 %collective-permute-start.52 = (bf16[2,1152,256]{2,1,0:T(8,128)(2,1)}, bf16[2,1152,256]{2,1,0:T(8,128)(2,1)S(1)}, u32[]{:S(2)}, u32[]{:S(2)}) collective-permute-start(bf16[2,1152,256]{2,1,0:T(8,128)(2,1)} %get-tuple-element.128.refs_3_.refs_0_), channel_id=1, source_target_pairs={{0,8},{24,16},{8,0},{16,24},{1,9},{25,17},{9,1},{17,25},{2,10},{26... | collective-permute-start | bytes 3538952 | tf_op jit(solution)/shard_map/ppermute | solution.py:482
  (93 other events, 953.2 us)
Sparse Core Ops, SparseCore 0:
  9.6 53.5 all-gather.6
  64.7 50.8 all-gather.8
  117.7 50.8 all-gather.10

commit v4 on v3

--- a/solution.py
+++ b/solution.py
@@ -52,20 +52,21 @@
     def body(lhs_ref, *rest):
         mats, (out_ref, acc_ref) = rest[:groups], rest[-2:]
         step = pl.program_id(0)
-        for g in range(groups):
-            part = jnp.dot(lhs_ref[...], mats[g][...], preferred_element_type=F32)
-
-            @pl.when(step == 0)
-            def _():
-                acc_ref[g] = part
-
-            @pl.when(step > 0)
-            def _():
-                acc_ref[g] += part
+        wide = jnp.concatenate([mat[...] for mat in mats], axis=1) if groups > 1 else mats[0][...]
+        part = jnp.dot(lhs_ref[...], wide, preferred_element_type=F32)
+
+        @pl.when(step == 0)
+        def _():
+            acc_ref[...] = part
+
+        @pl.when(step > 0)
+        def _():
+            acc_ref[...] += part
 
         @pl.when(step == steps - 1)
         def _():
-            out_ref[...] = acc_ref[...].astype(BF16)
+            for g in range(groups):
+                out_ref[g] = acc_ref[:, g * WIDTH : (g + 1) * WIDTH].astype(BF16)
 
     return pl.pallas_call(
         body,
@@ -75,7 +76,7 @@
         + [pl.BlockSpec((depth, WIDTH), lambda k, g=g: (k, group + g)) for g in range(groups)]
         + [ANY] * len(deps),
         out_specs=pl.BlockSpec((groups, tokens, WIDTH), lambda k: (0, 0, 0)),
-        scratch_shapes=[pltpu.VMEM((groups, tokens, WIDTH), F32)],
+        scratch_shapes=[pltpu.VMEM((tokens, groups * WIDTH), F32)],
         compiler_params=pltpu.CompilerParams(vmem_limit_bytes=VMEM_LIMIT),
         cost_estimate=COST,
         name="group_product",
@@ -603,7 +604,12 @@
         start_pass(-2, slot_call(plan, flags, last, send=inward(0), deps=[near[-1], cross[0]]))
     lead = batches[0]
     outer_cuts = [cut(plan, [task], list(sent_pass.values())) for task in near[1:]]
-    product = group_product(full_acts, weight, 0, 1, deps=[x[0] for x in outer_cuts])
+    rest = list(batches[1:])
+    first_of = lambda b: min(i for i, p in enumerate(plan.pieces) if p.group == b.first)
+    fused = last == 1 and plan.unit % 128 == 0 and plan.rows % (AHEAD**2 * 128) == 0
+    fused = fused and all(first_of(b) >= AHEAD * (i + 1) for i, b in enumerate(rest))
+    early = 1 + (min(LAG, len(rest)) if fused else len(rest))
+    products = group_product(full_acts, weight, 0, early, deps=[x[0] for x in outer_cuts])
     gather_col = lambda x: lax.all_gather(x, "col", axis=0)
     outer_parts = [[gather_col(x) for x in task] for task in outer_cuts]
 
@@ -617,7 +623,7 @@
         b.oth = [gather_rows(crossed[:, g]) for g in range(b.groups)]
         return crossed
 
-    lead_far = at_once(lead, product)
+    lead_far = at_once(lead, products[:1])
     own_square = squares(full_acts, [lead.near[0]])
     carries, crossings, starts = {}, {}, {}
 
@@ -631,15 +637,9 @@
         start_pass(-1, slot_call(plan, flags, last, send=inward(1), deps=[own_square, lead.outer[0]] + list(came_pass.values())))
     other_cuts = cut(plan, cross, [own_square] + list(sent_pass.values())[-1:])
     other_parts = [gather_col(x) for x in other_cuts]
-    early = min(LAG, plan.groups - 1) if last == 1 else plan.groups - 1
-    deps = [other_cuts[0], lead.outer[0]] + list(sent_pass.values())[-1:]
-    next_products = group_product(full_acts, weight, 1, early, deps=deps)
-    fused = last == 1 and plan.unit % 128 == 0 and plan.rows % (AHEAD**2 * 128) == 0
-    first_of = lambda b: min(i for i, p in enumerate(plan.pieces) if p.group == b.first)
-    rest = list(batches[1:])
-    if fused and all(first_of(b) >= AHEAD * (i + 1) for i, b in enumerate(rest)):
+    if fused:
         for slot, b in enumerate(rest[:LAG]):
-            b.start(next_products[slot : slot + 1])
+            b.start(products[1 + slot : 2 + slot])
             ship(slot, b)
         turn = 0
         for b in rest[LAG:]:
@@ -651,7 +651,7 @@
             ship(slot, b)
     else:
         for i, b in enumerate(rest):
-            at_once(b, next_products[i : i + 1])
+            at_once(b, products[1 + i : 2 + i])
     if last > 1:
         for index in range(min(LAG, count)):
             start_pass(index - LAG, slot_call(plan, flags, last, send=inward(index)))
@@ -659,7 +659,7 @@
     came_mid, backs = {}, {}
     buffer = None
     results = []
-    chain = [next_products, lead_far]
+    chain = [other_cuts[0], lead_far]
     ahead_total, result_total = None, None
     for slot in range(count + 3 * LAG):
         deps = list(chain)
@@ -683,10 +683,6 @@
             stage["fold"] = (piece, weight, came_pass[slot - LAG], side_of(piece))
         if now(slot + LAG):
             stage["send"] = inward(slot + LAG)
-        if slot < max(carries, default=0):
-            stage.setdefault("cross", packed(lead.near[0][0]))
-            if slot == 0:
-                stage.setdefault("carry", lead.inwards(0))
         index = slot - LAG
         if now(index):
             piece = plan.pieces[index]

time: 641 us -> 639 us (level)
  waiting for transfers between devices: 109 us -> 150 us
  starting transfers between devices: 192 us -> 157 us
  Pallas kernels: 263 us -> 255 us
    ppermute x22, waiting for transfers between devices: 28.1 us -> 62.6 us  [local(): lax.ppermute(x, 'task', step_in(last - 1) + step_out(last - 1))]
    ppermute x22, starting transfers between devices: 128 us -> 106 us  [local(): lax.ppermute(x, 'task', step_in(last - 1) + step_out(last - 1))]
    ppermute x20, starting transfers between devices: 28.9 us -> 16.7 us  [local(): lax.ppermute(x, 'row', [(i, (i + s) % rows_n) for i in range(rows_n)])]
    pallas_call x2 -> x1, Pallas kernels: 20.7 us -> 12.4 us  [group_product(): pl.pallas_call(body, grid=(steps,), out_shape=jax.ShapeDtypeStruct((group...]
  transfers between devices with their start and end apart: 66 -> 66, of which waited for: 23 -> 29; matrix products, arithmetic and copies ran while one was open for 4% -> 4% of each run, Pallas kernels for 42% -> 41%
where the time goes in v4:
time: 639 us; the launch traced here: 628 us
  Pallas kernels  255 us (40%)
  starting transfers between devices  157 us (25%)
  waiting for transfers between devices  150 us (23%)
  local copies, waits for them, and re-layouts  41.3 us (6%)
  between operations  15.3 us (2%)
  other arithmetic  9.01 us (1%)
    pallas_call x23, Pallas kernels, slot_call(): pl.pallas_call(body, grid_spec=pltpu.PrefetchScalarGridSpec(num_scalar_pr...  225 us
    ppermute x22, starting transfers between devices, local(): lax.ppermute(x, 'task', step_in(last - 1) + step_out(last - 1))  106 us
    ppermute x22, waiting for transfers between devices, local(): lax.ppermute(x, 'task', step_in(last - 1) + step_out(last - 1))  62.6 us
    ppermute x20, waiting for transfers between devices, local(): lax.ppermute(x, 'row', [(i, (i + s) % rows_n) for i in range(rows_n)])  52 us
    ppermute x1, waiting for transfers between devices, local(): send_in = lambda x: lax.ppermute(x, 'task', all_in)  34.6 us
    ppermute x20, starting transfers between devices, local(): lax.ppermute(x, 'task', [(last, side_n), (side_n, last)])  29.6 us
    unnamed x119, local copies, waits for them, and re-layouts  23.3 us
    ppermute x20, starting transfers between devices, local(): lax.ppermute(x, 'row', [(i, (i + s) % rows_n) for i in range(rows_n)])  16.7 us
  transfers between devices with their start and end apart: 66, of which 29 were waited for; matrix products, arithmetic and copies ran while one was open for 4% of the time, Pallas kernels for 41%

profile of v4, /device:TPU:0, one launch (start us, length us, event | category | flops | bytes accessed | tf_op | source)
XLA Modules:
  0.0 628.4 jit_solution(7239811909936094356)
XLA Ops:
  16.5 34.6 %collective-permute-done.refs_0_ = bf16[128,6912]{1,0:T(8,128)(2,1)S(1)} collective-permute-done((bf16[128,6912]{1,0:T(8,128)(2,1)}, bf16[128,6912]{1,0:T(8,128)(2,1)S(1)}, u32[]{:S(2)}, u32[]{:S(2)}) %collective-permute-start) | collective-permute-done | bytes 1769504 | tf_op jit(solution)/shard_map/ppermute | solution.py:481
  64.9 12.4 %group_product.1 = bf16[3,512,256]{2,1,0:T(8,128)(2,1)} custom-call(bf16[512,6912]{1,0:T(8,128)(2,1)} %bitcast.222, bf16[6912,1280]{1,0:T(8,128)(2,1)} %bitcast.155, bf16[6912,1280]{1,0:T(8,128)(2,1)} %bitcast.156, bf16[6912,1280]{1,0:T(8,128)(2,1)} %bitcast.157, bf16[2,3456,128]{2,1,0:T(8,128)(2,1)} %cut.2.rest_3_), custom_call_target="tpu_custom_call" | custom-call | tf_op jit(solution)/shard_map/group_product/pallas_call | solution.py:71
  93.1 10.2 %squares.1.refs_2_.refs_6_.refs_8_ = bf16[6912,512]{1,0:T(8,128)(2,1)} custom-call(bf16[512,6912]{1,0:T(8,128)(2,1)} %bitcast.223, bf16[1,256,256]{2,1,0:T(8,128)(2,1)} %copy-done.39), custom_call_target="tpu_custom_call" | custom-call | tf_op jit(solution)/shard_map/squares/pallas_call | solution.py:94
  124.5 9.1 %slot.25 = (bf16[2,1280,256]{2,1,0:T(8,128)(2,1)}, bf16[2,1280,256]{2,1,0:T(8,128)(2,1)}, f32[512,256]{1,0:T(8,128)}) custom-call(s32[2]{0:T(128)} %pad_add_fusion.flag, bf16[6912,1280]{1,0:T(8,128)(2,1)} %bitcast.160, bf16[2,1152,256]{2,1,0:T(8,128)(2,1)} %copy-done.22, bf16[6912,512]{1,0:T(8,128)(2,1)} %squares.1.refs_2_.refs_6_.refs_8_, ...), custom_call_target="tpu_custom_call" | custom-call | tf_op jit(solution)/shard_map/slot/pallas_call | solution.py:449
  144.4 8.8 %slot.26 = (bf16[2,1280,256]{2,1,0:T(8,128)(2,1)}, bf16[2,1280,256]{2,1,0:T(8,128)(2,1)}, f32[512,256]{1,0:T(8,128)}) custom-call(s32[2]{0:T(128)} %pad_add_fusion.flag, bf16[6912,1280]{1,0:T(8,128)(2,1)} %bitcast.167, bf16[2,1152,256]{2,1,0:T(8,128)(2,1)} %copy-done.29, bf16[6912,512]{1,0:T(8,128)(2,1)} %squares.1.refs_2_.refs_6_.refs_8_, ...), custom_call_target="tpu_custom_call" | custom-call | tf_op jit(solution)/shard_map/slot/pallas_call | solution.py:449
  160.3 11.3 %collective-permute-done.9.refs_1_.refs_7_ = bf16[2,1280,256]{2,1,0:T(8,128)(2,1)} collective-permute-done((bf16[2,1280,256]{2,1,0:T(8,128)(2,1)}, bf16[2,1280,256]{2,1,0:T(8,128)(2,1)}, u32[]{:S(2)}, u32[]{:S(2)}) %collective-permute-start.9) | collective-permute-done | bytes 1310752 | tf_op jit(solution)/shard_map/ppermute | solution.py:483
  173.2 11.1 %slot.27 = (bf16[2,1280,256]{2,1,0:T(8,128)(2,1)}, bf16[2,1152,256]{2,1,0:T(8,128)(2,1)}, f32[512,256]{1,0:T(8,128)}) custom-call(s32[2]{0:T(128)} %pad_add_fusion.flag, bf16[6912,1280]{1,0:T(8,128)(2,1)} %bitcast.168, bf16[2,1280,256]{2,1,0:T(8,128)(2,1)} %collective-permute-done.9.refs_1_.refs_7_, bf16[6912,512]{1,0:T(8,128)(2,1)} %squares.1.refs_2_.refs_6_.refs_8_, ...), custom_call_target="tpu_custom_call" | custom-call | tf_op jit(solution)/shard_map/slot/pallas_call | solution.py:449
  188.6 11.0 %collective-permute-done.18.refs_1_.refs_7_ = bf16[2,1280,256]{2,1,0:T(8,128)(2,1)S(1)} collective-permute-done((bf16[2,1280,256]{2,1,0:T(8,128)(2,1)}, bf16[2,1280,256]{2,1,0:T(8,128)(2,1)S(1)}, u32[]{:S(2)}, u32[]{:S(2)}) %collective-permute-start.18) | collective-permute-done | bytes 1310752 | tf_op jit(solution)/shard_map/ppermute | solution.py:483
  201.2 10.8 %slot.28 = (bf16[2,1280,256]{2,1,0:T(8,128)(2,1)}, bf16[2,1152,256]{2,1,0:T(8,128)(2,1)}, f32[512,256]{1,0:T(8,128)}) custom-call(s32[2]{0:T(128)} %pad_add_fusion.flag, bf16[6912,1280]{1,0:T(8,128)(2,1)} %bitcast.173, bf16[2,1280,256]{2,1,0:T(8,128)(2,1)} %copy-done.27, bf16[6912,512]{1,0:T(8,128)(2,1)} %squares.1.refs_2_.refs_6_.refs_8_, ...), custom_call_target="tpu_custom_call" | custom-call | tf_op jit(solution)/shard_map/slot/pallas_call | solution.py:449
  225.9 11.2 %slot.29 = (bf16[2,1280,256]{2,1,0:T(8,128)(2,1)}, bf16[2,1280,256]{2,1,0:T(8,128)(2,1)}, f32[512,256]{1,0:T(8,128)}) custom-call(s32[2]{0:T(128)} %pad_add_fusion.flag, bf16[6912,1280]{1,0:T(8,128)(2,1)} %bitcast.178, bf16[2,1152,256]{2,1,0:T(8,128)(2,1)} %copy-done.23, bf16[6912,512]{1,0:T(8,128)(2,1)} %squares.1.refs_2_.refs_6_.refs_8_, ...), custom_call_target="tpu_custom_call" | custom-call | tf_op jit(solution)/shard_map/slot/pallas_call | solution.py:449
  251.2 10.8 %slot.30 = (bf16[2,1152,256]{2,1,0:T(8,128)(2,1)}, bf16[2,1152,256]{2,1,0:T(8,128)(2,1)}, f32[512,256]{1,0:T(8,128)}) custom-call(s32[2]{0:T(128)} %pad_add_fusion.flag, bf16[6912,1280]{1,0:T(8,128)(2,1)} %bitcast.187, bf16[2,1152,256]{2,1,0:T(8,128)(2,1)} %copy-done.24, bf16[6912,512]{1,0:T(8,128)(2,1)} %squares.1.refs_2_.refs_6_.refs_8_, ...), custom_call_target="tpu_custom_call" | custom-call | tf_op jit(solution)/shard_map/slot/pallas_call | solution.py:449
  268.3 9.9 %collective-permute-done.20.refs_1_.refs_24_.refs_7_.refs_21_ = bf16[2,1280,256]{2,1,0:T(8,128)(2,1)S(1)} collective-permute-done((bf16[2,1280,256]{2,1,0:T(8,128)(2,1)}, bf16[2,1280,256]{2,1,0:T(8,128)(2,1)S(1)}, u32[]{:S(2)}, u32[]{:S(2)}) %collective-permute-start.20) | collective-permute-done | bytes 1310752 | tf_op jit(solution)/shard_map/ppermute | solution.py:483
  279.3 12.3 %slot.31 = (bf16[2,1280,256]{2,1,0:T(8,128)(2,1)}, bf16[2,1152,256]{2,1,0:T(8,128)(2,1)}, bf16[2,3456,1280]{2,1,0:T(8,128)(2,1)}, f32[512,256]{1,0:T(8,128)}) custom-call(s32[2]{0:T(128)} %pad_add_fusion.flag, bf16[6912,1280]{1,0:T(8,128)(2,1)} %bitcast.188, bf16[2,1280,256]{2,1,0:T(8,128)(2,1)} %copy-done.15, ...), custom_call_target="tpu_custom_call" | custom-call | tf_op jit(solution)/shard_map/slot/pallas_call | solution.py:449
  306.6 12.5 %slot.32 = (bf16[2,1280,256]{2,1,0:T(8,128)(2,1)}, bf16[2,1280,256]{2,1,0:T(8,128)(2,1)}, bf16[2,3456,1280]{2,1,0:T(8,128)(2,1)}, f32[512,256]{1,0:T(8,128)}) custom-call(s32[2]{0:T(128)} %pad_add_fusion.flag, bf16[6912,1280]{1,0:T(8,128)(2,1)} %bitcast.192, bf16[2,1152,256]{2,1,0:T(8,128)(2,1)} %copy-done.20, ...), custom_call_target="tpu_custom_call", output_to_operand_aliasing={{2}: (27, {})} | custom-call | tf_op jit(solution)/shard_map/slot/pallas_call | solution.py:449
  328.9 12.3 %slot.33 = (bf16[2,1152,256]{2,1,0:T(8,128)(2,1)}, bf16[2,1152,256]{2,1,0:T(8,128)(2,1)}, bf16[2,3456,1280]{2,1,0:T(8,128)(2,1)}, f32[512,256]{1,0:T(8,128)}) custom-call(s32[2]{0:T(128)} %pad_add_fusion.flag, bf16[6912,1280]{1,0:T(8,128)(2,1)} %bitcast.196, ...), custom_call_target="tpu_custom_call", output_to_operand_aliasing={{2}: (25, {})} | custom-call | tf_op jit(solution)/shard_map/slot/pallas_call | solution.py:449
  341.3 8.2 %collective-permute-start.32 = (bf16[2,1152,256]{2,1,0:T(8,128)(2,1)}, bf16[2,1152,256]{2,1,0:T(8,128)(2,1)}, u32[]{:S(2)}, u32[]{:S(2)}) collective-permute-start(bf16[2,1152,256]{2,1,0:T(8,128)(2,1)} %get-tuple-element.99.refs_22_.refs_20_), channel_id=1, source_target_pairs={{0,8},{24,16},{8,0},{16,24},{1,9},{25,17},{9,1},{17,25},{2,10},{26... | collective-permute-start | bytes 3538952 | tf_op jit(solution)/shard_map/ppermute | solution.py:483
  359.7 12.3 %slot.34 = (bf16[2,1280,256]{2,1,0:T(8,128)(2,1)}, bf16[2,1152,256]{2,1,0:T(8,128)(2,1)}, bf16[2,3456,1280]{2,1,0:T(8,128)(2,1)}, f32[512,256]{1,0:T(8,128)}) custom-call(s32[2]{0:T(128)} %pad_add_fusion.flag, bf16[6912,1280]{1,0:T(8,128)(2,1)} %bitcast.203, bf16[2,1280,256]{2,1,0:T(8,128)(2,1)} %copy-done.16, ...), custom_call_target="tpu_custom_call", output_to_operand_aliasing={{2}: (26, {})} | custom-call | tf_op jit(solution)/shard_map/slot/pallas_call | solution.py:449
  373.7 6.9 %collective-permute-start.41 = (bf16[2,1152,256]{2,1,0:T(8,128)(2,1)}, bf16[2,1152,256]{2,1,0:T(8,128)(2,1)S(1)}, u32[]{:S(2)}, u32[]{:S(2)}) collective-permute-start(bf16[2,1152,256]{2,1,0:T(8,128)(2,1)} %get-tuple-element.108.refs_22_.refs_18_), channel_id=1, source_target_pairs={{0,8},{24,16},{8,0},{16,24},{1,9},{25,17},{9,1},{17,25},{2,10},{26... | collective-permute-start | bytes 3538952 | tf_op jit(solution)/shard_map/ppermute | solution.py:483
  382.3 12.1 %slot.35 = (bf16[2,1152,256]{2,1,0:T(8,128)(2,1)}, bf16[2,1152,256]{2,1,0:T(8,128)(2,1)}, bf16[2,3456,1280]{2,1,0:T(8,128)(2,1)}, f32[512,256]{1,0:T(8,128)}) custom-call(s32[2]{0:T(128)} %pad_add_fusion.flag, bf16[6912,1280]{1,0:T(8,128)(2,1)} %bitcast.204, ...), custom_call_target="tpu_custom_call", output_to_operand_aliasing={{2}: (25, {})} | custom-call | tf_op jit(solution)/shard_map/slot/pallas_call | solution.py:449
  394.5 8.3 %collective-permute-start.37 = (bf16[2,1152,256]{2,1,0:T(8,128)(2,1)}, bf16[2,1152,256]{2,1,0:T(8,128)(2,1)S(1)}, u32[]{:S(2)}, u32[]{:S(2)}) collective-permute-start(bf16[2,1152,256]{2,1,0:T(8,128)(2,1)} %get-tuple-element.106.refs_22_.refs_18_), channel_id=1, source_target_pairs={{0,8},{24,16},{8,0},{16,24},{1,9},{25,17},{9,1},{17,25},{2,10},{26... | collective-permute-start | bytes 3538952 | tf_op jit(solution)/shard_map/ppermute | solution.py:483
  414.1 12.2 %slot.36 = (bf16[2,1152,256]{2,1,0:T(8,128)(2,1)}, bf16[2,1152,256]{2,1,0:T(8,128)(2,1)}, bf16[2,3456,1280]{2,1,0:T(8,128)(2,1)}, f32[512,256]{1,0:T(8,128)}) custom-call(s32[2]{0:T(128)} %pad_add_fusion.flag, bf16[6912,1280]{1,0:T(8,128)(2,1)} %bitcast.208, bf16[2,1152,256]{2,1,0:T(8,128)(2,1)} %copy-done.21, ...), custom_call_target="tpu_custom_call", output_to_operand_aliasing={{2}: (25, {})} | custom-call | tf_op jit(solution)/shard_map/slot/pallas_call | solution.py:449
  434.0 12.0 %slot.37 = (bf16[2,1152,256]{2,1,0:T(8,128)(2,1)}, bf16[2,1152,256]{2,1,0:T(8,128)(2,1)}, bf16[2,3456,1280]{2,1,0:T(8,128)(2,1)}, f32[512,256]{1,0:T(8,128)}) custom-call(s32[2]{0:T(128)} %pad_add_fusion.flag, bf16[6912,1280]{1,0:T(8,128)(2,1)} %bitcast.212, bf16[2,1152,256]{2,1,0:T(8,128)(2,1)} %copy-done.17, ...), custom_call_target="tpu_custom_call", output_to_operand_aliasing={{2}: (25, {})} | custom-call | tf_op jit(solution)/shard_map/slot/pallas_call | solution.py:449
  446.0 9.9 %collective-permute-start.43 = (bf16[2,1152,256]{2,1,0:T(8,128)(2,1)}, bf16[2,1152,256]{2,1,0:T(8,128)(2,1)S(1)}, u32[]{:S(2)}, u32[]{:S(2)}) collective-permute-start(bf16[2,1152,256]{2,1,0:T(8,128)(2,1)} %get-tuple-element.113.refs_20_.refs_12_), channel_id=1, source_target_pairs={{0,8},{24,16},{8,0},{16,24},{1,9},{25,17},{9,1},{17,25},{2,10},{26... | collective-permute-start | bytes 3538952 | tf_op jit(solution)/shard_map/ppermute | solution.py:483
  467.0 11.8 %slot.38 = (bf16[2,1152,256]{2,1,0:T(8,128)(2,1)}, bf16[2,1152,256]{2,1,0:T(8,128)(2,1)}, bf16[2,3456,1280]{2,1,0:T(8,128)(2,1)}, f32[512,256]{1,0:T(8,128)}) custom-call(s32[2]{0:T(128)} %pad_add_fusion.flag, bf16[6912,1280]{1,0:T(8,128)(2,1)} %bitcast.216, bf16[2,1152,256]{2,1,0:T(8,128)(2,1)} %copy-done.18, ...), custom_call_target="tpu_custom_call", output_to_operand_aliasing={{2}: (23, {})} | custom-call | tf_op jit(solution)/shard_map/slot/pallas_call | solution.py:449
  484.5 11.8 %slot.39 = (bf16[2,1152,256]{2,1,0:T(8,128)(2,1)}, bf16[2,1152,256]{2,1,0:T(8,128)(2,1)}, bf16[2,3456,1280]{2,1,0:T(8,128)(2,1)}, f32[512,256]{1,0:T(8,128)}) custom-call(s32[2]{0:T(128)} %pad_add_fusion.flag, bf16[6912,1280]{1,0:T(8,128)(2,1)} %bitcast.218, bf16[2,1152,256]{2,1,0:T(8,128)(2,1)} %copy-done.19, ...), custom_call_target="tpu_custom_call", output_to_operand_aliasing={{2}: (23, {})} | custom-call | tf_op jit(solution)/shard_map/slot/pallas_call | solution.py:449
  498.1 10.2 %collective-permute-start.49 = (bf16[2,1152,256]{2,1,0:T(8,128)(2,1)}, bf16[2,1152,256]{2,1,0:T(8,128)(2,1)S(1)}, u32[]{:S(2)}, u32[]{:S(2)}) collective-permute-start(bf16[2,1152,256]{2,1,0:T(8,128)(2,1)} %get-tuple-element.122.refs_14_.refs_1_), channel_id=1, source_target_pairs={{0,8},{24,16},{8,0},{16,24},{1,9},{25,17},{9,1},{17,25},{2,10},{26... | collective-permute-start | bytes 3538952 | tf_op jit(solution)/shard_map/ppermute | solution.py:483
  510.2 10.1 %slot.40 = (bf16[1,1152,256]{2,1,0:T(8,128)(2,1)}, bf16[2,1152,256]{2,1,0:T(8,128)(2,1)}, bf16[2,3456,1280]{2,1,0:T(8,128)(2,1)}, f32[512,256]{1,0:T(8,128)}) custom-call(s32[2]{0:T(128)} %pad_add_fusion.flag, bf16[6912,1280]{1,0:T(8,128)(2,1)} %bitcast.220, bf16[2,1152,256]{2,1,0:T(8,128)(2,1)} %copy-done.18, ...), custom_call_target="tpu_custom_call", output_to_operand_aliasing={{2}: (17, {})} | custom-call | tf_op jit(solution)/shard_map/slot/pallas_call | solution.py:449
  520.3 10.7 %collective-permute-start.55 = (bf16[2,1152,256]{2,1,0:T(8,128)(2,1)}, bf16[2,1152,256]{2,1,0:T(8,128)(2,1)S(1)}, u32[]{:S(2)}, u32[]{:S(2)}) collective-permute-start(bf16[2,1152,256]{2,1,0:T(8,128)(2,1)} %get-tuple-element.130.refs_3_.refs_0_), channel_id=1, source_target_pairs={{0,8},{24,16},{8,0},{16,24},{1,9},{25,17},{9,1},{17,25},{2,10},{26... | collective-permute-start | bytes 3538952 | tf_op jit(solution)/shard_map/ppermute | solution.py:483
  536.5 10.4 %slot.41 = (bf16[1,1152,256]{2,1,0:T(8,128)(2,1)}, bf16[2,1152,256]{2,1,0:T(8,128)(2,1)}, bf16[2,3456,1280]{2,1,0:T(8,128)(2,1)}, f32[512,256]{1,0:T(8,128)}) custom-call(s32[2]{0:T(128)} %pad_add_fusion.flag, bf16[6912,1280]{1,0:T(8,128)(2,1)} %bitcast.221, bf16[2,1152,256]{2,1,0:T(8,128)(2,1)} %copy-done.19, ...), custom_call_target="tpu_custom_call", output_to_operand_aliasing={{2}: (17, {})} | custom-call | tf_op jit(solution)/shard_map/slot/pallas_call | solution.py:449
  561.7 6.6 %slot.42 = (bf16[1,1152,256]{2,1,0:T(8,128)(2,1)}, bf16[2,3456,1280]{2,1,0:T(8,128)(2,1)}, f32[512,256]{1,0:T(8,128)}) custom-call(s32[2]{0:T(128)} %pad_add_fusion.flag, bf16[1,1152,256]{2,1,0:T(8,128)(2,1)} %copy-done.51, bf16[2,1152,256]{2,1,0:T(8,128)(2,1)} %get-tuple-element.123.refs_14_.refs_1_, ...), custom_call_target="tpu_custom_call", output_to_operand_aliasing={{1}: (6, {})} | custom-call | tf_op jit(solution)/shard_map/slot/pallas_call | solution.py:449
  568.3 10.9 %collective-permute-start.57 = (bf16[1,1152,256]{2,1,0:T(8,128)(2,1)}, bf16[1,1152,256]{2,1,0:T(8,128)(2,1)S(1)}, u32[]{:S(2)}, u32[]{:S(2)}) collective-permute-start(bf16[1,1152,256]{2,1,0:T(8,128)(2,1)} %get-tuple-element.134.refs_8_.refs_2_), channel_id=1, source_target_pairs={{0,8},{24,16},{8,0},{16,24},{1,9},{25,17},{9,1},{17,25},{2,10},{26... | collective-permute-start | bytes 1769480 | tf_op jit(solution)/shard_map/ppermute | solution.py:483
  579.2 6.8 %collective-permute-done.52.refs_4_.refs_1_ = bf16[2,1152,256]{2,1,0:T(8,128)(2,1)S(1)} collective-permute-done((bf16[2,1152,256]{2,1,0:T(8,128)(2,1)}, bf16[2,1152,256]{2,1,0:T(8,128)(2,1)S(1)}, u32[]{:S(2)}, u32[]{:S(2)}) %collective-permute-start.52) | collective-permute-done | bytes 1179680 | tf_op jit(solution)/shard_map/ppermute | solution.py:483
  (333 shorter events, 253.5 us)
Async XLA Ops:
  7.2 57.7 %all-gather.7.cloned.1.call-start = ((), (), s32[]{:S(2)}) async-start(), calls=%async_computation | async-start | bytes 8847360 | tf_op jit(solution)/shard_map/all_gather | solution.py:501
  7.9 115.7 %all-gather.9.cloned.1.call-start = ((), (), s32[]{:S(2)}) async-start(), calls=%async_computation.1 | async-start | bytes 8847360 | tf_op jit(solution)/shard_map/all_gather | solution.py:613
  8.0 43.1 %collective-permute-start = (bf16[128,6912]{1,0:T(8,128)(2,1)}, bf16[128,6912]{1,0:T(8,128)(2,1)S(1)}, u32[]{:S(2)}, u32[]{:S(2)}) collective-permute-start(bf16[128,6912]{1,0:T(8,128)(2,1)} %bitcast.321), channel_id=1, source_target_pairs={{0,8},{24,16},{1,9},{25,17},{2,10},{26,18},{3,11},{27,19},{4,12},{... | collective-permute-start | bytes 5308424 | tf_op jit(solution)/shard_map/ppermute | solution.py:481
  60.2 113.0 %all-gather.11.cloned.1.call-start = ((), (), s32[]{:S(2)}) async-start(), calls=%async_computation.2 | async-start | bytes 8847360 | tf_op jit(solution)/shard_map/all_gather | solution.py:613
  60.8 42.4 %collective-permute-start.2 = (bf16[2,1152,256]{2,1,0:T(8,128)(2,1)}, bf16[2,1152,256]{2,1,0:T(8,128)(2,1)S(1)}, u32[]{:S(2)}, u32[]{:S(2)}) collective-permute-start(bf16[2,1152,256]{2,1,0:T(8,128)(2,1)} %slot.23.refs_6_), channel_id=1, source_target_pairs={{0,8},{24,16},{8,0},{16,24},{1,9},{25,17},{9,1},{17,25},{2,10},{26... | collective-permute-start | bytes 3538952 | tf_op jit(solution)/shard_map/ppermute | solution.py:483
  64.1 44.1 %collective-permute-start.7 = (bf16[128,3456]{1,0:T(8,128)(2,1)}, bf16[128,3456]{1,0:T(8,128)(2,1)S(1)}, u32[]{:S(2)}, u32[]{:S(2)}) collective-permute-start(bf16[128,3456]{1,0:T(8,128)(2,1)} %constant_dynamic-slice_fusion.1), channel_id=1, source_target_pairs={{8,16},{16,8},{9,17},{17,9},{10,18},{18,10},{11,19},{19,11},{12,20... | collective-permute-start | bytes 2654216 | tf_op jit(solution)/shard_map/ppermute | solution.py:482
  133.6 38.0 %collective-permute-start.9 = (bf16[2,1280,256]{2,1,0:T(8,128)(2,1)}, bf16[2,1280,256]{2,1,0:T(8,128)(2,1)}, u32[]{:S(2)}, u32[]{:S(2)}) collective-permute-start(bf16[2,1280,256]{2,1,0:T(8,128)(2,1)} %get-tuple-element.74), channel_id=1, source_target_pairs={{0,8},{24,16},{8,0},{16,24},{1,9},{25,17},{9,1},{17,25},{2,10},{26... | collective-permute-start | bytes 3932168 | tf_op jit(solution)/shard_map/ppermute | solution.py:483
  137.5 35.7 %collective-permute-start.10 = (bf16[2,1280,256]{2,1,0:T(8,128)(2,1)}, bf16[2,1280,256]{2,1,0:T(8,128)(2,1)}, u32[]{:S(2)}, u32[]{:S(2)}) collective-permute-start(bf16[2,1280,256]{2,1,0:T(8,128)(2,1)} %get-tuple-element.75.refs_13_), channel_id=1, source_target_pairs={{8,16},{16,8},{9,17},{17,9},{10,18},{18,10},{11,19},{19,11},{12,20... | collective-permute-start | bytes 3932168 | tf_op jit(solution)/shard_map/ppermute | solution.py:482
  153.2 46.4 %collective-permute-start.18 = (bf16[2,1280,256]{2,1,0:T(8,128)(2,1)}, bf16[2,1280,256]{2,1,0:T(8,128)(2,1)S(1)}, u32[]{:S(2)}, u32[]{:S(2)}) collective-permute-start(bf16[2,1280,256]{2,1,0:T(8,128)(2,1)} %get-tuple-element.82), channel_id=1, source_target_pairs={{0,8},{24,16},{8,0},{16,24},{1,9},{25,17},{9,1},{17,25},{2,10},{26... | collective-permute-start | bytes 3932168 | tf_op jit(solution)/shard_map/ppermute | solution.py:483
  155.4 45.3 %collective-permute-start.19 = (bf16[2,1280,256]{2,1,0:T(8,128)(2,1)}, bf16[2,1280,256]{2,1,0:T(8,128)(2,1)}, u32[]{:S(2)}, u32[]{:S(2)}) collective-permute-start(bf16[2,1280,256]{2,1,0:T(8,128)(2,1)} %get-tuple-element.78.refs_23_), channel_id=1, source_target_pairs={{8,16},{16,8},{9,17},{17,9},{10,18},{18,10},{11,19},{19,11},{12,20... | collective-permute-start | bytes 3932168 | tf_op jit(solution)/shard_map/ppermute | solution.py:482
  184.3 40.6 %collective-permute-start.16 = (bf16[2,1280,256]{2,1,0:T(8,128)(2,1)}, bf16[2,1280,256]{2,1,0:T(8,128)(2,1)}, u32[]{:S(2)}, u32[]{:S(2)}) collective-permute-start(bf16[2,1280,256]{2,1,0:T(8,128)(2,1)} %get-tuple-element.80.refs_22_), channel_id=1, source_target_pairs={{8,16},{16,8},{9,17},{17,9},{10,18},{18,10},{11,19},{19,11},{12,20... | collective-permute-start | bytes 3932168 | tf_op jit(solution)/shard_map/ppermute | solution.py:482
  186.2 38.7 %collective-permute-start.14 = (bf16[2,1152,256]{2,1,0:T(8,128)(2,1)}, bf16[2,1152,256]{2,1,0:T(8,128)(2,1)S(1)}, u32[]{:S(2)}, u32[]{:S(2)}) collective-permute-start(bf16[2,1152,256]{2,1,0:T(8,128)(2,1)} %get-tuple-element.79.refs_21_), channel_id=1, source_target_pairs={{0,8},{24,16},{8,0},{16,24},{1,9},{25,17},{9,1},{17,25},{2,10},{26... | collective-permute-start | bytes 3538952 | tf_op jit(solution)/shard_map/ppermute | solution.py:483
  212.0 38.2 %collective-permute-start.25 = (bf16[2,1280,256]{2,1,0:T(8,128)(2,1)}, bf16[2,1280,256]{2,1,0:T(8,128)(2,1)}, u32[]{:S(2)}, u32[]{:S(2)}) collective-permute-start(bf16[2,1280,256]{2,1,0:T(8,128)(2,1)} %get-tuple-element.84.refs_25_), channel_id=1, source_target_pairs={{8,16},{16,8},{9,17},{17,9},{10,18},{18,10},{11,19},{19,11},{12,20... | collective-permute-start | bytes 3932168 | tf_op jit(solution)/shard_map/ppermute | solution.py:482
  237.1 41.1 %collective-permute-start.20 = (bf16[2,1280,256]{2,1,0:T(8,128)(2,1)}, bf16[2,1280,256]{2,1,0:T(8,128)(2,1)S(1)}, u32[]{:S(2)}, u32[]{:S(2)}) collective-permute-start(bf16[2,1280,256]{2,1,0:T(8,128)(2,1)} %get-tuple-element.85.refs_23_.refs_20_), channel_id=1, source_target_pairs={{0,8},{24,16},{8,0},{16,24},{1,9},{25,17},{9,1},{17,25},{2,10},{26... | collective-permute-start | bytes 3932168 | tf_op jit(solution)/shard_map/ppermute | solution.py:483
  238.8 40.1 %collective-permute-start.22 = (bf16[2,1280,256]{2,1,0:T(8,128)(2,1)}, bf16[2,1280,256]{2,1,0:T(8,128)(2,1)}, u32[]{:S(2)}, u32[]{:S(2)}) collective-permute-start(bf16[2,1280,256]{2,1,0:T(8,128)(2,1)} %get-tuple-element.86.refs_23_), channel_id=1, source_target_pairs={{8,16},{16,8},{9,17},{17,9},{10,18},{18,10},{11,19},{19,11},{12,20... | collective-permute-start | bytes 3932168 | tf_op jit(solution)/shard_map/ppermute | solution.py:482
  262.0 43.5 %collective-permute-start.29 = (bf16[2,1152,256]{2,1,0:T(8,128)(2,1)}, bf16[2,1152,256]{2,1,0:T(8,128)(2,1)S(1)}, u32[]{:S(2)}, u32[]{:S(2)}) collective-permute-start(bf16[2,1152,256]{2,1,0:T(8,128)(2,1)} %get-tuple-element.92.refs_24_.refs_21_), channel_id=1, source_target_pairs={{0,8},{24,16},{8,0},{16,24},{1,9},{25,17},{9,1},{17,25},{2,10},{26... | collective-permute-start | bytes 3538952 | tf_op jit(solution)/shard_map/ppermute | solution.py:483
  266.5 39.0 %collective-permute-start.30 = (bf16[2,1152,256]{2,1,0:T(8,128)(2,1)}, bf16[2,1152,256]{2,1,0:T(8,128)(2,1)}, u32[]{:S(2)}, u32[]{:S(2)}) collective-permute-start(bf16[2,1152,256]{2,1,0:T(8,128)(2,1)} %get-tuple-element.89.refs_27_), channel_id=1, source_target_pairs={{8,16},{16,8},{9,17},{17,9},{10,18},{18,10},{11,19},{19,11},{12,20... | collective-permute-start | bytes 3538952 | tf_op jit(solution)/shard_map/ppermute | solution.py:482
  291.7 37.2 %collective-permute-start.27 = (bf16[2,1280,256]{2,1,0:T(8,128)(2,1)}, bf16[2,1280,256]{2,1,0:T(8,128)(2,1)}, u32[]{:S(2)}, u32[]{:S(2)}) collective-permute-start(bf16[2,1280,256]{2,1,0:T(8,128)(2,1)} %get-tuple-element.91.refs_30_), channel_id=1, source_target_pairs={{8,16},{16,8},{9,17},{17,9},{10,18},{18,10},{11,19},{19,11},{12,20... | collective-permute-start | bytes 3932168 | tf_op jit(solution)/shard_map/ppermute | solution.py:482
  293.4 35.5 %collective-permute-start.26 = (bf16[2,1152,256]{2,1,0:T(8,128)(2,1)}, bf16[2,1152,256]{2,1,0:T(8,128)(2,1)}, u32[]{:S(2)}, u32[]{:S(2)}) collective-permute-start(bf16[2,1152,256]{2,1,0:T(8,128)(2,1)} %get-tuple-element.90.refs_22_.refs_20_), channel_id=1, source_target_pairs={{0,8},{24,16},{8,0},{16,24},{1,9},{25,17},{9,1},{17,25},{2,10},{26... | collective-permute-start | bytes 3538952 | tf_op jit(solution)/shard_map/ppermute | solution.py:483
  319.0 38.8 %collective-permute-start.35 = (bf16[2,1280,256]{2,1,0:T(8,128)(2,1)}, bf16[2,1280,256]{2,1,0:T(8,128)(2,1)S(1)}, u32[]{:S(2)}, u32[]{:S(2)}) collective-permute-start(bf16[2,1280,256]{2,1,0:T(8,128)(2,1)} %get-tuple-element.101.refs_23_.refs_20_), channel_id=1, source_target_pairs={{0,8},{24,16},{8,0},{16,24},{1,9},{25,17},{9,1},{17,25},{2,10},{26... | collective-permute-start | bytes 3932168 | tf_op jit(solution)/shard_map/ppermute | solution.py:483
  321.6 37.0 %collective-permute-start.36 = (bf16[2,1280,256]{2,1,0:T(8,128)(2,1)}, bf16[2,1280,256]{2,1,0:T(8,128)(2,1)S(1)}, u32[]{:S(2)}, u32[]{:S(2)}) collective-permute-start(bf16[2,1280,256]{2,1,0:T(8,128)(2,1)} %get-tuple-element.98.refs_28_), channel_id=1, source_target_pairs={{8,16},{16,8},{9,17},{17,9},{10,18},{18,10},{11,19},{19,11},{12,20... | collective-permute-start | bytes 3932168 | tf_op jit(solution)/shard_map/ppermute | solution.py:482
  341.3 41.0 %collective-permute-start.32 = (bf16[2,1152,256]{2,1,0:T(8,128)(2,1)}, bf16[2,1152,256]{2,1,0:T(8,128)(2,1)}, u32[]{:S(2)}, u32[]{:S(2)}) collective-permute-start(bf16[2,1152,256]{2,1,0:T(8,128)(2,1)} %get-tuple-element.99.refs_22_.refs_20_), channel_id=1, source_target_pairs={{0,8},{24,16},{8,0},{16,24},{1,9},{25,17},{9,1},{17,25},{2,10},{26... | collective-permute-start | bytes 3538952 | tf_op jit(solution)/shard_map/ppermute | solution.py:483
  372.0 41.0 %collective-permute-start.42 = (bf16[2,1280,256]{2,1,0:T(8,128)(2,1)}, bf16[2,1280,256]{2,1,0:T(8,128)(2,1)}, u32[]{:S(2)}, u32[]{:S(2)}) collective-permute-start(bf16[2,1280,256]{2,1,0:T(8,128)(2,1)} %get-tuple-element.105.refs_28_), channel_id=1, source_target_pairs={{8,16},{16,8},{9,17},{17,9},{10,18},{18,10},{11,19},{19,11},{12,20... | collective-permute-start | bytes 3932168 | tf_op jit(solution)/shard_map/ppermute | solution.py:482
  373.7 39.2 %collective-permute-start.41 = (bf16[2,1152,256]{2,1,0:T(8,128)(2,1)}, bf16[2,1152,256]{2,1,0:T(8,128)(2,1)S(1)}, u32[]{:S(2)}, u32[]{:S(2)}) collective-permute-start(bf16[2,1152,256]{2,1,0:T(8,128)(2,1)} %get-tuple-element.108.refs_22_.refs_18_), channel_id=1, source_target_pairs={{0,8},{24,16},{8,0},{16,24},{1,9},{25,17},{9,1},{17,25},{2,10},{26... | collective-permute-start | bytes 3538952 | tf_op jit(solution)/shard_map/ppermute | solution.py:483
  394.5 38.5 %collective-permute-start.37 = (bf16[2,1152,256]{2,1,0:T(8,128)(2,1)}, bf16[2,1152,256]{2,1,0:T(8,128)(2,1)S(1)}, u32[]{:S(2)}, u32[]{:S(2)}) collective-permute-start(bf16[2,1152,256]{2,1,0:T(8,128)(2,1)} %get-tuple-element.106.refs_22_.refs_18_), channel_id=1, source_target_pairs={{0,8},{24,16},{8,0},{16,24},{1,9},{25,17},{9,1},{17,25},{2,10},{26... | collective-permute-start | bytes 3538952 | tf_op jit(solution)/shard_map/ppermute | solution.py:483
  426.3 39.6 %collective-permute-start.46 = (bf16[2,1152,256]{2,1,0:T(8,128)(2,1)}, bf16[2,1152,256]{2,1,0:T(8,128)(2,1)S(1)}, u32[]{:S(2)}, u32[]{:S(2)}) collective-permute-start(bf16[2,1152,256]{2,1,0:T(8,128)(2,1)} %get-tuple-element.115.refs_20_.refs_12_), channel_id=1, source_target_pairs={{0,8},{24,16},{8,0},{16,24},{1,9},{25,17},{9,1},{17,25},{2,10},{26... | collective-permute-start | bytes 3538952 | tf_op jit(solution)/shard_map/ppermute | solution.py:483
  430.8 35.1 %collective-permute-start.47 = (bf16[2,1152,256]{2,1,0:T(8,128)(2,1)}, bf16[2,1152,256]{2,1,0:T(8,128)(2,1)}, u32[]{:S(2)}, u32[]{:S(2)}) collective-permute-start(bf16[2,1152,256]{2,1,0:T(8,128)(2,1)} %get-tuple-element.112.refs_27_), channel_id=1, source_target_pairs={{8,16},{16,8},{9,17},{17,9},{10,18},{18,10},{11,19},{19,11},{12,20... | collective-permute-start | bytes 3538952 | tf_op jit(solution)/shard_map/ppermute | solution.py:482
  446.0 37.6 %collective-permute-start.43 = (bf16[2,1152,256]{2,1,0:T(8,128)(2,1)}, bf16[2,1152,256]{2,1,0:T(8,128)(2,1)S(1)}, u32[]{:S(2)}, u32[]{:S(2)}) collective-permute-start(bf16[2,1152,256]{2,1,0:T(8,128)(2,1)} %get-tuple-element.113.refs_20_.refs_12_), channel_id=1, source_target_pairs={{0,8},{24,16},{8,0},{16,24},{1,9},{25,17},{9,1},{17,25},{2,10},{26... | collective-permute-start | bytes 3538952 | tf_op jit(solution)/shard_map/ppermute | solution.py:483
  498.1 37.3 %collective-permute-start.49 = (bf16[2,1152,256]{2,1,0:T(8,128)(2,1)}, bf16[2,1152,256]{2,1,0:T(8,128)(2,1)S(1)}, u32[]{:S(2)}, u32[]{:S(2)}) collective-permute-start(bf16[2,1152,256]{2,1,0:T(8,128)(2,1)} %get-tuple-element.122.refs_14_.refs_1_), channel_id=1, source_target_pairs={{0,8},{24,16},{8,0},{16,24},{1,9},{25,17},{9,1},{17,25},{2,10},{26... | collective-permute-start | bytes 3538952 | tf_op jit(solution)/shard_map/ppermute | solution.py:483
  520.3 40.4 %collective-permute-start.55 = (bf16[2,1152,256]{2,1,0:T(8,128)(2,1)}, bf16[2,1152,256]{2,1,0:T(8,128)(2,1)S(1)}, u32[]{:S(2)}, u32[]{:S(2)}) collective-permute-start(bf16[2,1152,256]{2,1,0:T(8,128)(2,1)} %get-tuple-element.130.refs_3_.refs_0_), channel_id=1, source_target_pairs={{0,8},{24,16},{8,0},{16,24},{1,9},{25,17},{9,1},{17,25},{2,10},{26... | collective-permute-start | bytes 3538952 | tf_op jit(solution)/shard_map/ppermute | solution.py:483
  546.9 39.0 %collective-permute-start.52 = (bf16[2,1152,256]{2,1,0:T(8,128)(2,1)}, bf16[2,1152,256]{2,1,0:T(8,128)(2,1)S(1)}, u32[]{:S(2)}, u32[]{:S(2)}) collective-permute-start(bf16[2,1152,256]{2,1,0:T(8,128)(2,1)} %get-tuple-element.128.refs_3_.refs_0_), channel_id=1, source_target_pairs={{0,8},{24,16},{8,0},{16,24},{1,9},{25,17},{9,1},{17,25},{2,10},{26... | collective-permute-start | bytes 3538952 | tf_op jit(solution)/shard_map/ppermute | solution.py:483
  559.5 36.4 %collective-permute-start.59 = (bf16[1,256,256]{2,1,0:T(8,128)(2,1)}, bf16[1,256,256]{2,1,0:T(8,128)(2,1)}, u32[]{:S(2)}, u32[]{:S(2)}) collective-permute-start(bf16[1,256,256]{2,1,0:T(8,128)(2,1)} %dynamic-slice_bitcast_fusion.4), channel_id=1, source_target_pairs={{0,4},{4,0},{1,5},{5,1},{2,6},{6,2},{3,7},{7,3},{8,12},{12,8},{9,1... | collective-permute-start | bytes 393224 | tf_op jit(solution)/shard_map/ppermute | solution.py:484
  (93 other events, 949.0 us)
Sparse Core Ops, SparseCore 0:
  9.6 53.5 all-gather.6
  64.7 50.8 all-gather.8
  117.7 50.8 all-gather.10

commit v5 on v4

--- a/solution.py
+++ b/solution.py
@@ -46,7 +46,7 @@
 
 def group_product(lhs, mat, group, groups, deps=()):
     tokens, rows = lhs.shape
-    depth = largest_divisor(rows, 1152, 128)
+    depth = largest_divisor(rows, 2304, 128)
     steps = rows // depth
 
     def body(lhs_ref, *rest):

time: 639 us -> 638 us (level)
  transfers between devices with their start and end apart: 66 -> 66, of which waited for: 29 -> 28; matrix products, arithmetic and copies ran while one was open for 4% -> 4% of each run, Pallas kernels for 41% -> 41%
where the time goes in v5:
time: 638 us; the launch traced here: 628 us
  Pallas kernels  255 us (40%)
  starting transfers between devices  156 us (24%)
  waiting for transfers between devices  151 us (24%)
  local copies, waits for them, and re-layouts  41.4 us (6%)
  between operations  15.3 us (2%)
  other arithmetic  9.01 us (1%)
    pallas_call x23, Pallas kernels, slot_call(): pl.pallas_call(body, grid_spec=pltpu.PrefetchScalarGridSpec(num_scalar_pr...  225 us
    ppermute x22, starting transfers between devices, local(): lax.ppermute(x, 'task', step_in(last - 1) + step_out(last - 1))  100 us
    ppermute x22, waiting for transfers between devices, local(): lax.ppermute(x, 'task', step_in(last - 1) + step_out(last - 1))  66.3 us
    ppermute x20, waiting for transfers between devices, local(): lax.ppermute(x, 'row', [(i, (i + s) % rows_n) for i in range(rows_n)])  49.2 us
    ppermute x1, waiting for transfers between devices, local(): send_in = lambda x: lax.ppermute(x, 'task', all_in)  34.6 us
    ppermute x20, starting transfers between devices, local(): lax.ppermute(x, 'task', [(last, side_n), (side_n, last)])  29.6 us
    unnamed x119, local copies, waits for them, and re-layouts  23.5 us
    ppermute x20, starting transfers between devices, local(): lax.ppermute(x, 'row', [(i, (i + s) % rows_n) for i in range(rows_n)])  21 us
  transfers between devices with their start and end apart: 66, of which 28 were waited for; matrix products, arithmetic and copies ran while one was open for 4% of the time, Pallas kernels for 41%

profile of v5, /device:TPU:0, one launch (start us, length us, event | category | flops | bytes accessed | tf_op | source)
XLA Modules:
  0.0 627.6 jit_solution(4076794999272517854)
XLA Ops:
  16.5 34.6 %collective-permute-done.refs_0_ = bf16[128,6912]{1,0:T(8,128)(2,1)S(1)} collective-permute-done((bf16[128,6912]{1,0:T(8,128)(2,1)}, bf16[128,6912]{1,0:T(8,128)(2,1)S(1)}, u32[]{:S(2)}, u32[]{:S(2)}) %collective-permute-start) | collective-permute-done | bytes 1769504 | tf_op jit(solution)/shard_map/ppermute | solution.py:481
  64.9 11.4 %group_product.1 = bf16[3,512,256]{2,1,0:T(8,128)(2,1)} custom-call(bf16[512,6912]{1,0:T(8,128)(2,1)} %bitcast.222, bf16[6912,1280]{1,0:T(8,128)(2,1)} %bitcast.155, bf16[6912,1280]{1,0:T(8,128)(2,1)} %bitcast.156, bf16[6912,1280]{1,0:T(8,128)(2,1)} %bitcast.157, bf16[2,3456,128]{2,1,0:T(8,128)(2,1)} %cut.2.rest_3_), custom_call_target="tpu_custom_call" | custom-call | tf_op jit(solution)/shard_map/group_product/pallas_call | solution.py:71
  91.8 10.2 %squares.1.refs_2_.refs_6_.refs_8_ = bf16[6912,512]{1,0:T(8,128)(2,1)} custom-call(bf16[512,6912]{1,0:T(8,128)(2,1)} %bitcast.223, bf16[1,256,256]{2,1,0:T(8,128)(2,1)} %copy-done.39), custom_call_target="tpu_custom_call" | custom-call | tf_op jit(solution)/shard_map/squares/pallas_call | solution.py:94
  123.2 9.5 %slot.25 = (bf16[2,1280,256]{2,1,0:T(8,128)(2,1)}, bf16[2,1280,256]{2,1,0:T(8,128)(2,1)}, f32[512,256]{1,0:T(8,128)}) custom-call(s32[2]{0:T(128)} %pad_add_fusion.flag, bf16[6912,1280]{1,0:T(8,128)(2,1)} %bitcast.160, bf16[2,1152,256]{2,1,0:T(8,128)(2,1)} %copy-done.22, bf16[6912,512]{1,0:T(8,128)(2,1)} %squares.1.refs_2_.refs_6_.refs_8_, ...), custom_call_target="tpu_custom_call" | custom-call | tf_op jit(solution)/shard_map/slot/pallas_call | solution.py:449
  143.2 8.8 %slot.26 = (bf16[2,1280,256]{2,1,0:T(8,128)(2,1)}, bf16[2,1280,256]{2,1,0:T(8,128)(2,1)}, f32[512,256]{1,0:T(8,128)}) custom-call(s32[2]{0:T(128)} %pad_add_fusion.flag, bf16[6912,1280]{1,0:T(8,128)(2,1)} %bitcast.167, bf16[2,1152,256]{2,1,0:T(8,128)(2,1)} %copy-done.29, bf16[6912,512]{1,0:T(8,128)(2,1)} %squares.1.refs_2_.refs_6_.refs_8_, ...), custom_call_target="tpu_custom_call" | custom-call | tf_op jit(solution)/shard_map/slot/pallas_call | solution.py:449
  159.0 11.3 %collective-permute-done.9.refs_1_.refs_7_ = bf16[2,1280,256]{2,1,0:T(8,128)(2,1)} collective-permute-done((bf16[2,1280,256]{2,1,0:T(8,128)(2,1)}, bf16[2,1280,256]{2,1,0:T(8,128)(2,1)}, u32[]{:S(2)}, u32[]{:S(2)}) %collective-permute-start.9) | collective-permute-done | bytes 1310752 | tf_op jit(solution)/shard_map/ppermute | solution.py:483
  171.9 11.1 %slot.27 = (bf16[2,1280,256]{2,1,0:T(8,128)(2,1)}, bf16[2,1152,256]{2,1,0:T(8,128)(2,1)}, f32[512,256]{1,0:T(8,128)}) custom-call(s32[2]{0:T(128)} %pad_add_fusion.flag, bf16[6912,1280]{1,0:T(8,128)(2,1)} %bitcast.168, bf16[2,1280,256]{2,1,0:T(8,128)(2,1)} %collective-permute-done.9.refs_1_.refs_7_, bf16[6912,512]{1,0:T(8,128)(2,1)} %squares.1.refs_2_.refs_6_.refs_8_, ...), custom_call_target="tpu_custom_call" | custom-call | tf_op jit(solution)/shard_map/slot/pallas_call | solution.py:449
  187.5 10.8 %collective-permute-done.18.refs_1_.refs_7_ = bf16[2,1280,256]{2,1,0:T(8,128)(2,1)S(1)} collective-permute-done((bf16[2,1280,256]{2,1,0:T(8,128)(2,1)}, bf16[2,1280,256]{2,1,0:T(8,128)(2,1)S(1)}, u32[]{:S(2)}, u32[]{:S(2)}) %collective-permute-start.18) | collective-permute-done | bytes 1310752 | tf_op jit(solution)/shard_map/ppermute | solution.py:483
  199.9 10.8 %slot.28 = (bf16[2,1280,256]{2,1,0:T(8,128)(2,1)}, bf16[2,1152,256]{2,1,0:T(8,128)(2,1)}, f32[512,256]{1,0:T(8,128)}) custom-call(s32[2]{0:T(128)} %pad_add_fusion.flag, bf16[6912,1280]{1,0:T(8,128)(2,1)} %bitcast.173, bf16[2,1280,256]{2,1,0:T(8,128)(2,1)} %copy-done.27, bf16[6912,512]{1,0:T(8,128)(2,1)} %squares.1.refs_2_.refs_6_.refs_8_, ...), custom_call_target="tpu_custom_call" | custom-call | tf_op jit(solution)/shard_map/slot/pallas_call | solution.py:449
  224.6 11.2 %slot.29 = (bf16[2,1280,256]{2,1,0:T(8,128)(2,1)}, bf16[2,1280,256]{2,1,0:T(8,128)(2,1)}, f32[512,256]{1,0:T(8,128)}) custom-call(s32[2]{0:T(128)} %pad_add_fusion.flag, bf16[6912,1280]{1,0:T(8,128)(2,1)} %bitcast.178, bf16[2,1152,256]{2,1,0:T(8,128)(2,1)} %copy-done.23, bf16[6912,512]{1,0:T(8,128)(2,1)} %squares.1.refs_2_.refs_6_.refs_8_, ...), custom_call_target="tpu_custom_call" | custom-call | tf_op jit(solution)/shard_map/slot/pallas_call | solution.py:449
  250.3 10.8 %slot.30 = (bf16[2,1152,256]{2,1,0:T(8,128)(2,1)}, bf16[2,1152,256]{2,1,0:T(8,128)(2,1)}, f32[512,256]{1,0:T(8,128)}) custom-call(s32[2]{0:T(128)} %pad_add_fusion.flag, bf16[6912,1280]{1,0:T(8,128)(2,1)} %bitcast.187, bf16[2,1152,256]{2,1,0:T(8,128)(2,1)} %copy-done.24, bf16[6912,512]{1,0:T(8,128)(2,1)} %squares.1.refs_2_.refs_6_.refs_8_, ...), custom_call_target="tpu_custom_call" | custom-call | tf_op jit(solution)/shard_map/slot/pallas_call | solution.py:449
  266.5 10.4 %collective-permute-done.20.refs_1_.refs_24_.refs_7_.refs_21_ = bf16[2,1280,256]{2,1,0:T(8,128)(2,1)S(1)} collective-permute-done((bf16[2,1280,256]{2,1,0:T(8,128)(2,1)}, bf16[2,1280,256]{2,1,0:T(8,128)(2,1)S(1)}, u32[]{:S(2)}, u32[]{:S(2)}) %collective-permute-start.20) | collective-permute-done | bytes 1310752 | tf_op jit(solution)/shard_map/ppermute | solution.py:483
  278.1 12.3 %slot.31 = (bf16[2,1280,256]{2,1,0:T(8,128)(2,1)}, bf16[2,1152,256]{2,1,0:T(8,128)(2,1)}, bf16[2,3456,1280]{2,1,0:T(8,128)(2,1)}, f32[512,256]{1,0:T(8,128)}) custom-call(s32[2]{0:T(128)} %pad_add_fusion.flag, bf16[6912,1280]{1,0:T(8,128)(2,1)} %bitcast.188, bf16[2,1280,256]{2,1,0:T(8,128)(2,1)} %copy-done.15, ...), custom_call_target="tpu_custom_call" | custom-call | tf_op jit(solution)/shard_map/slot/pallas_call | solution.py:449
  305.5 12.5 %slot.32 = (bf16[2,1280,256]{2,1,0:T(8,128)(2,1)}, bf16[2,1280,256]{2,1,0:T(8,128)(2,1)}, bf16[2,3456,1280]{2,1,0:T(8,128)(2,1)}, f32[512,256]{1,0:T(8,128)}) custom-call(s32[2]{0:T(128)} %pad_add_fusion.flag, bf16[6912,1280]{1,0:T(8,128)(2,1)} %bitcast.192, bf16[2,1152,256]{2,1,0:T(8,128)(2,1)} %copy-done.20, ...), custom_call_target="tpu_custom_call", output_to_operand_aliasing={{2}: (27, {})} | custom-call | tf_op jit(solution)/shard_map/slot/pallas_call | solution.py:449
  320.7 7.0 %collective-permute-done.26.refs_1_.refs_23_.refs_7_.refs_21_ = bf16[2,1152,256]{2,1,0:T(8,128)(2,1)} collective-permute-done((bf16[2,1152,256]{2,1,0:T(8,128)(2,1)}, bf16[2,1152,256]{2,1,0:T(8,128)(2,1)}, u32[]{:S(2)}, u32[]{:S(2)}) %collective-permute-start.26) | collective-permute-done | bytes 1179680 | tf_op jit(solution)/shard_map/ppermute | solution.py:483
  327.7 12.3 %slot.33 = (bf16[2,1152,256]{2,1,0:T(8,128)(2,1)}, bf16[2,1152,256]{2,1,0:T(8,128)(2,1)}, bf16[2,3456,1280]{2,1,0:T(8,128)(2,1)}, f32[512,256]{1,0:T(8,128)}) custom-call(s32[2]{0:T(128)} %pad_add_fusion.flag, bf16[6912,1280]{1,0:T(8,128)(2,1)} %bitcast.196, ...), custom_call_target="tpu_custom_call", output_to_operand_aliasing={{2}: (25, {})} | custom-call | tf_op jit(solution)/shard_map/slot/pallas_call | solution.py:449
  340.0 7.7 %collective-permute-start.32 = (bf16[2,1152,256]{2,1,0:T(8,128)(2,1)}, bf16[2,1152,256]{2,1,0:T(8,128)(2,1)}, u32[]{:S(2)}, u32[]{:S(2)}) collective-permute-start(bf16[2,1152,256]{2,1,0:T(8,128)(2,1)} %get-tuple-element.99.refs_22_.refs_20_), channel_id=1, source_target_pairs={{0,8},{24,16},{8,0},{16,24},{1,9},{25,17},{9,1},{17,25},{2,10},{26... | collective-permute-start | bytes 3538952 | tf_op jit(solution)/shard_map/ppermute | solution.py:483
  357.9 12.3 %slot.34 = (bf16[2,1280,256]{2,1,0:T(8,128)(2,1)}, bf16[2,1152,256]{2,1,0:T(8,128)(2,1)}, bf16[2,3456,1280]{2,1,0:T(8,128)(2,1)}, f32[512,256]{1,0:T(8,128)}) custom-call(s32[2]{0:T(128)} %pad_add_fusion.flag, bf16[6912,1280]{1,0:T(8,128)(2,1)} %bitcast.203, bf16[2,1280,256]{2,1,0:T(8,128)(2,1)} %copy-done.16, ...), custom_call_target="tpu_custom_call", output_to_operand_aliasing={{2}: (26, {})} | custom-call | tf_op jit(solution)/shard_map/slot/pallas_call | solution.py:449
  372.0 7.6 %collective-permute-start.41 = (bf16[2,1152,256]{2,1,0:T(8,128)(2,1)}, bf16[2,1152,256]{2,1,0:T(8,128)(2,1)S(1)}, u32[]{:S(2)}, u32[]{:S(2)}) collective-permute-start(bf16[2,1152,256]{2,1,0:T(8,128)(2,1)} %get-tuple-element.108.refs_22_.refs_18_), channel_id=1, source_target_pairs={{0,8},{24,16},{8,0},{16,24},{1,9},{25,17},{9,1},{17,25},{2,10},{26... | collective-permute-start | bytes 3538952 | tf_op jit(solution)/shard_map/ppermute | solution.py:483
  381.0 12.1 %slot.35 = (bf16[2,1152,256]{2,1,0:T(8,128)(2,1)}, bf16[2,1152,256]{2,1,0:T(8,128)(2,1)}, bf16[2,3456,1280]{2,1,0:T(8,128)(2,1)}, f32[512,256]{1,0:T(8,128)}) custom-call(s32[2]{0:T(128)} %pad_add_fusion.flag, bf16[6912,1280]{1,0:T(8,128)(2,1)} %bitcast.204, ...), custom_call_target="tpu_custom_call", output_to_operand_aliasing={{2}: (25, {})} | custom-call | tf_op jit(solution)/shard_map/slot/pallas_call | solution.py:449
  393.2 7.8 %collective-permute-start.37 = (bf16[2,1152,256]{2,1,0:T(8,128)(2,1)}, bf16[2,1152,256]{2,1,0:T(8,128)(2,1)S(1)}, u32[]{:S(2)}, u32[]{:S(2)}) collective-permute-start(bf16[2,1152,256]{2,1,0:T(8,128)(2,1)} %get-tuple-element.106.refs_22_.refs_18_), channel_id=1, source_target_pairs={{0,8},{24,16},{8,0},{16,24},{1,9},{25,17},{9,1},{17,25},{2,10},{26... | collective-permute-start | bytes 3538952 | tf_op jit(solution)/shard_map/ppermute | solution.py:483
  413.1 12.2 %slot.36 = (bf16[2,1152,256]{2,1,0:T(8,128)(2,1)}, bf16[2,1152,256]{2,1,0:T(8,128)(2,1)}, bf16[2,3456,1280]{2,1,0:T(8,128)(2,1)}, f32[512,256]{1,0:T(8,128)}) custom-call(s32[2]{0:T(128)} %pad_add_fusion.flag, bf16[6912,1280]{1,0:T(8,128)(2,1)} %bitcast.208, bf16[2,1152,256]{2,1,0:T(8,128)(2,1)} %copy-done.21, ...), custom_call_target="tpu_custom_call", output_to_operand_aliasing={{2}: (25, {})} | custom-call | tf_op jit(solution)/shard_map/slot/pallas_call | solution.py:449
  432.9 12.0 %slot.37 = (bf16[2,1152,256]{2,1,0:T(8,128)(2,1)}, bf16[2,1152,256]{2,1,0:T(8,128)(2,1)}, bf16[2,3456,1280]{2,1,0:T(8,128)(2,1)}, f32[512,256]{1,0:T(8,128)}) custom-call(s32[2]{0:T(128)} %pad_add_fusion.flag, bf16[6912,1280]{1,0:T(8,128)(2,1)} %bitcast.212, bf16[2,1152,256]{2,1,0:T(8,128)(2,1)} %copy-done.17, ...), custom_call_target="tpu_custom_call", output_to_operand_aliasing={{2}: (25, {})} | custom-call | tf_op jit(solution)/shard_map/slot/pallas_call | solution.py:449
  444.9 9.2 %collective-permute-start.43 = (bf16[2,1152,256]{2,1,0:T(8,128)(2,1)}, bf16[2,1152,256]{2,1,0:T(8,128)(2,1)S(1)}, u32[]{:S(2)}, u32[]{:S(2)}) collective-permute-start(bf16[2,1152,256]{2,1,0:T(8,128)(2,1)} %get-tuple-element.113.refs_20_.refs_12_), channel_id=1, source_target_pairs={{0,8},{24,16},{8,0},{16,24},{1,9},{25,17},{9,1},{17,25},{2,10},{26... | collective-permute-start | bytes 3538952 | tf_op jit(solution)/shard_map/ppermute | solution.py:483
  465.2 11.8 %slot.38 = (bf16[2,1152,256]{2,1,0:T(8,128)(2,1)}, bf16[2,1152,256]{2,1,0:T(8,128)(2,1)}, bf16[2,3456,1280]{2,1,0:T(8,128)(2,1)}, f32[512,256]{1,0:T(8,128)}) custom-call(s32[2]{0:T(128)} %pad_add_fusion.flag, bf16[6912,1280]{1,0:T(8,128)(2,1)} %bitcast.216, bf16[2,1152,256]{2,1,0:T(8,128)(2,1)} %copy-done.18, ...), custom_call_target="tpu_custom_call", output_to_operand_aliasing={{2}: (23, {})} | custom-call | tf_op jit(solution)/shard_map/slot/pallas_call | solution.py:449
  483.5 11.8 %slot.39 = (bf16[2,1152,256]{2,1,0:T(8,128)(2,1)}, bf16[2,1152,256]{2,1,0:T(8,128)(2,1)}, bf16[2,3456,1280]{2,1,0:T(8,128)(2,1)}, f32[512,256]{1,0:T(8,128)}) custom-call(s32[2]{0:T(128)} %pad_add_fusion.flag, bf16[6912,1280]{1,0:T(8,128)(2,1)} %bitcast.218, bf16[2,1152,256]{2,1,0:T(8,128)(2,1)} %copy-done.19, ...), custom_call_target="tpu_custom_call", output_to_operand_aliasing={{2}: (23, {})} | custom-call | tf_op jit(solution)/shard_map/slot/pallas_call | solution.py:449
  497.0 10.2 %collective-permute-start.49 = (bf16[2,1152,256]{2,1,0:T(8,128)(2,1)}, bf16[2,1152,256]{2,1,0:T(8,128)(2,1)S(1)}, u32[]{:S(2)}, u32[]{:S(2)}) collective-permute-start(bf16[2,1152,256]{2,1,0:T(8,128)(2,1)} %get-tuple-element.122.refs_14_.refs_1_), channel_id=1, source_target_pairs={{0,8},{24,16},{8,0},{16,24},{1,9},{25,17},{9,1},{17,25},{2,10},{26... | collective-permute-start | bytes 3538952 | tf_op jit(solution)/shard_map/ppermute | solution.py:483
  509.7 10.1 %slot.40 = (bf16[1,1152,256]{2,1,0:T(8,128)(2,1)}, bf16[2,1152,256]{2,1,0:T(8,128)(2,1)}, bf16[2,3456,1280]{2,1,0:T(8,128)(2,1)}, f32[512,256]{1,0:T(8,128)}) custom-call(s32[2]{0:T(128)} %pad_add_fusion.flag, bf16[6912,1280]{1,0:T(8,128)(2,1)} %bitcast.220, bf16[2,1152,256]{2,1,0:T(8,128)(2,1)} %copy-done.18, ...), custom_call_target="tpu_custom_call", output_to_operand_aliasing={{2}: (17, {})} | custom-call | tf_op jit(solution)/shard_map/slot/pallas_call | solution.py:449
  519.8 9.4 %collective-permute-start.55 = (bf16[2,1152,256]{2,1,0:T(8,128)(2,1)}, bf16[2,1152,256]{2,1,0:T(8,128)(2,1)S(1)}, u32[]{:S(2)}, u32[]{:S(2)}) collective-permute-start(bf16[2,1152,256]{2,1,0:T(8,128)(2,1)} %get-tuple-element.130.refs_3_.refs_0_), channel_id=1, source_target_pairs={{0,8},{24,16},{8,0},{16,24},{1,9},{25,17},{9,1},{17,25},{2,10},{26... | collective-permute-start | bytes 3538952 | tf_op jit(solution)/shard_map/ppermute | solution.py:483
  535.4 10.4 %slot.41 = (bf16[1,1152,256]{2,1,0:T(8,128)(2,1)}, bf16[2,1152,256]{2,1,0:T(8,128)(2,1)}, bf16[2,3456,1280]{2,1,0:T(8,128)(2,1)}, f32[512,256]{1,0:T(8,128)}) custom-call(s32[2]{0:T(128)} %pad_add_fusion.flag, bf16[6912,1280]{1,0:T(8,128)(2,1)} %bitcast.221, bf16[2,1152,256]{2,1,0:T(8,128)(2,1)} %copy-done.19, ...), custom_call_target="tpu_custom_call", output_to_operand_aliasing={{2}: (17, {})} | custom-call | tf_op jit(solution)/shard_map/slot/pallas_call | solution.py:449
  567.3 10.4 %collective-permute-start.57 = (bf16[1,1152,256]{2,1,0:T(8,128)(2,1)}, bf16[1,1152,256]{2,1,0:T(8,128)(2,1)S(1)}, u32[]{:S(2)}, u32[]{:S(2)}) collective-permute-start(bf16[1,1152,256]{2,1,0:T(8,128)(2,1)} %get-tuple-element.134.refs_8_.refs_2_), channel_id=1, source_target_pairs={{0,8},{24,16},{8,0},{16,24},{1,9},{25,17},{9,1},{17,25},{2,10},{26... | collective-permute-start | bytes 1769480 | tf_op jit(solution)/shard_map/ppermute | solution.py:483
  577.7 7.2 %collective-permute-done.52.refs_4_.refs_1_ = bf16[2,1152,256]{2,1,0:T(8,128)(2,1)S(1)} collective-permute-done((bf16[2,1152,256]{2,1,0:T(8,128)(2,1)}, bf16[2,1152,256]{2,1,0:T(8,128)(2,1)S(1)}, u32[]{:S(2)}, u32[]{:S(2)}) %collective-permute-start.52) | collective-permute-done | bytes 1179680 | tf_op jit(solution)/shard_map/ppermute | solution.py:483
  (333 shorter events, 254.8 us)
Async XLA Ops:
  7.2 57.7 %all-gather.7.cloned.1.call-start = ((), (), s32[]{:S(2)}) async-start(), calls=%async_computation | async-start | bytes 8847360 | tf_op jit(solution)/shard_map/all_gather | solution.py:501
  7.9 114.4 %all-gather.9.cloned.1.call-start = ((), (), s32[]{:S(2)}) async-start(), calls=%async_computation.1 | async-start | bytes 8847360 | tf_op jit(solution)/shard_map/all_gather | solution.py:613
  8.0 43.1 %collective-permute-start = (bf16[128,6912]{1,0:T(8,128)(2,1)}, bf16[128,6912]{1,0:T(8,128)(2,1)S(1)}, u32[]{:S(2)}, u32[]{:S(2)}) collective-permute-start(bf16[128,6912]{1,0:T(8,128)(2,1)} %bitcast.321), channel_id=1, source_target_pairs={{0,8},{24,16},{1,9},{25,17},{2,10},{26,18},{3,11},{27,19},{4,12},{... | collective-permute-start | bytes 5308424 | tf_op jit(solution)/shard_map/ppermute | solution.py:481
  60.2 111.7 %all-gather.11.cloned.1.call-start = ((), (), s32[]{:S(2)}) async-start(), calls=%async_computation.2 | async-start | bytes 8847360 | tf_op jit(solution)/shard_map/all_gather | solution.py:613
  60.8 41.2 %collective-permute-start.2 = (bf16[2,1152,256]{2,1,0:T(8,128)(2,1)}, bf16[2,1152,256]{2,1,0:T(8,128)(2,1)S(1)}, u32[]{:S(2)}, u32[]{:S(2)}) collective-permute-start(bf16[2,1152,256]{2,1,0:T(8,128)(2,1)} %slot.23.refs_6_), channel_id=1, source_target_pairs={{0,8},{24,16},{8,0},{16,24},{1,9},{25,17},{9,1},{17,25},{2,10},{26... | collective-permute-start | bytes 3538952 | tf_op jit(solution)/shard_map/ppermute | solution.py:483
  64.1 42.8 %collective-permute-start.7 = (bf16[128,3456]{1,0:T(8,128)(2,1)}, bf16[128,3456]{1,0:T(8,128)(2,1)S(1)}, u32[]{:S(2)}, u32[]{:S(2)}) collective-permute-start(bf16[128,3456]{1,0:T(8,128)(2,1)} %constant_dynamic-slice_fusion.1), channel_id=1, source_target_pairs={{8,16},{16,8},{9,17},{17,9},{10,18},{18,10},{11,19},{19,11},{12,20... | collective-permute-start | bytes 2654216 | tf_op jit(solution)/shard_map/ppermute | solution.py:482
  132.7 37.7 %collective-permute-start.9 = (bf16[2,1280,256]{2,1,0:T(8,128)(2,1)}, bf16[2,1280,256]{2,1,0:T(8,128)(2,1)}, u32[]{:S(2)}, u32[]{:S(2)}) collective-permute-start(bf16[2,1280,256]{2,1,0:T(8,128)(2,1)} %get-tuple-element.74), channel_id=1, source_target_pairs={{0,8},{24,16},{8,0},{16,24},{1,9},{25,17},{9,1},{17,25},{2,10},{26... | collective-permute-start | bytes 3932168 | tf_op jit(solution)/shard_map/ppermute | solution.py:483
  135.7 36.2 %collective-permute-start.10 = (bf16[2,1280,256]{2,1,0:T(8,128)(2,1)}, bf16[2,1280,256]{2,1,0:T(8,128)(2,1)}, u32[]{:S(2)}, u32[]{:S(2)}) collective-permute-start(bf16[2,1280,256]{2,1,0:T(8,128)(2,1)} %get-tuple-element.75.refs_13_), channel_id=1, source_target_pairs={{8,16},{16,8},{9,17},{17,9},{10,18},{18,10},{11,19},{19,11},{12,20... | collective-permute-start | bytes 3932168 | tf_op jit(solution)/shard_map/ppermute | solution.py:482
  152.0 46.3 %collective-permute-start.18 = (bf16[2,1280,256]{2,1,0:T(8,128)(2,1)}, bf16[2,1280,256]{2,1,0:T(8,128)(2,1)S(1)}, u32[]{:S(2)}, u32[]{:S(2)}) collective-permute-start(bf16[2,1280,256]{2,1,0:T(8,128)(2,1)} %get-tuple-element.82), channel_id=1, source_target_pairs={{0,8},{24,16},{8,0},{16,24},{1,9},{25,17},{9,1},{17,25},{2,10},{26... | collective-permute-start | bytes 3932168 | tf_op jit(solution)/shard_map/ppermute | solution.py:483
  154.1 45.4 %collective-permute-start.19 = (bf16[2,1280,256]{2,1,0:T(8,128)(2,1)}, bf16[2,1280,256]{2,1,0:T(8,128)(2,1)}, u32[]{:S(2)}, u32[]{:S(2)}) collective-permute-start(bf16[2,1280,256]{2,1,0:T(8,128)(2,1)} %get-tuple-element.78.refs_23_), channel_id=1, source_target_pairs={{8,16},{16,8},{9,17},{17,9},{10,18},{18,10},{11,19},{19,11},{12,20... | collective-permute-start | bytes 3932168 | tf_op jit(solution)/shard_map/ppermute | solution.py:482
  183.0 40.6 %collective-permute-start.16 = (bf16[2,1280,256]{2,1,0:T(8,128)(2,1)}, bf16[2,1280,256]{2,1,0:T(8,128)(2,1)}, u32[]{:S(2)}, u32[]{:S(2)}) collective-permute-start(bf16[2,1280,256]{2,1,0:T(8,128)(2,1)} %get-tuple-element.80.refs_22_), channel_id=1, source_target_pairs={{8,16},{16,8},{9,17},{17,9},{10,18},{18,10},{11,19},{19,11},{12,20... | collective-permute-start | bytes 3932168 | tf_op jit(solution)/shard_map/ppermute | solution.py:482
  184.9 38.7 %collective-permute-start.14 = (bf16[2,1152,256]{2,1,0:T(8,128)(2,1)}, bf16[2,1152,256]{2,1,0:T(8,128)(2,1)S(1)}, u32[]{:S(2)}, u32[]{:S(2)}) collective-permute-start(bf16[2,1152,256]{2,1,0:T(8,128)(2,1)} %get-tuple-element.79.refs_21_), channel_id=1, source_target_pairs={{0,8},{24,16},{8,0},{16,24},{1,9},{25,17},{9,1},{17,25},{2,10},{26... | collective-permute-start | bytes 3538952 | tf_op jit(solution)/shard_map/ppermute | solution.py:483
  210.7 38.5 %collective-permute-start.25 = (bf16[2,1280,256]{2,1,0:T(8,128)(2,1)}, bf16[2,1280,256]{2,1,0:T(8,128)(2,1)}, u32[]{:S(2)}, u32[]{:S(2)}) collective-permute-start(bf16[2,1280,256]{2,1,0:T(8,128)(2,1)} %get-tuple-element.84.refs_25_), channel_id=1, source_target_pairs={{8,16},{16,8},{9,17},{17,9},{10,18},{18,10},{11,19},{19,11},{12,20... | collective-permute-start | bytes 3932168 | tf_op jit(solution)/shard_map/ppermute | solution.py:482
  235.9 41.1 %collective-permute-start.20 = (bf16[2,1280,256]{2,1,0:T(8,128)(2,1)}, bf16[2,1280,256]{2,1,0:T(8,128)(2,1)S(1)}, u32[]{:S(2)}, u32[]{:S(2)}) collective-permute-start(bf16[2,1280,256]{2,1,0:T(8,128)(2,1)} %get-tuple-element.85.refs_23_.refs_20_), channel_id=1, source_target_pairs={{0,8},{24,16},{8,0},{16,24},{1,9},{25,17},{9,1},{17,25},{2,10},{26... | collective-permute-start | bytes 3932168 | tf_op jit(solution)/shard_map/ppermute | solution.py:483
  237.1 40.6 %collective-permute-start.22 = (bf16[2,1280,256]{2,1,0:T(8,128)(2,1)}, bf16[2,1280,256]{2,1,0:T(8,128)(2,1)}, u32[]{:S(2)}, u32[]{:S(2)}) collective-permute-start(bf16[2,1280,256]{2,1,0:T(8,128)(2,1)} %get-tuple-element.86.refs_23_), channel_id=1, source_target_pairs={{8,16},{16,8},{9,17},{17,9},{10,18},{18,10},{11,19},{19,11},{12,20... | collective-permute-start | bytes 3932168 | tf_op jit(solution)/shard_map/ppermute | solution.py:482
  261.1 43.3 %collective-permute-start.29 = (bf16[2,1152,256]{2,1,0:T(8,128)(2,1)}, bf16[2,1152,256]{2,1,0:T(8,128)(2,1)S(1)}, u32[]{:S(2)}, u32[]{:S(2)}) collective-permute-start(bf16[2,1152,256]{2,1,0:T(8,128)(2,1)} %get-tuple-element.92.refs_24_.refs_21_), channel_id=1, source_target_pairs={{0,8},{24,16},{8,0},{16,24},{1,9},{25,17},{9,1},{17,25},{2,10},{26... | collective-permute-start | bytes 3538952 | tf_op jit(solution)/shard_map/ppermute | solution.py:483
  264.7 39.7 %collective-permute-start.30 = (bf16[2,1152,256]{2,1,0:T(8,128)(2,1)}, bf16[2,1152,256]{2,1,0:T(8,128)(2,1)}, u32[]{:S(2)}, u32[]{:S(2)}) collective-permute-start(bf16[2,1152,256]{2,1,0:T(8,128)(2,1)} %get-tuple-element.89.refs_27_), channel_id=1, source_target_pairs={{8,16},{16,8},{9,17},{17,9},{10,18},{18,10},{11,19},{19,11},{12,20... | collective-permute-start | bytes 3538952 | tf_op jit(solution)/shard_map/ppermute | solution.py:482
  290.4 37.2 %collective-permute-start.27 = (bf16[2,1280,256]{2,1,0:T(8,128)(2,1)}, bf16[2,1280,256]{2,1,0:T(8,128)(2,1)}, u32[]{:S(2)}, u32[]{:S(2)}) collective-permute-start(bf16[2,1280,256]{2,1,0:T(8,128)(2,1)} %get-tuple-element.91.refs_30_), channel_id=1, source_target_pairs={{8,16},{16,8},{9,17},{17,9},{10,18},{18,10},{11,19},{19,11},{12,20... | collective-permute-start | bytes 3932168 | tf_op jit(solution)/shard_map/ppermute | solution.py:482
  292.1 35.5 %collective-permute-start.26 = (bf16[2,1152,256]{2,1,0:T(8,128)(2,1)}, bf16[2,1152,256]{2,1,0:T(8,128)(2,1)}, u32[]{:S(2)}, u32[]{:S(2)}) collective-permute-start(bf16[2,1152,256]{2,1,0:T(8,128)(2,1)} %get-tuple-element.90.refs_22_.refs_20_), channel_id=1, source_target_pairs={{0,8},{24,16},{8,0},{16,24},{1,9},{25,17},{9,1},{17,25},{2,10},{26... | collective-permute-start | bytes 3538952 | tf_op jit(solution)/shard_map/ppermute | solution.py:483
  318.0 38.1 %collective-permute-start.35 = (bf16[2,1280,256]{2,1,0:T(8,128)(2,1)}, bf16[2,1280,256]{2,1,0:T(8,128)(2,1)S(1)}, u32[]{:S(2)}, u32[]{:S(2)}) collective-permute-start(bf16[2,1280,256]{2,1,0:T(8,128)(2,1)} %get-tuple-element.101.refs_23_.refs_20_), channel_id=1, source_target_pairs={{0,8},{24,16},{8,0},{16,24},{1,9},{25,17},{9,1},{17,25},{2,10},{26... | collective-permute-start | bytes 3932168 | tf_op jit(solution)/shard_map/ppermute | solution.py:483
  319.8 37.0 %collective-permute-start.36 = (bf16[2,1280,256]{2,1,0:T(8,128)(2,1)}, bf16[2,1280,256]{2,1,0:T(8,128)(2,1)S(1)}, u32[]{:S(2)}, u32[]{:S(2)}) collective-permute-start(bf16[2,1280,256]{2,1,0:T(8,128)(2,1)} %get-tuple-element.98.refs_28_), channel_id=1, source_target_pairs={{8,16},{16,8},{9,17},{17,9},{10,18},{18,10},{11,19},{19,11},{12,20... | collective-permute-start | bytes 3932168 | tf_op jit(solution)/shard_map/ppermute | solution.py:482
  340.0 41.0 %collective-permute-start.32 = (bf16[2,1152,256]{2,1,0:T(8,128)(2,1)}, bf16[2,1152,256]{2,1,0:T(8,128)(2,1)}, u32[]{:S(2)}, u32[]{:S(2)}) collective-permute-start(bf16[2,1152,256]{2,1,0:T(8,128)(2,1)} %get-tuple-element.99.refs_22_.refs_20_), channel_id=1, source_target_pairs={{0,8},{24,16},{8,0},{16,24},{1,9},{25,17},{9,1},{17,25},{2,10},{26... | collective-permute-start | bytes 3538952 | tf_op jit(solution)/shard_map/ppermute | solution.py:483
  370.2 41.8 %collective-permute-start.42 = (bf16[2,1280,256]{2,1,0:T(8,128)(2,1)}, bf16[2,1280,256]{2,1,0:T(8,128)(2,1)}, u32[]{:S(2)}, u32[]{:S(2)}) collective-permute-start(bf16[2,1280,256]{2,1,0:T(8,128)(2,1)} %get-tuple-element.105.refs_28_), channel_id=1, source_target_pairs={{8,16},{16,8},{9,17},{17,9},{10,18},{18,10},{11,19},{19,11},{12,20... | collective-permute-start | bytes 3932168 | tf_op jit(solution)/shard_map/ppermute | solution.py:482
  372.0 40.0 %collective-permute-start.41 = (bf16[2,1152,256]{2,1,0:T(8,128)(2,1)}, bf16[2,1152,256]{2,1,0:T(8,128)(2,1)S(1)}, u32[]{:S(2)}, u32[]{:S(2)}) collective-permute-start(bf16[2,1152,256]{2,1,0:T(8,128)(2,1)} %get-tuple-element.108.refs_22_.refs_18_), channel_id=1, source_target_pairs={{0,8},{24,16},{8,0},{16,24},{1,9},{25,17},{9,1},{17,25},{2,10},{26... | collective-permute-start | bytes 3538952 | tf_op jit(solution)/shard_map/ppermute | solution.py:483
  393.2 38.7 %collective-permute-start.37 = (bf16[2,1152,256]{2,1,0:T(8,128)(2,1)}, bf16[2,1152,256]{2,1,0:T(8,128)(2,1)S(1)}, u32[]{:S(2)}, u32[]{:S(2)}) collective-permute-start(bf16[2,1152,256]{2,1,0:T(8,128)(2,1)} %get-tuple-element.106.refs_22_.refs_18_), channel_id=1, source_target_pairs={{0,8},{24,16},{8,0},{16,24},{1,9},{25,17},{9,1},{17,25},{2,10},{26... | collective-permute-start | bytes 3538952 | tf_op jit(solution)/shard_map/ppermute | solution.py:483
  425.3 38.8 %collective-permute-start.46 = (bf16[2,1152,256]{2,1,0:T(8,128)(2,1)}, bf16[2,1152,256]{2,1,0:T(8,128)(2,1)S(1)}, u32[]{:S(2)}, u32[]{:S(2)}) collective-permute-start(bf16[2,1152,256]{2,1,0:T(8,128)(2,1)} %get-tuple-element.115.refs_20_.refs_12_), channel_id=1, source_target_pairs={{0,8},{24,16},{8,0},{16,24},{1,9},{25,17},{9,1},{17,25},{2,10},{26... | collective-permute-start | bytes 3538952 | tf_op jit(solution)/shard_map/ppermute | solution.py:483
  429.0 35.1 %collective-permute-start.47 = (bf16[2,1152,256]{2,1,0:T(8,128)(2,1)}, bf16[2,1152,256]{2,1,0:T(8,128)(2,1)}, u32[]{:S(2)}, u32[]{:S(2)}) collective-permute-start(bf16[2,1152,256]{2,1,0:T(8,128)(2,1)} %get-tuple-element.112.refs_27_), channel_id=1, source_target_pairs={{8,16},{16,8},{9,17},{17,9},{10,18},{18,10},{11,19},{19,11},{12,20... | collective-permute-start | bytes 3538952 | tf_op jit(solution)/shard_map/ppermute | solution.py:482
  444.9 37.6 %collective-permute-start.43 = (bf16[2,1152,256]{2,1,0:T(8,128)(2,1)}, bf16[2,1152,256]{2,1,0:T(8,128)(2,1)S(1)}, u32[]{:S(2)}, u32[]{:S(2)}) collective-permute-start(bf16[2,1152,256]{2,1,0:T(8,128)(2,1)} %get-tuple-element.113.refs_20_.refs_12_), channel_id=1, source_target_pairs={{0,8},{24,16},{8,0},{16,24},{1,9},{25,17},{9,1},{17,25},{2,10},{26... | collective-permute-start | bytes 3538952 | tf_op jit(solution)/shard_map/ppermute | solution.py:483
  497.0 37.3 %collective-permute-start.49 = (bf16[2,1152,256]{2,1,0:T(8,128)(2,1)}, bf16[2,1152,256]{2,1,0:T(8,128)(2,1)S(1)}, u32[]{:S(2)}, u32[]{:S(2)}) collective-permute-start(bf16[2,1152,256]{2,1,0:T(8,128)(2,1)} %get-tuple-element.122.refs_14_.refs_1_), channel_id=1, source_target_pairs={{0,8},{24,16},{8,0},{16,24},{1,9},{25,17},{9,1},{17,25},{2,10},{26... | collective-permute-start | bytes 3538952 | tf_op jit(solution)/shard_map/ppermute | solution.py:483
  519.8 39.8 %collective-permute-start.55 = (bf16[2,1152,256]{2,1,0:T(8,128)(2,1)}, bf16[2,1152,256]{2,1,0:T(8,128)(2,1)S(1)}, u32[]{:S(2)}, u32[]{:S(2)}) collective-permute-start(bf16[2,1152,256]{2,1,0:T(8,128)(2,1)} %get-tuple-element.130.refs_3_.refs_0_), channel_id=1, source_target_pairs={{0,8},{24,16},{8,0},{16,24},{1,9},{25,17},{9,1},{17,25},{2,10},{26... | collective-permute-start | bytes 3538952 | tf_op jit(solution)/shard_map/ppermute | solution.py:483
  545.9 39.0 %collective-permute-start.52 = (bf16[2,1152,256]{2,1,0:T(8,128)(2,1)}, bf16[2,1152,256]{2,1,0:T(8,128)(2,1)S(1)}, u32[]{:S(2)}, u32[]{:S(2)}) collective-permute-start(bf16[2,1152,256]{2,1,0:T(8,128)(2,1)} %get-tuple-element.128.refs_3_.refs_0_), channel_id=1, source_target_pairs={{0,8},{24,16},{8,0},{16,24},{1,9},{25,17},{9,1},{17,25},{2,10},{26... | collective-permute-start | bytes 3538952 | tf_op jit(solution)/shard_map/ppermute | solution.py:483
  558.2 36.8 %collective-permute-start.59 = (bf16[1,256,256]{2,1,0:T(8,128)(2,1)}, bf16[1,256,256]{2,1,0:T(8,128)(2,1)}, u32[]{:S(2)}, u32[]{:S(2)}) collective-permute-start(bf16[1,256,256]{2,1,0:T(8,128)(2,1)} %dynamic-slice_bitcast_fusion.4), channel_id=1, source_target_pairs={{0,4},{4,0},{1,5},{5,1},{2,6},{6,2},{3,7},{7,3},{8,12},{12,8},{9,1... | collective-permute-start | bytes 393224 | tf_op jit(solution)/shard_map/ppermute | solution.py:484
  (93 other events, 952.0 us)
Sparse Core Ops, SparseCore 0:
  9.6 53.5 all-gather.6
  64.7 50.8 all-gather.8
  117.7 50.8 all-gather.10
